TPU v7x, 128 devices: a whole 4x4x4 slice. The times are simulated.
128 devices in a mesh: dp: 8 (over x_hi, z), tensor: 16 (over y, x_lo, core).
Axes of the slice: x: 4 (x_hi: 2, x_lo: 2; x = x_hi * 2 + x_lo), y: 4, z: 4, core: 2. Of those that a mesh axis runs over, the one named last changes fastest.
Arguments:
- cls_states: bfloat16 [4096, 5120], P(('dp', 'tensor')), may hold values from -6 to 6
- fc1_weight: bfloat16 [5120, 12800], P(None, 'tensor'), may hold values from -0.078125 to 0.078125
- fc2_weight: bfloat16 [12800, 5120], P('tensor'), may hold values from -0.0546875 to 0.0546875
- proj_weight: bfloat16 [5120, 1536], P('tensor'), may hold values from -0.078125 to 0.078125
- text_pooled: bfloat16 [4096, 1280], P(('dp', 'tensor')), may hold values from -6 to 6
- text_proj: bfloat16 [1280, 1536], replicated, may hold values from -0.15625 to 0.15625
- pair_owner: int32 [4096, 1], P(('dp', 'tensor')), may hold values from 0 to 7; in each aligned block of 32 rows (0 to 31, 32 to 63, ...) at most 8 rows name the same one
- pair_slot: int32 [4096], P(('dp', 'tensor')), may hold values from 0 to 31
- threshold: float32 [1], replicated, may hold values from -0.03 to 0.03
Outputs:
- filtered: bfloat16 [4096, 1536], P(('dp', 'tensor'))
- weight: float32 [4096], P(('dp', 'tensor'))
Inputs may be any that keep to these rules, and one draw needn't show every extreme that they name: `pair_owner`: among the rows of one device, at most 8 images share an owner, and in some device exactly 8 do.
All inputs are finite; a program needn't handle non-finite values.
Results may differ from a plain program's by a relative error of at most 0.029.
Values may be sent and summed in bfloat16 or wider, within the bound.
No kernel may reach another device: no remote copies, remote signals or barrier semaphores. Data moves between devices by JAX's collectives and lax.ppermute only.
A program may use at most 128 MiB of HBM per device.

v0:
```python
import jax
import jax.numpy as jnp
from jax import lax
from jax.sharding import PartitionSpec as P

CAP = 8


eps = 1e-06
sharpness = 40.0


def layer_norm(values):
    average = jnp.mean(values, axis=-1, keepdims=True)
    centred = values - average
    variance = jnp.mean(centred * centred, axis=-1, keepdims=True)
    return centred * lax.rsqrt(variance + eps)


def shards(
    cls_states,
    fc1_weight,
    fc2_weight,
    proj_weight,
    text_pooled,
    text_proj,
    pair_owner,
    pair_slot,
    threshold,
):
    embed_width = proj_weight.shape[1]
    normed = layer_norm(
        lax.all_gather(cls_states, "tensor", axis=0, tiled=True).astype(jnp.float32)
    ).astype(jnp.bfloat16)
    hidden = jax.nn.gelu(
        jnp.dot(normed, fc1_weight, preferred_element_type=jnp.float32), approximate=False
    ).astype(jnp.bfloat16)
    mlp_out = lax.psum_scatter(
        jnp.dot(hidden, fc2_weight, preferred_element_type=jnp.float32).astype(jnp.bfloat16),
        "tensor",
        scatter_dimension=0,
        tiled=True,
    ).astype(jnp.float32)
    final = layer_norm(cls_states.astype(jnp.float32) + mlp_out).astype(jnp.bfloat16)
    embedded = jnp.dot(
        final,
        lax.all_gather(proj_weight, "tensor", axis=0, tiled=True),
        preferred_element_type=jnp.float32,
    )
    image_unit = (
        embedded * lax.rsqrt(jnp.sum(embedded * embedded, axis=-1, keepdims=True) + eps)
    ).astype(jnp.bfloat16)
    text_normed = layer_norm(text_pooled.astype(jnp.float32)).astype(jnp.bfloat16)
    text_embedded = jnp.dot(text_normed, text_proj, preferred_element_type=jnp.float32)
    text_unit = text_embedded * lax.rsqrt(
        jnp.sum(text_embedded * text_embedded, axis=-1, keepdims=True) + eps
    )
    caption_count = text_unit.shape[0]
    n_owner = lax.axis_size("dp")
    owners = pair_owner[:, 0]
    onehot = (owners[:, None] == jnp.arange(n_owner, dtype=jnp.int32)[None, :]).astype(jnp.int32)
    before = jnp.cumsum(onehot, axis=0) - onehot
    position = jnp.sum(before * onehot, axis=1)
    send_embed = (
        jnp.zeros((n_owner, CAP, embed_width), jnp.bfloat16).at[owners, position].set(image_unit)
    )
    send_slot = jnp.zeros((n_owner, CAP), jnp.int32).at[owners, position].set(pair_slot)
    embed_in = lax.all_to_all(send_embed, "dp", split_axis=0, concat_axis=0, tiled=True)
    slot_in = lax.all_to_all(send_slot, "dp", split_axis=0, concat_axis=0, tiled=True)
    picker = (
        slot_in[:, :, None] == jnp.arange(caption_count, dtype=jnp.int32)[None, None, :]
    ).astype(jnp.float32)
    matched = jnp.einsum("dks,se->dke", picker, text_unit, precision=lax.Precision.HIGHEST)
    cosine = jnp.sum(embed_in.astype(jnp.float32) * matched, axis=-1)
    scored = jax.nn.sigmoid(sharpness * (cosine - threshold[0]))
    returned = lax.all_to_all(scored, "dp", split_axis=0, concat_axis=0, tiled=True)
    weight = returned[owners, position]
    filtered = (weight[:, None] * image_unit.astype(jnp.float32)).astype(jnp.bfloat16)
    return (filtered, weight)


def solution(mesh):
    placed = (
        P(("dp", "tensor"), None),
        P(None, "tensor"),
        P("tensor", None),
        P("tensor", None),
        P(("dp", "tensor"), None),
        P(),
        P(("dp", "tensor"), None),
        P(("dp", "tensor")),
        P(),
    )
    return jax.shard_map(
        shards,
        mesh=mesh,
        in_specs=placed,
        out_specs=(P(("dp", "tensor"), None), P(("dp", "tensor"))),
        check_vma=False,
    )
```

profile of v0, /device:TPU:0, one launch (start us, length us, event | category | flops | bytes accessed | tf_op | source)
XLA Modules:
  0.0 296.6 jit_solution(14737828004271628181)
XLA Ops:
  7.2 0.0 all-gather.3.cloned.1.call-start
  7.2 0.7 all-gather.3.cloned.1.call-update
  7.9 0.0 reduce-scatter.2.cloned.1.call-start
  7.9 43.8 %all-gather.3.cloned.1.call-done = bf16[512,5120]{1,0:T(8,128)(2,1)} async-done(((bf16[32,5120]{1,0:T(8,128)(2,1)}), bf16[512,5120]{1,0:T(8,128)(2,1)}) %all-gather.3.cloned.1.call-update) | async-done | bytes 5242896 | tf_op jit(solution)/shard_map/all_gather | solution.py:33
  51.8 0.0 copy-start
  51.8 3.4 %convert_reduce_fusion = f32[512]{0:T(512)S(1)} fusion(bf16[512,5120]{1,0:T(8,128)(2,1)} %all-gather.3.cloned.1.call-done), kind=kLoop, calls=%fused_computation.4 | loop fusion | flops 5242368 | bytes 5244928 | tf_op jit(solution)/shard_map/reduce_sum | solution.py:14
  55.2 0.6 copy-done
  55.8 1.5 fusion.2
  57.3 30.1 %convolution_convert_fusion = bf16[512,5120]{1,0:T(8,128)(2,1)} fusion(bf16[800,5120]{1,0:T(8,128)(2,1)} %param.11, bf16[5120,800]{0,1:T(8,128)(2,1)} %param.10, bf16[512,5120]{1,0:T(8,128)(2,1)} %all-gather.3.cloned.1.call-done, f32[512]{0:T(512)S(1)} %add_rsqrt_fusion, f32[512]{0:T(512)S(1)} %broadcast_multiply_fusion), kind=kOutput, calls=%fused_computation.9 | convolution fusion | flops 8428339200 | bytes 26873856 | tf_op jit(solution)/shard_map/dot_general | solution.py:39
  87.4 0.0 copy-start.4
  87.4 0.0 copy-start.6
  87.4 0.0 reduce-scatter.2.cloned.1.call-update
  87.4 0.0 copy-start.3
  87.4 0.2 all-gather.5.cloned.1.call-start
  87.7 0.5 all-gather.5.cloned.1.call-update
  88.2 0.0 copy-done.4
  88.2 0.1 fusion.52
  88.2 0.1 reduce_window_sum.11
  88.3 0.2 select_reduce_fusion
  88.5 0.6 broadcast_in_dim.5
  89.1 0.0 copy-done.6
  89.1 5.4 %scatter_fusion.1 = s32[8,8]{1,0:T(8,128)} fusion(s32[8,8]{1,0:T(8,128)} %broadcast_in_dim.5, s32[32]{0:T(128)S(1)} %get-tuple-element.2, s32[32]{0:T(128)S(1)} %copy-done.6), kind=kCustom, calls=%fused_computation.2 | custom fusion | bytes 640 | tf_op jit(solution)/shard_map/scatter | solution.py:67
  94.5 6.4 %all-to-all-start.1 = ((s32[8,1,8]{2,1,0:T(1,128)}), s32[8,1,8]{2,1,0:T(1,128)S(1)}, u32[]{:S(2)}, u32[]{:S(2)}) async-start(s32[8,1,8]{2,1,0:T(1,128)} %bitcast.4), calls=%async_computation.2 | async-start | bytes 8192 | tf_op jit(solution)/shard_map/all_to_all | solution.py:69
  101.5 0.0 copy-done.3
  101.5 0.1 convert_reduce_fusion.1
  101.7 0.2 fusion.44
  101.9 0.0 copy-start.1
  101.9 3.1 %multiply_reduce_fusion.1 = (f32[32]{0:T(128)S(1)}, f32[32,1536]{1,0:T(8,128)S(1)}) fusion(bf16[1280,1536]{1,0:T(8,128)(2,1)} %param.14, bf16[32,1280]{1,0:T(8,128)(2,1)S(1)} %copy-done.3, f32[32]{0:T(128)S(1)} %add_rsqrt_fusion.2, f32[32]{0:T(128)S(1)} %broadcast_multiply_fusion.1), kind=kOutput, calls=%fused_computation.59 | convolution fusion | flops 126091232 | bytes 4211072 | tf_op jit(solution)/shard_map/dot_general | solution.py:54
  105.0 55.4 %reduce-scatter.2.cloned.1.call-done = bf16[32,5120]{1,0:T(8,128)(2,1)} async-done(((bf16[512,5120]{1,0:T(8,128)(2,1)}), bf16[32,5120]{1,0:T(8,128)(2,1)}) %reduce-scatter.2.cloned.1.call-update) | async-done | bytes 327696 | tf_op jit(solution)/shard_map/reduce_scatter | solution.py:38
  160.4 0.0 copy-done.1
  160.4 0.0 copy-start.2
  160.4 1.2 fusion.36
  161.7 1.2 multiply_reduce_fusion
  162.9 84.6 %all-gather.5.cloned.1.call-done = bf16[5120,1536]{1,0:T(8,128)(2,1)} async-done(((bf16[320,1536]{1,0:T(8,128)(2,1)}), bf16[5120,1536]{1,0:T(8,128)(2,1)}) %all-gather.5.cloned.1.call-update) | async-done | bytes 15728656 | tf_op jit(solution)/shard_map/all_gather | solution.py:47
  247.6 0.0 copy-done.2
  247.6 8.4 %multiply_reduce_fusion.2 = (f32[32]{0:T(128)S(1)}, f32[32,1536]{1,0:T(8,128)S(1)}) fusion(bf16[5120,1536]{1,0:T(8,128)(2,1)} %all-gather.5.cloned.1.call-done, bf16[32,5120]{1,0:T(8,128)(2,1)S(1)} %copy-done.2, bf16[32,5120]{1,0:T(8,128)(2,1)S(1)} %copy-done.1, f32[32]{0:T(128)S(1)} %add_rsqrt_fusion.4, f32[32]{0:T(128)S(1)} %broadcast_multiply_fusion.2), kind=kOutput, calls=%fused_computation.61 | convolution fusion | flops 504397792 | bytes 16580992 | tf_op jit(solution)/shard_map/dot_general | solution.py:45
  256.0 0.1 multiply_convert_fusion.3
  256.1 0.7 broadcast_in_dim.4
  256.8 5.8 %scatter_fusion = bf16[8,8,1536]{2,1,0:T(8,128)(2,1)} fusion(bf16[8,8,1536]{2,1,0:T(8,128)(2,1)} %broadcast_in_dim.4, s32[32]{0:T(128)S(1)} %get-tuple-element.2, bf16[32,1536]{1,0:T(8,128)(2,1)S(1)} %multiply_convert_fusion.3), kind=kCustom, calls=%fused_computation.1 | custom fusion | bytes 295168 | tf_op jit(solution)/shard_map/scatter | solution.py:65
  262.6 0.0 all-to-all-done.1
  262.6 6.8 %all-to-all-start = ((bf16[8,8,1536]{2,1,0:T(8,128)(2,1)}), bf16[8,8,1536]{2,1,0:T(8,128)(2,1)S(1)}, u32[]{:S(2)}, u32[]{:S(2)}) async-start(bf16[8,8,1536]{2,1,0:T(8,128)(2,1)} %scatter_fusion), calls=%async_computation.1 | async-start | bytes 393216 | tf_op jit(solution)/shard_map/all_to_all | solution.py:68
  269.4 8.6 %all-to-all-done = bf16[8,8,1536]{2,1,0:T(8,128)(2,1)S(1)} async-done(((bf16[8,8,1536]{2,1,0:T(8,128)(2,1)}), bf16[8,8,1536]{2,1,0:T(8,128)(2,1)S(1)}, u32[]{:S(2)}, u32[]{:S(2)}) %all-to-all-start) | async-done | bytes 196640 | tf_op jit(solution)/shard_map/all_to_all | solution.py:68
  278.0 0.5 fusion.20
  278.5 10.2 %all_to_all.23 = f32[8,1,8]{2,1,0:T(1,128)S(1)} all-to-all(f32[8,1,8]{2,1,0:T(1,128)S(1)} %bitcast.31), channel_id=1, replica_groups=mesh['dp'=8,'tensor'=16] {'dp'}, dimensions={0} | all-to-all | bytes 512 | tf_op jit(solution)/shard_map/all_to_all | solution.py:76
  288.6 0.7 gather_fusion
  289.3 0.0 copy-start.5
  289.3 0.7 multiply_convert_fusion.2
  290.1 0.0 copy-done.5
  (10 shorter events, 0.1 us)
Async XLA Ops:
  7.2 44.6 %all-gather.3.cloned.1.call-start = ((), (), s32[]{:S(2)}) async-start(), calls=%async_computation.4 | async-start | bytes 5570560 | tf_op jit(solution)/shard_map/all_gather | solution.py:33
  7.9 152.5 %reduce-scatter.2.cloned.1.call-start = ((), (), s32[]{:S(2)}) async-start(), calls=%async_computation.5 | async-start | bytes 5570560 | tf_op jit(solution)/shard_map/reduce_scatter | solution.py:38
  51.8 4.0 %copy-start = (bf16[512,5120]{1,0:T(8,128)(2,1)S(1)}, bf16[512,5120]{1,0:T(8,128)(2,1)}, u32[]{:S(2)}) copy-start(bf16[512,5120]{1,0:T(8,128)(2,1)} %all-gather.3.cloned.1.call-done) | copy-start | bytes 15728644
  87.4 0.8 copy-start.4
  87.4 1.7 copy-start.6
  87.4 14.1 %copy-start.3 = (bf16[32,1280]{1,0:T(8,128)(2,1)S(1)}, bf16[32,1280]{1,0:T(8,128)(2,1)}, u32[]{:S(2)}) copy-start(bf16[32,1280]{1,0:T(8,128)(2,1)} %param.13) | copy-start | bytes 245764
  87.4 160.1 %all-gather.5.cloned.1.call-start = ((), (), s32[]{:S(2)}) async-start(), calls=%async_computation.6 | async-start | bytes 16711680 | tf_op jit(solution)/shard_map/all_gather | solution.py:47
  94.5 168.1 %all-to-all-start.1 = ((s32[8,1,8]{2,1,0:T(1,128)}), s32[8,1,8]{2,1,0:T(1,128)S(1)}, u32[]{:S(2)}, u32[]{:S(2)}) async-start(s32[8,1,8]{2,1,0:T(1,128)} %bitcast.4), calls=%async_computation.2 | async-start | bytes 8192 | tf_op jit(solution)/shard_map/all_to_all | solution.py:69
  101.9 58.6 %copy-start.1 = (bf16[32,5120]{1,0:T(8,128)(2,1)S(1)}, bf16[32,5120]{1,0:T(8,128)(2,1)}, u32[]{:S(2)}) copy-start(bf16[32,5120]{1,0:T(8,128)(2,1)} %param.9) | copy-start | bytes 983044
  160.4 87.1 %copy-start.2 = (bf16[32,5120]{1,0:T(8,128)(2,1)S(1)}, bf16[32,5120]{1,0:T(8,128)(2,1)}, u32[]{:S(2)}) copy-start(bf16[32,5120]{1,0:T(8,128)(2,1)} %reduce-scatter.2.cloned.1.call-done) | copy-start | bytes 983044
  262.6 15.4 %all-to-all-start = ((bf16[8,8,1536]{2,1,0:T(8,128)(2,1)}), bf16[8,8,1536]{2,1,0:T(8,128)(2,1)S(1)}, u32[]{:S(2)}, u32[]{:S(2)}) async-start(bf16[8,8,1536]{2,1,0:T(8,128)(2,1)} %scatter_fusion), calls=%async_computation.1 | async-start | bytes 393216 | tf_op jit(solution)/shard_map/all_to_all | solution.py:68
  289.3 0.7 copy-start.5
Sparse Core Ops, SparseCore 0:
  9.7 42.0 all-gather.2
  87.5 72.8 reduce-scatter.1
  162.2 85.3 all-gather.4
where the time goes:
time: 297 us
  waiting for transfers between devices  194 us (65%)
  matrix products  42.1 us (14%)
  between operations  14.5 us (5%)
  local copies, waits for them, and re-layouts  13.7 us (5%)
  starting transfers between devices  13.5 us (5%)
  blocking collectives  10.2 us (3%)
  other arithmetic  8.87 us (3%)
    all_gather x1, waiting for transfers between devices, shards(): lax.all_gather(proj_weight, 'tensor', axis=0, tiled=True)  84.6 us
    reduce_scatter x1, waiting for transfers between devices, shards(): lax.psum_scatter(jnp.dot(hidden, fc2_weight, preferred_element_type=jnp.f...  55.4 us
    all_gather x1, waiting for transfers between devices, shards(): lax.all_gather(cls_states, 'tensor', axis=0, tiled=True).astype(jnp.float32)  43.8 us
    dot_general x1, matrix products, shards(): jnp.dot(hidden, fc2_weight, preferred_element_type=jnp.float32)  30.1 us
    all_to_all x1, blocking collectives, shards(): lax.all_to_all(scored, 'dp', split_axis=0, concat_axis=0, tiled=True)  10.2 us
    all_to_all x1, waiting for transfers between devices, shards(): lax.all_to_all(send_embed, 'dp', split_axis=0, concat_axis=0, tiled=True)  8.58 us
    dot_general x1, matrix products, shards(): jnp.dot(final, lax.all_gather(proj_weight, 'tensor', axis=0, tiled=True),...  8.44 us
    all_to_all x1, starting transfers between devices, shards(): lax.all_to_all(send_embed, 'dp', split_axis=0, concat_axis=0, tiled=True)  6.81 us
  transfers between devices with their start and end apart: 5, of which 4 were waited for; matrix products, arithmetic and copies ran while one was open for 9% of the time, Pallas kernels for 0%

commit v1 on v0

v1 whole, which is shorter than its diff:
```python
import functools

import jax
import jax.numpy as jnp
from jax import lax
from jax.experimental import pallas as pl
from jax.experimental.pallas import tpu as pltpu
from jax.sharding import PartitionSpec as P

eps = 1e-06
sharpness = 40.0
AXES = ("dp", "tensor")
BLK = 640
EW = 1536 + 128
f32 = jnp.float32
bf16 = jnp.bfloat16


def moves(dx=0, dy=0, mz=0, flip=False):
    def place(x, y, z, c):
        return ((x // 2) * 4 + z) * 16 + y * 4 + (x % 2) * 2 + c

    return [
        (place(x, y, z, c), place((x + dx) % 4, (y + dy) % 4, z ^ mz, c ^ int(flip)))
        for x in range(4)
        for y in range(4)
        for z in range(4)
        for c in range(2)
    ]


def shift(value, **step):
    return lax.ppermute(value, AXES, moves(**step))


def after(value, *others):
    return lax.optimization_barrier((value,) + others)[0]


NT = (((1,), (1,)), ((), ()))
TN = (((0,), (0,)), ((), ()))
VM = pl.BlockSpec(memory_space=pltpu.VMEM)
SM = pl.BlockSpec(memory_space=pltpu.SMEM)
HB = pl.BlockSpec(memory_space=pltpu.HBM)
HALF = 4 * BLK


def struct(shape, dtype):
    return jax.ShapeDtypeStruct(shape, dtype)


def call(body, scalars, arrays, outs, scratch=(), remote=0, limit=12, away=False, size=1024):
    inside = len(arrays) - remote
    return pl.pallas_call(
        body,
        in_specs=[SM] * len(scalars) + [VM] * inside + [HB] * remote,
        out_specs=((HB if away else VM),) * len(outs),
        out_shape=outs,
        scratch_shapes=scratch,
        compiler_params=pltpu.CompilerParams(vmem_limit_bytes=limit * 1024 * 1024),
        cost_estimate=pl.CostEstimate(flops=1024, bytes_accessed=size, transcendentals=0),
    )(*scalars, *arrays)


def norm_kernel(cls_ref, normed_ref, r_ref, l_ref, centred_ref):
    values = cls_ref[...].astype(f32)
    centred = values - jnp.mean(values, axis=-1, keepdims=True)
    variance = jnp.mean(centred * centred, axis=-1, keepdims=True)
    centred_ref[...] = centred
    normed = (centred * lax.rsqrt(variance + eps)).astype(bf16)
    normed_ref[...] = normed
    r_ref[...] = normed[:16]
    l_ref[...] = normed[16:]


def norm_call(cls_states):
    width = cls_states.shape[1]
    outs = (struct((32, width), bf16), struct((16, width), bf16), struct((16, width), bf16), struct((32, width), f32))
    return call(norm_kernel, (), (cls_states,), outs)


def halves_kernel(*refs):
    *ins, r_ref, l_ref = refs
    for k, ref in enumerate(ins):
        r_ref[16 * k : 16 * k + 16] = ref[:16]
        l_ref[16 * k : 16 * k + 16] = ref[16:]


def halves_call(*ins):
    outs = (struct((16 * len(ins), ins[0].shape[1]), bf16),) * 2
    return call(halves_kernel, (), ins, outs)


def prep_kernel(parity, f_ref, a_ref, b_ref, means, sems):
    copies = []
    for k in range(4):
        for half, out in ((1 - parity[0], a_ref), (parity[0], b_ref)):
            at = pl.ds(pl.multiple_of((2 * k + half) * BLK, 128), BLK)
            sem = sems.at[len(copies)]
            copies.append(pltpu.make_async_copy(f_ref.at[:, at], out.at[:, pl.ds(k * BLK, BLK)], sem))
    start(copies)
    mean = jnp.sum(f_ref[...].astype(f32), axis=-1, keepdims=True) / f_ref.shape[1]
    high = mean.astype(bf16).astype(f32)
    lane = lax.broadcasted_iota(jnp.int32, means.shape, 1)
    means[...] = jnp.where(lane == 0, high, jnp.where(lane == 1, mean - high, 0.0)).astype(bf16)
    last = pltpu.make_async_copy(means, a_ref.at[:, pl.ds(HALF, 128)], sems.at[8])
    last.start()
    wait(copies)
    last.wait()


def prep_call(parity, f):
    rows = f.shape[0]
    return call(
        prep_kernel,
        (parity,),
        (f,),
        (struct((rows, HALF + 128), bf16), struct((rows, HALF), bf16)),
        scratch=[pltpu.VMEM((rows, 128), bf16), pltpu.SemaphoreType.DMA((9,))],
        away=True,
        size=16 * 1024 * 1024,
    )


def fetch(f_ref, o_ref, cols, first, buf, sems):
    copies = []
    for q in range(2):
        at = pl.ds(pl.multiple_of(cols[first + q] // 2 * BLK, 128), BLK)
        for k, ref in enumerate((f_ref, o_ref)):
            to = buf.at[pl.ds(800 * k, 800), pl.ds(BLK * q, BLK)]
            copies.append(pltpu.make_async_copy(ref.at[:, at], to, sems.at[2 * q + k]))
    return copies


def start(copies):
    for copy in copies:
        copy.start()


def wait(copies):
    for copy in copies:
        copy.wait()


def fc2_pair(cols, first, h_ref, mean_ref, buf, res_ref):
    pair = lax.dot_general(h_ref[...], buf[...], TN, preferred_element_type=f32)
    for q in range(2):
        part = pair[:, BLK * q : BLK * q + BLK] - mean_ref[:, :1]
        res = res_ref[:, pl.ds(pl.multiple_of(cols[first + q] * BLK, 128), BLK)]
        upper = jnp.concatenate([part[0:16] + res[0:16], part[16:128]], axis=0)
        lower = jnp.concatenate([part[128:192], part[192:208] + res[16:32], part[208:256]], axis=0)
        yield q, upper, lower


def first_kernel(cols, *refs):
    (n0, n1, n2, n3, a0, a13, a2, b0, b13, b2, res_ref, w_ref, v_ref, f_ref, o_ref) = refs[:15]
    h_ref, mean_ref, to_r, to_l, rows, wbuf, fbuf, mbuf, sems, fsems = refs[15:]
    spans = ((0, w_ref, 0, 160), (160, w_ref, 160, 640), (800, v_ref, 0, 400), (1200, v_ref, 400, 400))
    loads = [
        pltpu.make_async_copy(ref.at[pl.ds(at, size)], wbuf.at[pl.ds(base, size)], sems.at[k])
        for k, (base, ref, at, size) in enumerate(spans)
    ]
    columns = fetch(f_ref, o_ref, cols, 0, fbuf, fsems) + [
        pltpu.make_async_copy(ref.at[:, pl.ds(HALF, 128)], mbuf.at[pl.ds(800 * k, 800)], fsems.at[4 + k])
        for k, ref in enumerate((f_ref, o_ref))
    ]
    loads[0].start()
    loads[1].start()
    own = (n0, n1, n2, n3)
    for k in range(4):
        rows[16 * k : 16 * k + 16] = own[k][0:16]
        rows[192 + 16 * k : 208 + 16 * k] = own[k][16:32]
    for base, (p0, p13, p2) in ((64, (b0, b13, b2)), (128, (a0, a13, a2))):
        rows[base : base + 16] = p0[...]
        rows[base + 16 : base + 32] = p13[0:16]
        rows[base + 32 : base + 48] = p2[...]
        rows[base + 48 : base + 64] = p13[16:32]
    for k, (base, _, _, size) in enumerate(spans):
        loads[k].wait()
        if k < 2:
            loads[k + 2].start()
        if k == 2:
            start(columns)
        z = lax.dot_general(wbuf[base : base + size], rows[...], NT, preferred_element_type=f32)
        act = 0.5 * z * (1.0 + lax.erf(z * (0.5**0.5)))
        h_ref[base : base + size] = act.astype(bf16)
    wait(columns)
    means = lax.dot_general(h_ref[...], mbuf[...], TN, preferred_element_type=f32)
    mean_ref[...] = jnp.broadcast_to(jnp.sum(means, axis=-1, keepdims=True), mean_ref.shape)
    for q, upper, lower in fc2_pair(cols, 0, h_ref, mean_ref, fbuf, res_ref):
        to_r[q] = upper.astype(bf16)
        to_l[q] = lower.astype(bf16)


def first_call(cols, pieces, centred, w, v, f, o):
    outs = (
        struct((1600, 256), bf16),
        struct((256, 128), f32),
        struct((2, 128, BLK), bf16),
        struct((2, 128, BLK), bf16),
    )
    return call(
        first_kernel,
        (cols,),
        (*pieces, centred, w, v, f, o),
        outs,
        scratch=[
            pltpu.VMEM((256, w.shape[1]), bf16),
            pltpu.VMEM((1600, w.shape[1]), bf16),
            pltpu.VMEM((1600, 2 * BLK), bf16),
            pltpu.VMEM((1600, 128), bf16),
            pltpu.SemaphoreType.DMA((4,)),
            pltpu.SemaphoreType.DMA((6,)),
        ],
        remote=4,
        limit=52,
    )


def second_kernel(cols, h_ref, mean_ref, res_ref, f_ref, o_ref, fb_ref, ob_ref, to_r, to_l, own_ref, fbuf, sems):
    loads = [fetch(f_ref, o_ref, cols, 0, fbuf.at[0], sems.at[0])] + [
        fetch(fb_ref, ob_ref, cols, 2 * k, fbuf.at[k], sems.at[k]) for k in (1, 2)
    ]
    start(loads[0])
    start(loads[1])
    for k in range(3):
        wait(loads[k])
        if k == 0:
            start(loads[2])
        for q, upper, lower in fc2_pair(cols, 2 * k, h_ref, mean_ref, fbuf.at[k], res_ref):
            if k == 0:
                to_r[q] = upper.astype(bf16)
                to_l[q] = lower.astype(bf16)
            else:
                own_ref[2 * k - 2 + q, 0:128] = upper
                own_ref[2 * k - 2 + q, 128:256] = lower


def second_call(cols, h, h_mean, centred, f, o, fb, ob):
    outs = (struct((2, 128, BLK), bf16), struct((2, 128, BLK), bf16), struct((4, 256, BLK), f32))
    return call(
        second_kernel,
        (cols,),
        (h, h_mean, centred, f, o, fb, ob),
        outs,
        scratch=[pltpu.VMEM((3, 1600, 2 * BLK), bf16), pltpu.SemaphoreType.DMA((3, 4))],
        remote=4,
        limit=40,
    )


def add_kernel(place, own_ref, up_ref, low_ref, *outs):
    for k, out in enumerate(outs):
        out[0:128] = (own_ref[place + k, :128] + up_ref[k].astype(f32)).astype(bf16)
        out[128:256] = (own_ref[place + k, 128:] + low_ref[k].astype(f32)).astype(bf16)


def add_call(place, count, own, up, low):
    outs = (struct((256, BLK), bf16),) * count
    return call(functools.partial(add_kernel, place), (), (own, up, low), outs)


def proj_kernel(core, own_ref, up_ref, low_ref, t1, t2, t3, w_ref, o_ref, home_ref, a_ref, b_ref, total, weight):
    weight[pl.ds(pl.multiple_of(core[0] * 320, 64), 320)] = w_ref[...]
    weight[pl.ds(pl.multiple_of((1 - core[0]) * 320, 64), 320)] = o_ref[...]
    total[0:128] = own_ref[3, :128] + up_ref[1].astype(f32)
    total[128:256] = own_ref[3, 128:] + low_ref[1].astype(f32)
    for k, got in ((1, t1), (2, t2), (3, t3)):
        for group in range(4):
            for j in range(4):
                mine = 64 * group + 16 * ((j - k) % 4)
                theirs = 64 * group + 16 * j
                total[mine : mine + 16] += got[theirs : theirs + 16].astype(f32)
    x = total[...]
    squares = jnp.sum(x * x, axis=-1, keepdims=True)
    high = squares.astype(bf16).astype(f32)
    lane = lax.broadcasted_iota(jnp.int32, (256, 128), 1)
    extra = jnp.where(lane == 0, high, jnp.where(lane == 1, squares - high, 0.0)).astype(bf16)
    e = jnp.dot(x.astype(bf16), weight[...], preferred_element_type=f32).astype(bf16)
    for k in range(4):
        for at, base in ((0, 0), (16, 192)):
            src = slice(base + 16 * k, base + 16 * k + 16)
            home_ref[k, at : at + 16, :1536] = e[src]
            home_ref[k, at : at + 16, 1536:] = extra[src]
    b_ref[:, :1536] = e[64:128]
    b_ref[:, 1536:] = extra[64:128]
    a_ref[:, :1536] = e[128:192]
    a_ref[:, 1536:] = extra[128:192]


def proj_call(core, own, up, low, ts, w, o):
    outs = (struct((4, 32, EW), bf16), struct((64, EW), bf16), struct((64, EW), bf16))
    return call(
        proj_kernel,
        (core,),
        (own, up, low, *ts, w, o),
        outs,
        scratch=[pltpu.VMEM((256, BLK), f32), pltpu.VMEM((BLK, 1536), bf16)],
    )


def pair_kernel(home_ref, r_ref, l_ref, s0, s1, s2, s3):
    for k, out in enumerate((s0, s1, s2, s3)):
        at = slice(16 * k, 16 * k + 16)
        out[0:16] = (home_ref[k, 0:16].astype(f32) + r_ref[at].astype(f32)).astype(out.dtype)
        out[16:32] = (home_ref[k, 16:32].astype(f32) + l_ref[at].astype(f32)).astype(out.dtype)


def pair_call(home, r, l):
    outs = (struct((32, EW), f32),) + (struct((32, EW), bf16),) * 3
    return call(pair_kernel, (), (home, r, l), outs)


def text_kernel(index_ref, pooled_ref, proj_ref, out_ref):
    count = pooled_ref.shape[0]
    lane = lax.broadcasted_iota(jnp.int32, (32, count), 1)
    picker = jnp.where(lane == index_ref[...], 1.0, 0.0).astype(bf16)
    values = jnp.dot(picker, pooled_ref[...], preferred_element_type=f32)
    centred = values - jnp.mean(values, axis=-1, keepdims=True)
    variance = jnp.mean(centred * centred, axis=-1, keepdims=True)
    normed = (centred * lax.rsqrt(variance + eps)).astype(bf16)
    u = jnp.dot(normed, proj_ref[...], preferred_element_type=f32)
    out_ref[...] = u * lax.rsqrt(jnp.sum(u * u, axis=-1, keepdims=True) + eps)


def text_call(index, pooled, text_proj):
    outs = (struct((32, text_proj.shape[1]), f32),)
    return call(
        text_kernel, (), (index, pooled, text_proj), outs
    )[0]


def last_kernel(threshold_ref, s0, s1, s2, s3, text_ref, filtered_ref, weight_ref):
    total = s0[...] + s1[...].astype(f32) + s2[...].astype(f32) + s3[...].astype(f32)
    squares = jnp.sum(total[:, 1536:], axis=-1, keepdims=True)
    scale = lax.rsqrt(squares / 5120.0 + eps)
    e = total[:, :1536] * scale
    unit = (e * lax.rsqrt(jnp.sum(e * e, axis=-1, keepdims=True) + eps)).astype(bf16).astype(f32)
    cosine = jnp.sum(unit * text_ref[...], axis=-1, keepdims=True)
    weight = jax.nn.sigmoid(sharpness * (cosine - threshold_ref[0]))
    filtered_ref[...] = (weight * unit).astype(bf16)
    row = lax.broadcasted_iota(jnp.int32, (32, 32), 0)
    column = lax.broadcasted_iota(jnp.int32, (32, 32), 1)
    weight_ref[...] = jnp.sum(jnp.where(row == column, weight, 0.0), axis=0, keepdims=True)


def last_call(parts, text, threshold):
    outs = (struct((32, 1536), bf16), struct((1, 32), f32))
    return call(last_kernel, (threshold,), (*parts, text), outs)


def shards(
    cls_states, fc1_weight, fc2_weight, proj_weight, text_pooled, text_proj, pair_owner, pair_slot, threshold
):
    d = lax.axis_index("dp")
    t = lax.axis_index("tensor")
    x_hi, z, y, x_lo, core = d // 4, d % 4, t // 4, (t // 2) % 2, t % 2

    fc1_rows = fc1_weight.T

    fc1_other = shift(fc1_rows, flip=True)
    normed, r0, l0, centred = norm_call(cls_states)
    n1, n3 = shift(normed, dy=-1), shift(normed, dy=1)
    a0, b0 = shift(r0, dx=1), shift(l0, dx=-1)
    fc2_a, fc2_b = prep_call(x_lo.astype(jnp.int32).reshape(1), fc2_weight)
    n2 = shift(after(normed, a0, b0, fc2_a), dy=2)
    tz = after(text_pooled, a0, b0, fc2_a)
    tz = jnp.concatenate([tz, shift(tz, mz=1)])
    tz = jnp.concatenate([tz, shift(tz, mz=2)])
    fc2_a_other = shift(after(fc2_a, tz), flip=True)
    r13, l13 = halves_call(n1, n3)
    a13, b13 = shift(r13, dx=1), shift(l13, dx=-1)
    r2, l2 = halves_call(n2)
    a2, b2 = shift(r2, dx=1), shift(l2, dx=-1)
    fc2_b_other = shift(after(fc2_b, a13, b13, a2, b2), flip=True)
    pooled = jnp.concatenate([tz, shift(after(tz, a13, b13, a2, b2), dx=2)])

    def blocks(parity, *ks):
        return [2 * ((y + k) % 4) + parity for k in ks]

    pieces = (normed, n1, n2, n3, a0, a13, a2, b0, b13, b2)
    cols = jnp.stack(blocks(1 - x_lo, 1, 3)).astype(jnp.int32)
    h, h_mean, to_r, to_l = first_call(cols, pieces, centred, fc1_rows, fc1_other, fc2_a, fc2_a_other)
    got_r, got_l = shift(to_l, dx=-1), shift(to_r, dx=1)
    proj_other = shift(after(proj_weight, h), flip=True)
    cols = jnp.stack(blocks(1 - x_lo, 2, 0) + blocks(x_lo, 1, 3, 2, 0)).astype(jnp.int32)
    to_r2, to_l2, own = second_call(cols, h, h_mean, centred, fc2_a, fc2_a_other, fc2_b, fc2_b_other)
    got_r2, got_l2 = shift(to_l2, dx=-1), shift(to_r2, dx=1)
    s1, s3 = add_call(0, 2, own, got_r, got_l)
    t1, t3 = shift(s1, dy=1), shift(s3, dy=-1)
    (s2,) = add_call(2, 1, own, got_r2, got_l2)
    t2 = shift(s2, dy=2)

    owner = pair_owner[:, 0]
    relative = ((owner // 4) ^ x_hi) * 4 + ((owner % 4) ^ z)
    index = (relative * 32 + pair_slot).reshape(32, 1)
    text = text_call(after(index, s2), pooled, text_proj)

    core_index = core.astype(jnp.int32).reshape(1)
    home, e_a, e_b = proj_call(
        core_index, own, got_r2, got_l2, (t1, t2, t3), after(proj_weight, text), proj_other
    )
    s0, s1, s2, s3 = pair_call(home, shift(e_a, dx=-1), shift(e_b, dx=1))
    parts = (s0, shift(s1, dy=1), shift(s2, dy=2), shift(s3, dy=3))
    filtered, weight = last_call(parts, text, threshold)
    return filtered, weight.reshape(32)


def solution(mesh):
    placed = (
        P(("dp", "tensor"), None),
        P(None, "tensor"),
        P("tensor", None),
        P("tensor", None),
        P(("dp", "tensor"), None),
        P(),
        P(("dp", "tensor"), None),
        P(("dp", "tensor")),
        P(),
    )
    return jax.shard_map(
        shards,
        mesh=mesh,
        in_specs=placed,
        out_specs=(P(("dp", "tensor"), None), P(("dp", "tensor"))),
        check_vma=False,
    )
```

time: 297 us -> 126 us (0.42)
  waiting for transfers between devices: 194 us -> 37.1 us
  matrix products: 42.1 us -> 0 us
  Pallas kernels: 0 us -> 35.9 us
  starting transfers between devices: 13.5 us -> 39.3 us
  between operations: 14.5 us -> 1.66 us
  blocking collectives: 10.2 us -> 0 us
  other arithmetic: 8.87 us -> 1.16 us
  local copies, waits for them, and re-layouts: 13.7 us -> 10.6 us
    all_gather x2 -> x0, waiting for transfers between devices: 128 us -> none  [the longest x1 84.6 us: shards(): lax.all_gather(proj_weight, 'tensor', axis=0, tiled=True)]
    reduce_scatter x1 -> x0, waiting for transfers between devices: 55.4 us -> none  [shards(): lax.psum_scatter(jnp.dot(hidden, fc2_weight, preferred_element_type=jnp.f...]
    dot_general x4 -> x0, matrix products: 42.1 us -> none  [the longest x1 30.1 us: shards(): jnp.dot(hidden, fc2_weight, preferred_element_type=jnp.float32)]
    ppermute x0 -> x28, starting transfers between devices: none -> 39.3 us  [shift(): return lax.ppermute(value, AXES, moves(**step))]
    ppermute x0 -> x28, waiting for transfers between devices: none -> 37.1 us  [shift(): return lax.ppermute(value, AXES, moves(**step))]
    pallas_call x0 -> x12, Pallas kernels: none -> 35.9 us  [call(): pl.pallas_call(body, in_specs=[SM] * len(scalars) + [VM] * inside + [HB]...]
    all_to_all x2 -> x0, starting transfers between devices: 13.2 us -> none  [the longest x1 6.81 us: shards(): lax.all_to_all(send_embed, 'dp', split_axis=0, concat_axis=0, tiled=True)]
    scatter x2 -> x0, local copies, waits for them, and re-layouts: 11.1 us -> none  [the longest x1 5.75 us: shards(): jnp.zeros((n_owner, CAP, embed_width), jnp.bfloat16).at[owners, position]]
  transfers between devices with their start and end apart: 5 -> 28, of which waited for: 4 -> 13; matrix products, arithmetic and copies ran while one was open for 9% -> 3% of each run, Pallas kernels for 0% -> 26%
where the time goes in v1:
time: 126 us
  starting transfers between devices  39.3 us (31%)
  waiting for transfers between devices  37.1 us (29%)
  Pallas kernels  35.9 us (28%)
  local copies, waits for them, and re-layouts  10.6 us (8%)
  between operations  1.66 us (1%)
    ppermute x28, starting transfers between devices, shift(): return lax.ppermute(value, AXES, moves(**step))  39.3 us
    ppermute x28, waiting for transfers between devices, shift(): return lax.ppermute(value, AXES, moves(**step))  37.1 us
    pallas_call x12, Pallas kernels, call(): pl.pallas_call(body, in_specs=[SM] * len(scalars) + [VM] * inside + [HB]...  35.9 us
    unnamed x44, local copies, waits for them, and re-layouts  9.72 us
  transfers between devices with their start and end apart: 28, of which 13 were waited for; matrix products, arithmetic and copies ran while one was open for 3% of the time, Pallas kernels for 26%

profile of v1, /device:TPU:0, one launch (start us, length us, event | category | flops | bytes accessed | tf_op | source)
XLA Modules:
  0.0 125.7 jit_solution(6508195008439093099)
XLA Ops:
  0.6 0.1 collective-permute-start.9
  0.7 1.0 copy-done.12
  1.7 0.3 shard_map.104
  2.1 0.8 copy-done.2
  2.9 1.6 %collective-permute-start.1 = (bf16[16,5120]{1,0:T(8,128)(2,1)S(1)}, bf16[16,5120]{1,0:T(8,128)(2,1)S(1)}, u32[]{:S(2)}, u32[]{:S(2)}) collective-permute-start(bf16[16,5120]{1,0:T(8,128)(2,1)S(1)} %get-tuple-element.39), channel_id=1, source_target_pairs={{0,2},{1,3},{16,18},{17,19},{32,34},{33,35},{48,50},{49,51},{4,6},... | collective-permute-start | bytes 491528 | tf_op jit(solution)/shard_map/ppermute | solution.py:33
  4.5 1.7 %collective-permute-start.2 = (bf16[16,5120]{1,0:T(8,128)(2,1)S(1)}, bf16[16,5120]{1,0:T(8,128)(2,1)S(1)}, u32[]{:S(2)}, u32[]{:S(2)}) collective-permute-start(bf16[16,5120]{1,0:T(8,128)(2,1)S(1)} %get-tuple-element.40), channel_id=1, source_target_pairs={{0,66},{1,67},{16,82},{17,83},{32,98},{33,99},{48,114},{49,115},{4... | collective-permute-start | bytes 491528 | tf_op jit(solution)/shard_map/ppermute | solution.py:33
  6.1 3.1 %collective-permute-start = (bf16[32,5120]{1,0:T(8,128)(2,1)S(1)}, bf16[32,5120]{1,0:T(8,128)(2,1)S(1)}, u32[]{:S(2)}, u32[]{:S(2)}) collective-permute-start(bf16[32,5120]{1,0:T(8,128)(2,1)S(1)} %get-tuple-element.42.refs_0_), channel_id=1, source_target_pairs={{0,12},{1,13},{16,28},{17,29},{32,44},{33,45},{48,60},{49,61},{4,0... | collective-permute-start | bytes 983048 | tf_op jit(solution)/shard_map/ppermute | solution.py:33
  9.2 0.0 collective-permute-start.4
  9.2 3.3 %copy-done = bf16[800,5120]{1,0:T(8,128)(2,1)S(1)} copy-done((bf16[800,5120]{1,0:T(8,128)(2,1)S(1)}, bf16[800,5120]{1,0:T(8,128)(2,1)}, u32[]{:S(2)}) %copy-start) | copy-done | bytes 8192024
  12.6 3.5 %shard_map.105 = (bf16[800,2688]{1,0:T(8,128)(2,1)}, bf16[800,2560]{1,0:T(8,128)(2,1)}) custom-call(s32[1]{0:T(128)} %bitcast.9.parity, bf16[800,5120]{1,0:T(8,128)(2,1)S(1)} %copy-done), custom_call_target="tpu_custom_call" | custom-call | flops 1024 | bytes 16777216 | tf_op jit(solution)/shard_map/pallas_call | solution.py:54
  16.1 2.0 %collective-permute-start.10 = (bf16[32,1280]{1,0:T(8,128)(2,1)S(1)}, bf16[32,1280]{1,0:T(8,128)(2,1)S(1)}, u32[]{:S(2)}, u32[]{:S(2)}) collective-permute-start(bf16[32,1280]{1,0:T(8,128)(2,1)S(1)} %copy-done.13), channel_id=1, source_target_pairs={{0,16},{1,17},{16,0},{17,1},{32,48},{33,49},{48,32},{49,33},{4,20}... | collective-permute-start | bytes 245768 | tf_op jit(solution)/shard_map/ppermute | solution.py:33
  18.1 0.6 constant_dynamic-update-slice_fusion.2
  18.7 2.2 %collective-permute-start.3 = (bf16[32,5120]{1,0:T(8,128)(2,1)S(1)}, bf16[32,5120]{1,0:T(8,128)(2,1)S(1)}, u32[]{:S(2)}, u32[]{:S(2)}) collective-permute-start(bf16[32,5120]{1,0:T(8,128)(2,1)S(1)} %get-tuple-element.42.refs_0_), channel_id=1, source_target_pairs={{0,8},{1,9},{16,24},{17,25},{32,40},{33,41},{48,56},{49,57},{4,12}... | collective-permute-start | bytes 983048 | tf_op jit(solution)/shard_map/ppermute | solution.py:33
  20.9 3.7 %collective-permute-start.11 = (bf16[64,1280]{1,0:T(8,128)(2,1)S(1)}, bf16[64,1280]{1,0:T(8,128)(2,1)S(1)}, u32[]{:S(2)}, u32[]{:S(2)}) collective-permute-start(bf16[64,1280]{1,0:T(8,128)(2,1)S(1)} %pad_maximum_fusion.1), channel_id=1, source_target_pairs={{0,32},{1,33},{16,48},{17,49},{32,0},{33,1},{48,16},{49,17},{4,36}... | collective-permute-start | bytes 491528 | tf_op jit(solution)/shard_map/ppermute | solution.py:33
  24.6 0.6 constant_dynamic-update-slice_fusion.1
  25.3 0.3 collective-permute-start.5
  25.7 2.2 %collective-permute-done.11 = bf16[64,1280]{1,0:T(8,128)(2,1)S(1)} collective-permute-done((bf16[64,1280]{1,0:T(8,128)(2,1)S(1)}, bf16[64,1280]{1,0:T(8,128)(2,1)S(1)}, u32[]{:S(2)}, u32[]{:S(2)}) %collective-permute-start.11) | collective-permute-done | bytes 163872 | tf_op jit(solution)/shard_map/ppermute | solution.py:33
  27.9 0.7 constant_dynamic-update-slice_fusion
  28.6 1.5 %collective-permute-start.7 = (bf16[32,5120]{1,0:T(8,128)(2,1)S(1)}, bf16[32,5120]{1,0:T(8,128)(2,1)S(1)}, u32[]{:S(2)}, u32[]{:S(2)}) collective-permute-start(bf16[32,5120]{1,0:T(8,128)(2,1)S(1)} %get-tuple-element.45), channel_id=1, source_target_pairs={{0,66},{1,67},{16,82},{17,83},{32,98},{33,99},{48,114},{49,115},{4... | collective-permute-start | bytes 983048 | tf_op jit(solution)/shard_map/ppermute | solution.py:33
  30.2 0.5 collective-permute-start.6
  30.8 4.3 %collective-permute-done.5.refs_5_ = bf16[32,5120]{1,0:T(8,128)(2,1)S(1)} collective-permute-done((bf16[32,5120]{1,0:T(8,128)(2,1)S(1)}, bf16[32,5120]{1,0:T(8,128)(2,1)S(1)}, u32[]{:S(2)}, u32[]{:S(2)}) %collective-permute-start.5) | collective-permute-done | bytes 327712 | tf_op jit(solution)/shard_map/ppermute | solution.py:33
  35.1 1.1 collective-permute-start.8
  36.2 2.1 %collective-permute-done.6.refs_6_ = bf16[16,5120]{1,0:T(8,128)(2,1)S(1)} collective-permute-done((bf16[16,5120]{1,0:T(8,128)(2,1)S(1)}, bf16[16,5120]{1,0:T(8,128)(2,1)S(1)}, u32[]{:S(2)}, u32[]{:S(2)}) %collective-permute-start.6) | collective-permute-done | bytes 163872 | tf_op jit(solution)/shard_map/ppermute | solution.py:33
  38.3 0.9 collective-permute-done.7.refs_8_
  39.1 3.1 %collective-permute-done.8.refs_9_ = bf16[16,5120]{1,0:T(8,128)(2,1)S(1)} collective-permute-done((bf16[16,5120]{1,0:T(8,128)(2,1)S(1)}, bf16[16,5120]{1,0:T(8,128)(2,1)S(1)}, u32[]{:S(2)}, u32[]{:S(2)}) %collective-permute-start.8) | collective-permute-done | bytes 163872 | tf_op jit(solution)/shard_map/ppermute | solution.py:33
  42.3 0.0 collective-permute-start.13
  42.3 0.1 pad_add_fusion.cols
  42.5 16.6 %shard_map.108 = (bf16[1600,256]{1,0:T(8,128)(2,1)}, f32[256,128]{1,0:T(8,128)S(1)}, bf16[2,128,640]{2,1,0:T(8,128)(2,1)}, bf16[2,128,640]{2,1,0:T(8,128)(2,1)}) custom-call(s32[2]{0:T(128)S(1)} %pad_add_fusion.cols, bf16[32,5120]{1,0:T(8,128)(2,1)S(1)} %get-tuple-element.42.refs_0_, bf16[32,5120]{1,0:T(8,128)(2,1)} %copy-done.4, ...), custom_call_target="tpu_custom_call" | custom-call | flops 1024 | bytes 1024 | tf_op jit(solution)/shard_map/pallas_call | solution.py:54
  59.0 0.5 collective-permute-start.22
  59.6 2.8 %collective-permute-start.16 = (bf16[2,128,640]{2,1,0:T(8,128)(2,1)}, bf16[2,128,640]{2,1,0:T(8,128)(2,1)}, u32[]{:S(2)}, u32[]{:S(2)}) collective-permute-start(bf16[2,128,640]{2,1,0:T(8,128)(2,1)} %get-tuple-element.57), channel_id=1, source_target_pairs={{0,66},{1,67},{16,82},{17,83},{32,98},{33,99},{48,114},{49,115},{4... | collective-permute-start | bytes 983048 | tf_op jit(solution)/shard_map/ppermute | solution.py:33
  62.3 0.1 stack.36.cols
  62.4 0.0 collective-permute-start.17
  62.4 1.1 copy-done.11
  63.6 7.5 %shard_map.109 = (bf16[2,128,640]{2,1,0:T(8,128)(2,1)}, bf16[2,128,640]{2,1,0:T(8,128)(2,1)}, f32[4,256,640]{2,1,0:T(8,128)S(1)}) custom-call(s32[6]{0:T(128)S(1)} %stack.36.cols, bf16[1600,256]{1,0:T(8,128)(2,1)S(1)} %copy-done.11, f32[256,128]{1,0:T(8,128)S(1)} %get-tuple-element.51.mean_ref, f32[32,5120]{1,0:T(8,128)S(1)} %copy-done.3, ...), custom_call_target="tpu_custom_call" | custom-call | flops 1024 | bytes 1024 | tf_op jit(solution)/shard_map/pallas_call | solution.py:54
  71.1 0.0 copy-start.19
  71.1 0.0 copy-start.20
  71.2 0.0 copy-start.15
  71.2 3.3 %collective-permute-start.14 = (bf16[2,128,640]{2,1,0:T(8,128)(2,1)}, bf16[2,128,640]{2,1,0:T(8,128)(2,1)S(1)}, u32[]{:S(2)}, u32[]{:S(2)}) collective-permute-start(bf16[2,128,640]{2,1,0:T(8,128)(2,1)} %get-tuple-element.55), channel_id=1, source_target_pairs={{0,66},{1,67},{16,82},{17,83},{32,98},{33,99},{48,114},{49,115},{4... | collective-permute-start | bytes 983048 | tf_op jit(solution)/shard_map/ppermute | solution.py:33
  74.5 1.5 %collective-permute-start.21 = (bf16[128,1280]{1,0:T(8,128)(2,1)}, bf16[128,1280]{1,0:T(8,128)(2,1)}, u32[]{:S(2)}, u32[]{:S(2)}) collective-permute-start(bf16[128,1280]{1,0:T(8,128)(2,1)} %constant_dynamic-update-slice_fusion), channel_id=1, source_target_pairs={{0,64},{1,65},{16,80},{17,81},{32,96},{33,97},{48,112},{49,113},{4... | collective-permute-start | bytes 983048 | tf_op jit(solution)/shard_map/ppermute | solution.py:33
  76.0 2.0 %shard_map.110 = (bf16[256,640]{1,0:T(8,128)(2,1)}, bf16[256,640]{1,0:T(8,128)(2,1)}) custom-call(f32[4,256,640]{2,1,0:T(8,128)S(1)} %get-tuple-element.54.own_ref, bf16[2,128,640]{2,1,0:T(8,128)(2,1)} %collective-permute-done.16.up_ref, bf16[2,128,640]{2,1,0:T(8,128)(2,1)} %collective-permute-done.17.low_ref), custom_call_target="tpu_custom_call" | custom-call | flops 1024 | bytes 1024 | tf_op jit(solution)/shard_map/pallas_call | solution.py:54
  78.0 2.0 %collective-permute-start.18 = (bf16[256,640]{1,0:T(8,128)(2,1)}, bf16[256,640]{1,0:T(8,128)(2,1)}, u32[]{:S(2)}, u32[]{:S(2)}) collective-permute-start(bf16[256,640]{1,0:T(8,128)(2,1)} %get-tuple-element.59), channel_id=1, source_target_pairs={{0,4},{1,5},{16,20},{17,21},{32,36},{33,37},{48,52},{49,53},{4,8},... | collective-permute-start | bytes 983048 | tf_op jit(solution)/shard_map/ppermute | solution.py:33
  79.9 8.5 %collective-permute-done.14.up_ref = bf16[2,128,640]{2,1,0:T(8,128)(2,1)S(1)} collective-permute-done((bf16[2,128,640]{2,1,0:T(8,128)(2,1)}, bf16[2,128,640]{2,1,0:T(8,128)(2,1)S(1)}, u32[]{:S(2)}, u32[]{:S(2)}) %collective-permute-start.14) | collective-permute-done | bytes 327712 | tf_op jit(solution)/shard_map/ppermute | solution.py:33
  88.4 3.3 %collective-permute-done.15.low_ref = bf16[2,128,640]{2,1,0:T(8,128)(2,1)S(1)} collective-permute-done((bf16[2,128,640]{2,1,0:T(8,128)(2,1)}, bf16[2,128,640]{2,1,0:T(8,128)(2,1)S(1)}, u32[]{:S(2)}, u32[]{:S(2)}) %collective-permute-start.15) | collective-permute-done | bytes 327712 | tf_op jit(solution)/shard_map/ppermute | solution.py:33
  91.8 0.8 shard_map.111
  92.6 2.2 %collective-permute-start.19 = (bf16[256,640]{1,0:T(8,128)(2,1)}, bf16[256,640]{1,0:T(8,128)(2,1)}, u32[]{:S(2)}, u32[]{:S(2)}) collective-permute-start(bf16[256,640]{1,0:T(8,128)(2,1)} %shard_map.111), channel_id=1, source_target_pairs={{0,8},{1,9},{16,24},{17,25},{32,40},{33,41},{48,56},{49,57},{4,12}... | collective-permute-start | bytes 983048 | tf_op jit(solution)/shard_map/ppermute | solution.py:33
  94.8 2.5 %collective-permute-start.20 = (bf16[256,640]{1,0:T(8,128)(2,1)}, bf16[256,640]{1,0:T(8,128)(2,1)}, u32[]{:S(2)}, u32[]{:S(2)}) collective-permute-start(bf16[256,640]{1,0:T(8,128)(2,1)} %get-tuple-element.60), channel_id=1, source_target_pairs={{0,12},{1,13},{16,28},{17,29},{32,44},{33,45},{48,60},{49,61},{4,0... | collective-permute-start | bytes 983048 | tf_op jit(solution)/shard_map/ppermute | solution.py:33
  97.3 1.1 pad_maximum_fusion.pooled_ref
  98.4 0.1 copy.11.index_ref
  98.4 2.1 %copy-done.1 = bf16[1280,1536]{1,0:T(8,128)(2,1)S(1)} copy-done((bf16[1280,1536]{1,0:T(8,128)(2,1)S(1)}, bf16[1280,1536]{1,0:T(8,128)(2,1)}, u32[]{:S(2)}) %copy-start.1) | copy-done | bytes 3932184
  100.6 1.3 %shard_map.112.text_ref = f32[32,1536]{1,0:T(8,128)S(1)} custom-call(s32[32,1]{1,0:T(8,128)S(1)} %copy.11.index_ref, bf16[256,1280]{1,0:T(8,128)(2,1)S(1)} %pad_maximum_fusion.pooled_ref, bf16[1280,1536]{1,0:T(8,128)(2,1)S(1)} %copy-done.1), custom_call_target="tpu_custom_call" | custom-call | flops 1024 | bytes 1024 | tf_op jit(solution)/shard_map/pallas_call | solution.py:54
  101.9 3.7 %collective-permute-done.20.t3 = bf16[256,640]{1,0:T(8,128)(2,1)} collective-permute-done((bf16[256,640]{1,0:T(8,128)(2,1)}, bf16[256,640]{1,0:T(8,128)(2,1)}, u32[]{:S(2)}, u32[]{:S(2)}) %collective-permute-start.20) | collective-permute-done | bytes 327712 | tf_op jit(solution)/shard_map/ppermute | solution.py:33
  105.6 2.7 %shard_map.113 = (bf16[4,32,1664]{2,1,0:T(8,128)(2,1)S(1)}, bf16[64,1664]{1,0:T(8,128)(2,1)S(1)}, bf16[64,1664]{1,0:T(8,128)(2,1)S(1)}) custom-call(s32[1]{0:T(128)} %bitcast.core, f32[4,256,640]{2,1,0:T(8,128)S(1)} %get-tuple-element.54.own_ref, bf16[2,128,640]{2,1,0:T(8,128)(2,1)S(1)} %copy-done.8, bf16[2,128,640]{2,1,0:T(8,128)(2,1)S(1)} %copy-done.10, ...), custom_call_target="tpu_custom_call" | custom-call | flops 1024 | bytes 1024 | tf_op jit(solution)/shard_map/pallas_call | solution.py:54
  108.4 0.4 collective-permute-start.23
  108.8 1.7 %collective-permute-start.24 = (bf16[64,1664]{1,0:T(8,128)(2,1)S(1)}, bf16[64,1664]{1,0:T(8,128)(2,1)S(1)}, u32[]{:S(2)}, u32[]{:S(2)}) collective-permute-start(bf16[64,1664]{1,0:T(8,128)(2,1)S(1)} %get-tuple-element.67), channel_id=1, source_target_pairs={{0,2},{1,3},{16,18},{17,19},{32,34},{33,35},{48,50},{49,51},{4,6},... | collective-permute-start | bytes 638984 | tf_op jit(solution)/shard_map/ppermute | solution.py:33
  110.5 3.8 %collective-permute-done.23.r_ref = bf16[64,1664]{1,0:T(8,128)(2,1)S(1)} collective-permute-done((bf16[64,1664]{1,0:T(8,128)(2,1)S(1)}, bf16[64,1664]{1,0:T(8,128)(2,1)S(1)}, u32[]{:S(2)}, u32[]{:S(2)}) %collective-permute-start.23) | collective-permute-done | bytes 213024 | tf_op jit(solution)/shard_map/ppermute | solution.py:33
  114.3 1.5 %collective-permute-done.24.l_ref = bf16[64,1664]{1,0:T(8,128)(2,1)S(1)} collective-permute-done((bf16[64,1664]{1,0:T(8,128)(2,1)S(1)}, bf16[64,1664]{1,0:T(8,128)(2,1)S(1)}, u32[]{:S(2)}, u32[]{:S(2)}) %collective-permute-start.24) | collective-permute-done | bytes 213024 | tf_op jit(solution)/shard_map/ppermute | solution.py:33
  115.8 0.1 shard_map.114
  115.9 1.4 %collective-permute-start.25 = (bf16[32,1664]{1,0:T(8,128)(2,1)S(1)}, bf16[32,1664]{1,0:T(8,128)(2,1)S(1)}, u32[]{:S(2)}, u32[]{:S(2)}) collective-permute-start(bf16[32,1664]{1,0:T(8,128)(2,1)S(1)} %get-tuple-element.69), channel_id=1, source_target_pairs={{0,4},{1,5},{16,20},{17,21},{32,36},{33,37},{48,52},{49,53},{4,8},... | collective-permute-start | bytes 319496 | tf_op jit(solution)/shard_map/ppermute | solution.py:33
  117.3 2.8 %collective-permute-start.26 = (bf16[32,1664]{1,0:T(8,128)(2,1)S(1)}, bf16[32,1664]{1,0:T(8,128)(2,1)S(1)}, u32[]{:S(2)}, u32[]{:S(2)}) collective-permute-start(bf16[32,1664]{1,0:T(8,128)(2,1)S(1)} %get-tuple-element.70), channel_id=1, source_target_pairs={{0,8},{1,9},{16,24},{17,25},{32,40},{33,41},{48,56},{49,57},{4,12}... | collective-permute-start | bytes 319496 | tf_op jit(solution)/shard_map/ppermute | solution.py:33
  120.1 0.5 collective-permute-start.27
  121.2 0.7 collective-permute-done.25.s1
  121.9 2.0 %collective-permute-done.26.s2 = bf16[32,1664]{1,0:T(8,128)(2,1)S(1)} collective-permute-done((bf16[32,1664]{1,0:T(8,128)(2,1)S(1)}, bf16[32,1664]{1,0:T(8,128)(2,1)S(1)}, u32[]{:S(2)}, u32[]{:S(2)}) %collective-permute-start.26) | collective-permute-done | bytes 106528 | tf_op jit(solution)/shard_map/ppermute | solution.py:33
  123.9 0.9 collective-permute-done.27.s3
  124.8 0.9 shard_map.115
  (55 shorter events, 0.2 us)
Async XLA Ops:
  0.6 41.8 %collective-permute-start.9 = (bf16[800,5120]{1,0:T(8,128)(2,1)}, bf16[800,5120]{1,0:T(8,128)(2,1)}, u32[]{:S(2)}, u32[]{:S(2)}) collective-permute-start(bf16[800,5120]{1,0:T(8,128)(2,1)} %bitcast.27), channel_id=1, source_target_pairs={{0,1},{1,0},{16,17},{17,16},{32,33},{33,32},{48,49},{49,48},{4,5},... | collective-permute-start | bytes 24576008 | tf_op jit(solution)/shard_map/ppermute | solution.py:33
  0.7 1.0 copy-start.12
  2.1 0.8 copy-start.2
  2.9 13.2 %collective-permute-start.1 = (bf16[16,5120]{1,0:T(8,128)(2,1)S(1)}, bf16[16,5120]{1,0:T(8,128)(2,1)S(1)}, u32[]{:S(2)}, u32[]{:S(2)}) collective-permute-start(bf16[16,5120]{1,0:T(8,128)(2,1)S(1)} %get-tuple-element.39), channel_id=1, source_target_pairs={{0,2},{1,3},{16,18},{17,19},{32,34},{33,35},{48,50},{49,51},{4,6},... | collective-permute-start | bytes 491528 | tf_op jit(solution)/shard_map/ppermute | solution.py:33
  4.5 11.6 %collective-permute-start.2 = (bf16[16,5120]{1,0:T(8,128)(2,1)S(1)}, bf16[16,5120]{1,0:T(8,128)(2,1)S(1)}, u32[]{:S(2)}, u32[]{:S(2)}) collective-permute-start(bf16[16,5120]{1,0:T(8,128)(2,1)S(1)} %get-tuple-element.40), channel_id=1, source_target_pairs={{0,66},{1,67},{16,82},{17,83},{32,98},{33,99},{48,114},{49,115},{4... | collective-permute-start | bytes 491528 | tf_op jit(solution)/shard_map/ppermute | solution.py:33
  6.1 19.1 %collective-permute-start = (bf16[32,5120]{1,0:T(8,128)(2,1)S(1)}, bf16[32,5120]{1,0:T(8,128)(2,1)S(1)}, u32[]{:S(2)}, u32[]{:S(2)}) collective-permute-start(bf16[32,5120]{1,0:T(8,128)(2,1)S(1)} %get-tuple-element.42.refs_0_), channel_id=1, source_target_pairs={{0,12},{1,13},{16,28},{17,29},{32,44},{33,45},{48,60},{49,61},{4,0... | collective-permute-start | bytes 983048 | tf_op jit(solution)/shard_map/ppermute | solution.py:33
  9.2 16.0 %collective-permute-start.4 = (bf16[32,5120]{1,0:T(8,128)(2,1)S(1)}, bf16[32,5120]{1,0:T(8,128)(2,1)S(1)}, u32[]{:S(2)}, u32[]{:S(2)}) collective-permute-start(bf16[32,5120]{1,0:T(8,128)(2,1)S(1)} %get-tuple-element.42.refs_0_), channel_id=1, source_target_pairs={{0,4},{1,5},{16,20},{17,21},{32,36},{33,37},{48,52},{49,53},{4,8},... | collective-permute-start | bytes 983048 | tf_op jit(solution)/shard_map/ppermute | solution.py:33
  9.2 3.3 %copy-start = (bf16[800,5120]{1,0:T(8,128)(2,1)S(1)}, bf16[800,5120]{1,0:T(8,128)(2,1)}, u32[]{:S(2)}) copy-start(bf16[800,5120]{1,0:T(8,128)(2,1)} %f_ref.1) | copy-start | bytes 24576004
  12.6 3.5 %copy-start.13 = (bf16[32,1280]{1,0:T(8,128)(2,1)S(1)}, bf16[32,1280]{1,0:T(8,128)(2,1)}, u32[]{:S(2)}) copy-start(bf16[32,1280]{1,0:T(8,128)(2,1)} %param.13) | copy-start | bytes 245764
  16.1 4.8 %collective-permute-start.10 = (bf16[32,1280]{1,0:T(8,128)(2,1)S(1)}, bf16[32,1280]{1,0:T(8,128)(2,1)S(1)}, u32[]{:S(2)}, u32[]{:S(2)}) collective-permute-start(bf16[32,1280]{1,0:T(8,128)(2,1)S(1)} %copy-done.13), channel_id=1, source_target_pairs={{0,16},{1,17},{16,0},{17,1},{32,48},{33,49},{48,32},{49,33},{4,20}... | collective-permute-start | bytes 245768 | tf_op jit(solution)/shard_map/ppermute | solution.py:33
  18.7 11.5 %collective-permute-start.3 = (bf16[32,5120]{1,0:T(8,128)(2,1)S(1)}, bf16[32,5120]{1,0:T(8,128)(2,1)S(1)}, u32[]{:S(2)}, u32[]{:S(2)}) collective-permute-start(bf16[32,5120]{1,0:T(8,128)(2,1)S(1)} %get-tuple-element.42.refs_0_), channel_id=1, source_target_pairs={{0,8},{1,9},{16,24},{17,25},{32,40},{33,41},{48,56},{49,57},{4,12}... | collective-permute-start | bytes 983048 | tf_op jit(solution)/shard_map/ppermute | solution.py:33
  20.9 9.3 %copy-start.14 = (bf16[32,1280]{1,0:T(8,128)(2,1)}, bf16[32,1280]{1,0:T(8,128)(2,1)S(1)}, u32[]{:S(2)}) copy-start(bf16[32,1280]{1,0:T(8,128)(2,1)S(1)} %collective-permute-done.10) | copy-start | bytes 245764
  20.9 7.0 %collective-permute-start.11 = (bf16[64,1280]{1,0:T(8,128)(2,1)S(1)}, bf16[64,1280]{1,0:T(8,128)(2,1)S(1)}, u32[]{:S(2)}, u32[]{:S(2)}) collective-permute-start(bf16[64,1280]{1,0:T(8,128)(2,1)S(1)} %pad_maximum_fusion.1), channel_id=1, source_target_pairs={{0,32},{1,33},{16,48},{17,49},{32,0},{33,1},{48,16},{49,17},{4,36}... | collective-permute-start | bytes 491528 | tf_op jit(solution)/shard_map/ppermute | solution.py:33
  25.2 17.2 %copy-start.4 = (bf16[32,5120]{1,0:T(8,128)(2,1)}, bf16[32,5120]{1,0:T(8,128)(2,1)S(1)}, u32[]{:S(2)}) copy-start(bf16[32,5120]{1,0:T(8,128)(2,1)S(1)} %collective-permute-done.refs_0_.refs_1_) | copy-start | bytes 983044
  25.3 17.2 %copy-start.5 = (bf16[32,5120]{1,0:T(8,128)(2,1)}, bf16[32,5120]{1,0:T(8,128)(2,1)S(1)}, u32[]{:S(2)}) copy-start(bf16[32,5120]{1,0:T(8,128)(2,1)S(1)} %collective-permute-done.4.refs_1_.refs_3_) | copy-start | bytes 983044
  25.3 9.8 %collective-permute-start.5 = (bf16[32,5120]{1,0:T(8,128)(2,1)S(1)}, bf16[32,5120]{1,0:T(8,128)(2,1)S(1)}, u32[]{:S(2)}, u32[]{:S(2)}) collective-permute-start(bf16[32,5120]{1,0:T(8,128)(2,1)S(1)} %get-tuple-element.43), channel_id=1, source_target_pairs={{0,2},{1,3},{16,18},{17,19},{32,34},{33,35},{48,50},{49,51},{4,6},... | collective-permute-start | bytes 983048 | tf_op jit(solution)/shard_map/ppermute | solution.py:33
  27.9 2.3 %copy-start.16 = (bf16[64,1280]{1,0:T(8,128)(2,1)}, bf16[64,1280]{1,0:T(8,128)(2,1)S(1)}, u32[]{:S(2)}) copy-start(bf16[64,1280]{1,0:T(8,128)(2,1)S(1)} %collective-permute-done.11) | copy-start | bytes 491524
  28.6 13.8 %collective-permute-start.12 = (bf16[800,2688]{1,0:T(8,128)(2,1)}, bf16[800,2688]{1,0:T(8,128)(2,1)}, u32[]{:S(2)}, u32[]{:S(2)}) collective-permute-start(bf16[800,2688]{1,0:T(8,128)(2,1)} %get-tuple-element.49.refs_13_.f_ref), channel_id=1, source_target_pairs={{0,1},{1,0},{16,17},{17,16},{32,33},{33,32},{48,49},{49,48},{4,5},... | collective-permute-start | bytes 12902408 | tf_op jit(solution)/shard_map/ppermute | solution.py:33
  28.6 10.5 %collective-permute-start.7 = (bf16[32,5120]{1,0:T(8,128)(2,1)S(1)}, bf16[32,5120]{1,0:T(8,128)(2,1)S(1)}, u32[]{:S(2)}, u32[]{:S(2)}) collective-permute-start(bf16[32,5120]{1,0:T(8,128)(2,1)S(1)} %get-tuple-element.45), channel_id=1, source_target_pairs={{0,66},{1,67},{16,82},{17,83},{32,98},{33,99},{48,114},{49,115},{4... | collective-permute-start | bytes 983048 | tf_op jit(solution)/shard_map/ppermute | solution.py:33
  30.2 12.3 %copy-start.6 = (bf16[32,5120]{1,0:T(8,128)(2,1)}, bf16[32,5120]{1,0:T(8,128)(2,1)S(1)}, u32[]{:S(2)}) copy-start(bf16[32,5120]{1,0:T(8,128)(2,1)S(1)} %collective-permute-done.3.refs_0_.refs_2_) | copy-start | bytes 983044
  30.2 8.0 %collective-permute-start.6 = (bf16[16,5120]{1,0:T(8,128)(2,1)S(1)}, bf16[16,5120]{1,0:T(8,128)(2,1)S(1)}, u32[]{:S(2)}, u32[]{:S(2)}) collective-permute-start(bf16[16,5120]{1,0:T(8,128)(2,1)S(1)} %get-tuple-element.44), channel_id=1, source_target_pairs={{0,2},{1,3},{16,18},{17,19},{32,34},{33,35},{48,50},{49,51},{4,6},... | collective-permute-start | bytes 491528 | tf_op jit(solution)/shard_map/ppermute | solution.py:33
  35.1 7.2 %copy-start.17 = (bf16[32,5120]{1,0:T(8,128)(2,1)}, bf16[32,5120]{1,0:T(8,128)(2,1)S(1)}, u32[]{:S(2)}) copy-start(bf16[32,5120]{1,0:T(8,128)(2,1)S(1)} %collective-permute-done.5.refs_5_) | copy-start | bytes 983044
  35.1 7.2 %collective-permute-start.8 = (bf16[16,5120]{1,0:T(8,128)(2,1)S(1)}, bf16[16,5120]{1,0:T(8,128)(2,1)S(1)}, u32[]{:S(2)}, u32[]{:S(2)}) collective-permute-start(bf16[16,5120]{1,0:T(8,128)(2,1)S(1)} %get-tuple-element.46), channel_id=1, source_target_pairs={{0,66},{1,67},{16,82},{17,83},{32,98},{33,99},{48,114},{49,115},{4... | collective-permute-start | bytes 491528 | tf_op jit(solution)/shard_map/ppermute | solution.py:33
  39.1 3.1 %copy-start.18 = (bf16[32,5120]{1,0:T(8,128)(2,1)}, bf16[32,5120]{1,0:T(8,128)(2,1)S(1)}, u32[]{:S(2)}) copy-start(bf16[32,5120]{1,0:T(8,128)(2,1)S(1)} %collective-permute-done.7.refs_8_) | copy-start | bytes 983044
  42.3 20.2 %collective-permute-start.13 = (bf16[800,2560]{1,0:T(8,128)(2,1)}, bf16[800,2560]{1,0:T(8,128)(2,1)}, u32[]{:S(2)}, u32[]{:S(2)}) collective-permute-start(bf16[800,2560]{1,0:T(8,128)(2,1)} %get-tuple-element.53.fb_ref), channel_id=1, source_target_pairs={{0,1},{1,0},{16,17},{17,16},{32,33},{33,32},{48,49},{49,48},{4,5},... | collective-permute-start | bytes 12288008 | tf_op jit(solution)/shard_map/ppermute | solution.py:33
  42.4 20.0 %copy-start.3 = (f32[32,5120]{1,0:T(8,128)S(1)}, f32[32,5120]{1,0:T(8,128)}, u32[]{:S(2)}) copy-start(f32[32,5120]{1,0:T(8,128)} %copy-done.2) | copy-start | bytes 1966084
  59.0 46.6 %collective-permute-start.22 = (bf16[320,1536]{1,0:T(8,128)(2,1)}, bf16[320,1536]{1,0:T(8,128)(2,1)}, u32[]{:S(2)}, u32[]{:S(2)}) collective-permute-start(bf16[320,1536]{1,0:T(8,128)(2,1)} %w_ref), channel_id=1, source_target_pairs={{0,1},{1,0},{16,17},{17,16},{32,33},{33,32},{48,49},{49,48},{4,5},... | collective-permute-start | bytes 2949128 | tf_op jit(solution)/shard_map/ppermute | solution.py:33
  59.6 14.9 %collective-permute-start.16 = (bf16[2,128,640]{2,1,0:T(8,128)(2,1)}, bf16[2,128,640]{2,1,0:T(8,128)(2,1)}, u32[]{:S(2)}, u32[]{:S(2)}) collective-permute-start(bf16[2,128,640]{2,1,0:T(8,128)(2,1)} %get-tuple-element.57), channel_id=1, source_target_pairs={{0,66},{1,67},{16,82},{17,83},{32,98},{33,99},{48,114},{49,115},{4... | collective-permute-start | bytes 983048 | tf_op jit(solution)/shard_map/ppermute | solution.py:33
  62.4 13.6 %collective-permute-start.17 = (bf16[2,128,640]{2,1,0:T(8,128)(2,1)}, bf16[2,128,640]{2,1,0:T(8,128)(2,1)}, u32[]{:S(2)}, u32[]{:S(2)}) collective-permute-start(bf16[2,128,640]{2,1,0:T(8,128)(2,1)} %get-tuple-element.58), channel_id=1, source_target_pairs={{0,2},{1,3},{16,18},{17,19},{32,34},{33,35},{48,50},{49,51},{4,6},... | collective-permute-start | bytes 983048 | tf_op jit(solution)/shard_map/ppermute | solution.py:33
  62.4 1.1 copy-start.11
  71.1 26.1 %copy-start.19 = (s32[32]{0:T(128)S(1)}, s32[32]{0:T(128)}, u32[]{:S(2)}) copy-start(s32[32]{0:T(128)} %param.16) | copy-start | bytes 388
  71.1 26.1 %copy-start.20 = (s32[32,1]{0,1:T(1,128)S(1)}, s32[32,1]{0,1:T(1,128)}, u32[]{:S(2)}) copy-start(s32[32,1]{0,1:T(1,128)} %param.15) | copy-start | bytes 388
  71.2 26.1 %copy-start.15 = (bf16[32,1280]{1,0:T(8,128)(2,1)S(1)}, bf16[32,1280]{1,0:T(8,128)(2,1)}, u32[]{:S(2)}) copy-start(bf16[32,1280]{1,0:T(8,128)(2,1)} %copy-done.14) | copy-start | bytes 245764
  71.2 17.3 %collective-permute-start.14 = (bf16[2,128,640]{2,1,0:T(8,128)(2,1)}, bf16[2,128,640]{2,1,0:T(8,128)(2,1)S(1)}, u32[]{:S(2)}, u32[]{:S(2)}) collective-permute-start(bf16[2,128,640]{2,1,0:T(8,128)(2,1)} %get-tuple-element.55), channel_id=1, source_target_pairs={{0,66},{1,67},{16,82},{17,83},{32,98},{33,99},{48,114},{49,115},{4... | collective-permute-start | bytes 983048 | tf_op jit(solution)/shard_map/ppermute | solution.py:33
  74.5 17.3 %collective-permute-start.15 = (bf16[2,128,640]{2,1,0:T(8,128)(2,1)}, bf16[2,128,640]{2,1,0:T(8,128)(2,1)S(1)}, u32[]{:S(2)}, u32[]{:S(2)}) collective-permute-start(bf16[2,128,640]{2,1,0:T(8,128)(2,1)} %get-tuple-element.56), channel_id=1, source_target_pairs={{0,2},{1,3},{16,18},{17,19},{32,34},{33,35},{48,50},{49,51},{4,6},... | collective-permute-start | bytes 983048 | tf_op jit(solution)/shard_map/ppermute | solution.py:33
  74.5 22.8 %collective-permute-start.21 = (bf16[128,1280]{1,0:T(8,128)(2,1)}, bf16[128,1280]{1,0:T(8,128)(2,1)}, u32[]{:S(2)}, u32[]{:S(2)}) collective-permute-start(bf16[128,1280]{1,0:T(8,128)(2,1)} %constant_dynamic-update-slice_fusion), channel_id=1, source_target_pairs={{0,64},{1,65},{16,80},{17,81},{32,96},{33,97},{48,112},{49,113},{4... | collective-permute-start | bytes 983048 | tf_op jit(solution)/shard_map/ppermute | solution.py:33
  78.0 23.9 %collective-permute-start.18 = (bf16[256,640]{1,0:T(8,128)(2,1)}, bf16[256,640]{1,0:T(8,128)(2,1)}, u32[]{:S(2)}, u32[]{:S(2)}) collective-permute-start(bf16[256,640]{1,0:T(8,128)(2,1)} %get-tuple-element.59), channel_id=1, source_target_pairs={{0,4},{1,5},{16,20},{17,21},{32,36},{33,37},{48,52},{49,53},{4,8},... | collective-permute-start | bytes 983048 | tf_op jit(solution)/shard_map/ppermute | solution.py:33
  88.4 8.8 %copy-start.7 = (bf16[2,128,640]{2,1,0:T(8,128)(2,1)}, bf16[2,128,640]{2,1,0:T(8,128)(2,1)S(1)}, u32[]{:S(2)}) copy-start(bf16[2,128,640]{2,1,0:T(8,128)(2,1)S(1)} %collective-permute-done.14.up_ref) | copy-start | bytes 983044
  91.8 5.5 %copy-start.9 = (bf16[2,128,640]{2,1,0:T(8,128)(2,1)}, bf16[2,128,640]{2,1,0:T(8,128)(2,1)S(1)}, u32[]{:S(2)}) copy-start(bf16[2,128,640]{2,1,0:T(8,128)(2,1)S(1)} %collective-permute-done.15.low_ref) | copy-start | bytes 983044
  92.6 9.3 %collective-permute-start.19 = (bf16[256,640]{1,0:T(8,128)(2,1)}, bf16[256,640]{1,0:T(8,128)(2,1)}, u32[]{:S(2)}, u32[]{:S(2)}) collective-permute-start(bf16[256,640]{1,0:T(8,128)(2,1)} %shard_map.111), channel_id=1, source_target_pairs={{0,8},{1,9},{16,24},{17,25},{32,40},{33,41},{48,56},{49,57},{4,12}... | collective-permute-start | bytes 983048 | tf_op jit(solution)/shard_map/ppermute | solution.py:33
  94.8 10.9 %collective-permute-start.20 = (bf16[256,640]{1,0:T(8,128)(2,1)}, bf16[256,640]{1,0:T(8,128)(2,1)}, u32[]{:S(2)}, u32[]{:S(2)}) collective-permute-start(bf16[256,640]{1,0:T(8,128)(2,1)} %get-tuple-element.60), channel_id=1, source_target_pairs={{0,12},{1,13},{16,28},{17,29},{32,44},{33,45},{48,60},{49,61},{4,0... | collective-permute-start | bytes 983048 | tf_op jit(solution)/shard_map/ppermute | solution.py:33
  98.4 2.1 %copy-start.1 = (bf16[1280,1536]{1,0:T(8,128)(2,1)S(1)}, bf16[1280,1536]{1,0:T(8,128)(2,1)}, u32[]{:S(2)}) copy-start(bf16[1280,1536]{1,0:T(8,128)(2,1)} %proj_ref.1) | copy-start | bytes 11796484
  100.6 5.1 %copy-start.8 = (bf16[2,128,640]{2,1,0:T(8,128)(2,1)S(1)}, bf16[2,128,640]{2,1,0:T(8,128)(2,1)}, u32[]{:S(2)}) copy-start(bf16[2,128,640]{2,1,0:T(8,128)(2,1)} %copy-done.7) | copy-start | bytes 983044
  100.6 5.1 %copy-start.10 = (bf16[2,128,640]{2,1,0:T(8,128)(2,1)S(1)}, bf16[2,128,640]{2,1,0:T(8,128)(2,1)}, u32[]{:S(2)}) copy-start(bf16[2,128,640]{2,1,0:T(8,128)(2,1)} %copy-done.9) | copy-start | bytes 983044
  108.4 5.9 %collective-permute-start.23 = (bf16[64,1664]{1,0:T(8,128)(2,1)S(1)}, bf16[64,1664]{1,0:T(8,128)(2,1)S(1)}, u32[]{:S(2)}, u32[]{:S(2)}) collective-permute-start(bf16[64,1664]{1,0:T(8,128)(2,1)S(1)} %get-tuple-element.66), channel_id=1, source_target_pairs={{0,66},{1,67},{16,82},{17,83},{32,98},{33,99},{48,114},{49,115},{4... | collective-permute-start | bytes 638984 | tf_op jit(solution)/shard_map/ppermute | solution.py:33
  108.8 7.1 %collective-permute-start.24 = (bf16[64,1664]{1,0:T(8,128)(2,1)S(1)}, bf16[64,1664]{1,0:T(8,128)(2,1)S(1)}, u32[]{:S(2)}, u32[]{:S(2)}) collective-permute-start(bf16[64,1664]{1,0:T(8,128)(2,1)S(1)} %get-tuple-element.67), channel_id=1, source_target_pairs={{0,2},{1,3},{16,18},{17,19},{32,34},{33,35},{48,50},{49,51},{4,6},... | collective-permute-start | bytes 638984 | tf_op jit(solution)/shard_map/ppermute | solution.py:33
  115.9 6.0 %collective-permute-start.25 = (bf16[32,1664]{1,0:T(8,128)(2,1)S(1)}, bf16[32,1664]{1,0:T(8,128)(2,1)S(1)}, u32[]{:S(2)}, u32[]{:S(2)}) collective-permute-start(bf16[32,1664]{1,0:T(8,128)(2,1)S(1)} %get-tuple-element.69), channel_id=1, source_target_pairs={{0,4},{1,5},{16,20},{17,21},{32,36},{33,37},{48,52},{49,53},{4,8},... | collective-permute-start | bytes 319496 | tf_op jit(solution)/shard_map/ppermute | solution.py:33
  117.3 6.6 %collective-permute-start.26 = (bf16[32,1664]{1,0:T(8,128)(2,1)S(1)}, bf16[32,1664]{1,0:T(8,128)(2,1)S(1)}, u32[]{:S(2)}, u32[]{:S(2)}) collective-permute-start(bf16[32,1664]{1,0:T(8,128)(2,1)S(1)} %get-tuple-element.70), channel_id=1, source_target_pairs={{0,8},{1,9},{16,24},{17,25},{32,40},{33,41},{48,56},{49,57},{4,12}... | collective-permute-start | bytes 319496 | tf_op jit(solution)/shard_map/ppermute | solution.py:33
  120.1 4.7 %collective-permute-start.27 = (bf16[32,1664]{1,0:T(8,128)(2,1)S(1)}, bf16[32,1664]{1,0:T(8,128)(2,1)S(1)}, u32[]{:S(2)}, u32[]{:S(2)}) collective-permute-start(bf16[32,1664]{1,0:T(8,128)(2,1)S(1)} %get-tuple-element.71), channel_id=1, source_target_pairs={{0,12},{1,13},{16,28},{17,29},{32,44},{33,45},{48,60},{49,61},{4,0... | collective-permute-start | bytes 319496 | tf_op jit(solution)/shard_map/ppermute | solution.py:33

commit v2 on v1

v2 whole, which is shorter than its diff:
```python
import functools

import jax
import jax.numpy as jnp
from jax import lax
from jax.experimental import pallas as pl
from jax.experimental.pallas import tpu as pltpu
from jax.sharding import PartitionSpec as P

eps = 1e-06
sharpness = 40.0
AXES = ("dp", "tensor")
BLK = 640
EW = 1536 + 128
f32 = jnp.float32
bf16 = jnp.bfloat16


def moves(dx=0, dy=0, mz=0, flip=False):
    def place(x, y, z, c):
        return ((x // 2) * 4 + z) * 16 + y * 4 + (x % 2) * 2 + c

    return [
        (place(x, y, z, c), place((x + dx) % 4, (y + dy) % 4, z ^ mz, c ^ int(flip)))
        for x in range(4)
        for y in range(4)
        for z in range(4)
        for c in range(2)
    ]


def shift(value, **step):
    return lax.ppermute(value, AXES, moves(**step))


def after(value, *others):
    return lax.optimization_barrier((value,) + others)[0]


NT = (((1,), (1,)), ((), ()))
TN = (((0,), (0,)), ((), ()))
VM = pl.BlockSpec(memory_space=pltpu.VMEM)
SM = pl.BlockSpec(memory_space=pltpu.SMEM)
HB = pl.BlockSpec(memory_space=pltpu.HBM)


def struct(shape, dtype):
    return jax.ShapeDtypeStruct(shape, dtype)


def call(body, scalars, arrays, outs, scratch=(), remote=0, limit=12, size=1024):
    inside = len(arrays) - remote
    return pl.pallas_call(
        body,
        in_specs=[SM] * len(scalars) + [VM] * inside + [HB] * remote,
        out_specs=(VM,) * len(outs),
        out_shape=outs,
        scratch_shapes=scratch,
        compiler_params=pltpu.CompilerParams(vmem_limit_bytes=limit * 1024 * 1024),
        cost_estimate=pl.CostEstimate(flops=1024, bytes_accessed=size, transcendentals=0),
    )(*scalars, *arrays)


def norm_kernel(cls_ref, normed_ref, centred_ref):
    values = cls_ref[...].astype(f32)
    centred = values - jnp.mean(values, axis=-1, keepdims=True)
    variance = jnp.mean(centred * centred, axis=-1, keepdims=True)
    centred_ref[...] = centred
    normed_ref[...] = (centred * lax.rsqrt(variance + eps)).astype(bf16)


def norm_call(cls_states):
    outs = (struct(cls_states.shape, bf16), struct(cls_states.shape, f32))
    return call(norm_kernel, (), (cls_states,), outs)


def halves_kernel(n0, n1, n2, n3, r_ref, l_ref):
    for k, ref in enumerate((n0, n1, n2, n3)):
        r_ref[16 * k : 16 * k + 16] = ref[:16]
        l_ref[16 * k : 16 * k + 16] = ref[16:]


def halves_call(*ins):
    outs = (struct((64, ins[0].shape[1]), bf16),) * 2
    return call(halves_kernel, (), ins, outs)


def mean_kernel(f_ref, out_ref):
    mean = jnp.sum(f_ref[...].astype(f32), axis=-1, keepdims=True) / f_ref.shape[1]
    high = mean.astype(bf16).astype(f32)
    lane = lax.broadcasted_iota(jnp.int32, out_ref.shape, 1)
    out_ref[...] = jnp.where(lane == 0, high, jnp.where(lane == 1, mean - high, 0.0)).astype(bf16)


def mean_call(f):
    return call(mean_kernel, (), (f,), (struct((f.shape[0], 128), bf16),), size=16 * 1024 * 1024)[0]


def start(copies):
    for copy in copies:
        copy.start()


def wait(copies):
    for copy in copies:
        copy.wait()


def stage_kernel(w_ref, v_ref, out_ref, sems):
    copies = [
        pltpu.make_async_copy(ref.at[pl.ds(at, 400)], out_ref.at[pl.ds(base + at, 400)], sems.at[(base + at) // 400])
        for base, ref in ((0, w_ref), (800, v_ref))
        for at in (0, 400)
    ]
    start(copies)
    wait(copies)


def stage_call(w, v):
    outs = (struct((1600, w.shape[1]), bf16),)
    return call(
        stage_kernel, (), (w, v), outs, [pltpu.SemaphoreType.DMA((4,))], remote=2, limit=4, size=32 * 1024 * 1024
    )[0]


def columns_kernel(cols, f_ref, o_ref, out_ref, sems):
    copies = []
    for q in range(4):
        at = pl.ds(pl.multiple_of(cols[q] * BLK, 128), BLK)
        for k, ref in enumerate((f_ref, o_ref)):
            to = out_ref.at[pl.ds(800 * k, 800), pl.ds(BLK * q, BLK)]
            copies.append(pltpu.make_async_copy(ref.at[:, at], to, sems.at[2 * q + k]))
    start(copies)
    wait(copies)


def columns_call(cols, f, o):
    outs = (struct((1600, 4 * BLK), bf16),)
    return call(
        columns_kernel, (cols,), (f, o), outs, [pltpu.SemaphoreType.DMA((8,))], remote=2, limit=4, size=16 * 1024 * 1024
    )[0]


def fc2_pair(cols, first, h_ref, mean_ref, f_ref, res_ref):
    pair = lax.dot_general(h_ref[...], f_ref[:, BLK * first : BLK * first + 2 * BLK], TN, preferred_element_type=f32)
    for q in range(2):
        part = pair[:, BLK * q : BLK * q + BLK] - mean_ref[:, :1]
        res = res_ref[:, pl.ds(pl.multiple_of(cols[first + q] * BLK, 128), BLK)]
        upper = jnp.concatenate([part[0:16] + res[0:16], part[16:128]], axis=0)
        lower = jnp.concatenate([part[128:192], part[192:208] + res[16:32], part[208:256]], axis=0)
        yield q, upper, lower


def fc1_kernel(w_ref, wm_ref, vm_ref, r, b, a, l, h_ref, mean_ref, rows, sems):
    parts = [pltpu.make_async_copy(ref, rows.at[pl.ds(64 * k, 64)], sems.at[k]) for k, ref in enumerate((r, b, a, l))]
    start(parts)
    wait(parts)
    for at in range(0, 1600, 400):
        z = lax.dot_general(w_ref[at : at + 400], rows[...], NT, preferred_element_type=f32)
        act = 0.5 * z * (1.0 + lax.erf(z * (0.5**0.5)))
        h_ref[at : at + 400] = act.astype(bf16)
    means = lax.dot_general(h_ref[0:800], wm_ref[...], TN, preferred_element_type=f32) + lax.dot_general(
        h_ref[800:1600], vm_ref[...], TN, preferred_element_type=f32
    )
    mean_ref[...] = jnp.broadcast_to(jnp.sum(means, axis=-1, keepdims=True), mean_ref.shape)


def fc1_call(rows, w, w_mean, v_mean):
    outs = (struct((1600, 256), bf16), struct((256, 128), f32))
    return call(
        fc1_kernel,
        (),
        (w, w_mean, v_mean, *rows),
        outs,
        scratch=[pltpu.VMEM((256, w.shape[1]), bf16), pltpu.SemaphoreType.DMA((4,))],
        remote=4,
        limit=10,
    )


def away_kernel(cols, h_ref, mean_ref, res_ref, f_ref, *outs):
    for k in range(2):
        for q, upper, lower in fc2_pair(cols, 2 * k, h_ref, mean_ref, f_ref, res_ref):
            outs[2 * k][q] = upper.astype(bf16)
            outs[2 * k + 1][q] = lower.astype(bf16)


def away_call(cols, h, h_mean, centred, f):
    outs = (struct((2, 128, BLK), bf16),) * 4
    return call(away_kernel, (cols,), (h, h_mean, centred, f), outs, limit=20)


def own_kernel(cols, h_ref, mean_ref, res_ref, f_ref, o_ref, own_ref, buf, sems):
    loads = []
    for q in range(4):
        at = pl.ds(pl.multiple_of(cols[q] * BLK, 128), BLK)
        for k, ref in enumerate((f_ref, o_ref)):
            to = buf.at[pl.ds(800 * k, 800), pl.ds(BLK * q, BLK)]
            loads.append(pltpu.make_async_copy(ref.at[:, at], to, sems.at[2 * q + k]))
    start(loads[:4])
    for k in range(2):
        wait(loads[4 * k : 4 * k + 4])
        if k == 0:
            start(loads[4:])
        for q, upper, lower in fc2_pair(cols, 2 * k, h_ref, mean_ref, buf, res_ref):
            own_ref[2 * k + q, 0:128] = upper
            own_ref[2 * k + q, 128:256] = lower


def own_call(cols, h, h_mean, centred, f, o):
    return call(
        own_kernel,
        (cols,),
        (h, h_mean, centred, f, o),
        (struct((4, 256, BLK), f32),),
        scratch=[pltpu.VMEM((1600, 4 * BLK), bf16), pltpu.SemaphoreType.DMA((8,))],
        remote=2,
        limit=29,
        size=16 * 1024 * 1024,
    )[0]


def add_kernel(place, own_ref, up_ref, low_ref, *outs):
    for k, out in enumerate(outs):
        out[0:128] = (own_ref[place + k, :128] + up_ref[k].astype(f32)).astype(bf16)
        out[128:256] = (own_ref[place + k, 128:] + low_ref[k].astype(f32)).astype(bf16)


def add_call(place, count, own, up, low):
    outs = (struct((256, BLK), bf16),) * count
    return call(functools.partial(add_kernel, place), (), (own, up, low), outs)


def proj_kernel(core, own_ref, up_ref, low_ref, t1, t2, t3, w_ref, o_ref, home_ref, a_ref, b_ref, total, weight):
    weight[pl.ds(pl.multiple_of(core[0] * 320, 64), 320)] = w_ref[...]
    weight[pl.ds(pl.multiple_of((1 - core[0]) * 320, 64), 320)] = o_ref[...]
    total[0:128] = own_ref[3, :128] + up_ref[1].astype(f32)
    total[128:256] = own_ref[3, 128:] + low_ref[1].astype(f32)
    for k, got in ((1, t1), (2, t2), (3, t3)):
        for group in range(4):
            for j in range(4):
                mine = 64 * group + 16 * ((j - k) % 4)
                theirs = 64 * group + 16 * j
                total[mine : mine + 16] += got[theirs : theirs + 16].astype(f32)
    x = total[...]
    squares = jnp.sum(x * x, axis=-1, keepdims=True)
    high = squares.astype(bf16).astype(f32)
    lane = lax.broadcasted_iota(jnp.int32, (256, 128), 1)
    extra = jnp.where(lane == 0, high, jnp.where(lane == 1, squares - high, 0.0)).astype(bf16)
    e = jnp.dot(x.astype(bf16), weight[...], preferred_element_type=f32).astype(bf16)
    for k in range(4):
        for at, base in ((0, 0), (16, 192)):
            src = slice(base + 16 * k, base + 16 * k + 16)
            home_ref[k, at : at + 16, :1536] = e[src]
            home_ref[k, at : at + 16, 1536:] = extra[src]
    b_ref[:, :1536] = e[64:128]
    b_ref[:, 1536:] = extra[64:128]
    a_ref[:, :1536] = e[128:192]
    a_ref[:, 1536:] = extra[128:192]


def proj_call(core, own, up, low, ts, w, o):
    outs = (struct((4, 32, EW), bf16), struct((64, EW), bf16), struct((64, EW), bf16))
    return call(
        proj_kernel,
        (core,),
        (own, up, low, *ts, w, o),
        outs,
        scratch=[pltpu.VMEM((256, BLK), f32), pltpu.VMEM((BLK, 1536), bf16)],
    )


def pair_kernel(home_ref, r_ref, l_ref, s0, s1, s2, s3):
    for k, out in enumerate((s0, s1, s2, s3)):
        at = slice(16 * k, 16 * k + 16)
        out[0:16] = (home_ref[k, 0:16].astype(f32) + r_ref[at].astype(f32)).astype(out.dtype)
        out[16:32] = (home_ref[k, 16:32].astype(f32) + l_ref[at].astype(f32)).astype(out.dtype)


def pair_call(home, r, l):
    outs = (struct((32, EW), f32),) + (struct((32, EW), bf16),) * 3
    return call(pair_kernel, (), (home, r, l), outs)


def text_kernel(index_ref, pooled_ref, proj_ref, out_ref):
    count = pooled_ref.shape[0]
    lane = lax.broadcasted_iota(jnp.int32, (32, count), 1)
    picker = jnp.where(lane == index_ref[...], 1.0, 0.0).astype(bf16)
    values = jnp.dot(picker, pooled_ref[...], preferred_element_type=f32)
    centred = values - jnp.mean(values, axis=-1, keepdims=True)
    variance = jnp.mean(centred * centred, axis=-1, keepdims=True)
    normed = (centred * lax.rsqrt(variance + eps)).astype(bf16)
    u = jnp.dot(normed, proj_ref[...], preferred_element_type=f32)
    out_ref[...] = u * lax.rsqrt(jnp.sum(u * u, axis=-1, keepdims=True) + eps)


def text_call(index, pooled, text_proj):
    outs = (struct((32, text_proj.shape[1]), f32),)
    return call(
        text_kernel, (), (index, pooled, text_proj), outs
    )[0]


def last_kernel(threshold_ref, s0, s1, s2, s3, text_ref, filtered_ref, weight_ref):
    total = s0[...] + s1[...].astype(f32) + s2[...].astype(f32) + s3[...].astype(f32)
    squares = jnp.sum(total[:, 1536:], axis=-1, keepdims=True)
    scale = lax.rsqrt(squares / 5120.0 + eps)
    e = total[:, :1536] * scale
    unit = (e * lax.rsqrt(jnp.sum(e * e, axis=-1, keepdims=True) + eps)).astype(bf16).astype(f32)
    cosine = jnp.sum(unit * text_ref[...], axis=-1, keepdims=True)
    weight = jax.nn.sigmoid(sharpness * (cosine - threshold_ref[0]))
    filtered_ref[...] = (weight * unit).astype(bf16)
    row = lax.broadcasted_iota(jnp.int32, (32, 32), 0)
    column = lax.broadcasted_iota(jnp.int32, (32, 32), 1)
    weight_ref[...] = jnp.sum(jnp.where(row == column, weight, 0.0), axis=0, keepdims=True)


def last_call(parts, text, threshold):
    outs = (struct((32, 1536), bf16), struct((1, 32), f32))
    return call(last_kernel, (threshold,), (*parts, text), outs)


def shards(
    cls_states, fc1_weight, fc2_weight, proj_weight, text_pooled, text_proj, pair_owner, pair_slot, threshold
):
    d = lax.axis_index("dp")
    t = lax.axis_index("tensor")
    x_hi, z, y, x_lo, core = d // 4, d % 4, t // 4, (t // 2) % 2, t % 2

    fc1_rows = fc1_weight.T

    fc1_other = shift(fc1_rows, flip=True)
    normed, centred = norm_call(cls_states)
    n1, n3, n2 = shift(normed, dy=-1), shift(normed, dy=1), shift(normed, dy=2)
    pooled = jnp.concatenate([text_pooled, shift(text_pooled, dx=2)])
    w_mean = mean_call(fc2_weight)
    r, l = halves_call(normed, n1, after(n2, w_mean, pooled), n3)
    a, b = shift(r, dx=1), shift(l, dx=-1)
    fc2_other = shift(after(fc2_weight, r), flip=True)
    v_mean = shift(after(w_mean, r), flip=True)
    proj_other = shift(after(proj_weight, r), flip=True)
    fc1_both = stage_call(after(fc1_rows, r), fc1_other)

    def blocks(parity, *ks):
        return jnp.stack([2 * ((y + k) % 4) + parity for k in ks]).astype(jnp.int32)

    cols = blocks(1 - x_lo, 1, 3, 2, 0)
    fc2_both = columns_call(cols, fc2_weight, fc2_other)
    h, h_mean = fc1_call((r, after(b, fc2_both, proj_other), a, l), fc1_both, w_mean, v_mean)
    to_r, to_l, to_r2, to_l2 = away_call(cols, h, h_mean, centred, fc2_both)
    got_r, got_l = shift(to_l, dx=-1), shift(to_r, dx=1)
    got_r2, got_l2 = shift(to_l2, dx=-1), shift(to_r2, dx=1)
    pooled = after(pooled, to_r)
    pooled = jnp.concatenate([pooled, shift(pooled, mz=1)])
    pooled = jnp.concatenate([pooled, shift(pooled, mz=2)])
    own = own_call(blocks(x_lo, 1, 3, 2, 0), h, h_mean, centred, fc2_weight, fc2_other)
    s1, s3 = add_call(0, 2, own, got_r, got_l)
    t1, t3 = shift(s1, dy=1), shift(s3, dy=-1)
    (s2,) = add_call(2, 1, own, got_r2, got_l2)
    t2 = shift(s2, dy=2)

    owner = pair_owner[:, 0]
    relative = ((owner % 4) ^ z) * 2 + ((owner // 4) ^ x_hi)
    index = (relative * 32 + pair_slot).reshape(32, 1)
    text = text_call(after(index, s2), pooled, text_proj)

    core_index = core.astype(jnp.int32).reshape(1)
    home, e_a, e_b = proj_call(
        core_index, own, got_r2, got_l2, (t1, t2, t3), after(proj_weight, text), proj_other
    )
    s0, s1, s2, s3 = pair_call(home, shift(e_a, dx=-1), shift(e_b, dx=1))
    parts = (s0, shift(s1, dy=1), shift(s2, dy=2), shift(s3, dy=3))
    filtered, weight = last_call(parts, text, threshold)
    return filtered, weight.reshape(32)


def solution(mesh):
    placed = (
        P(("dp", "tensor"), None),
        P(None, "tensor"),
        P("tensor", None),
        P("tensor", None),
        P(("dp", "tensor"), None),
        P(),
        P(("dp", "tensor"), None),
        P(("dp", "tensor")),
        P(),
    )
    return jax.shard_map(
        shards,
        mesh=mesh,
        in_specs=placed,
        out_specs=(P(("dp", "tensor"), None), P(("dp", "tensor"))),
        check_vma=False,
    )
```

time: 126 us -> 121 us (0.960)
  waiting for transfers between devices: 37.1 us -> 28.7 us
  local copies, waits for them, and re-layouts: 10.6 us -> 16.8 us
  starting transfers between devices: 39.3 us -> 33.2 us
  Pallas kernels: 35.9 us -> 38.6 us
    ppermute x28 -> x24, waiting for transfers between devices: 37.1 us -> 28.7 us  [shift(): return lax.ppermute(value, AXES, moves(**step))]
    unnamed x44 -> x47, local copies, waits for them, and re-layouts: 9.72 us -> 16.7 us
    ppermute x28 -> x24, starting transfers between devices: 39.3 us -> 33.2 us  [shift(): return lax.ppermute(value, AXES, moves(**step))]
    pallas_call x12 -> x14, Pallas kernels: 35.9 us -> 38.6 us  [call(): pl.pallas_call(body, in_specs=[SM] * len(scalars) + [VM] * inside + [HB]...]
  transfers between devices with their start and end apart: 28 -> 24, of which waited for: 13 -> 11; matrix products, arithmetic and copies ran while one was open for 3% -> 3% of each run, Pallas kernels for 26% -> 19%
where the time goes in v2:
time: 121 us
  Pallas kernels  38.6 us (32%)
  starting transfers between devices  33.2 us (27%)
  waiting for transfers between devices  28.7 us (24%)
  local copies, waits for them, and re-layouts  16.8 us (14%)
  other arithmetic  2.1 us (2%)
  between operations  1.57 us (1%)
    pallas_call x14, Pallas kernels, call(): pl.pallas_call(body, in_specs=[SM] * len(scalars) + [VM] * inside + [HB]...  38.6 us
    ppermute x24, starting transfers between devices, shift(): return lax.ppermute(value, AXES, moves(**step))  33.2 us
    ppermute x24, waiting for transfers between devices, shift(): return lax.ppermute(value, AXES, moves(**step))  28.7 us
    unnamed x47, local copies, waits for them, and re-layouts  16.7 us
  transfers between devices with their start and end apart: 24, of which 11 were waited for; matrix products, arithmetic and copies ran while one was open for 3% of the time, Pallas kernels for 19%

profile of v2, /device:TPU:0, one launch (start us, length us, event | category | flops | bytes accessed | tf_op | source)
XLA Modules:
  0.0 121.0 jit_solution(16538595138140752614)
XLA Ops:
  0.6 1.0 copy-done.16
  1.6 0.3 shard_map.104
  2.0 3.2 %collective-permute-start = (bf16[32,5120]{1,0:T(8,128)(2,1)S(1)}, bf16[32,5120]{1,0:T(8,128)(2,1)S(1)}, u32[]{:S(2)}, u32[]{:S(2)}) collective-permute-start(bf16[32,5120]{1,0:T(8,128)(2,1)S(1)} %get-tuple-element.32.n0), channel_id=1, source_target_pairs={{0,12},{1,13},{16,28},{17,29},{32,44},{33,45},{48,60},{49,61},{4,0... | collective-permute-start | bytes 983048 | tf_op jit(solution)/shard_map/ppermute | solution.py:33
  5.1 0.6 collective-permute-start.1
  5.8 1.0 collective-permute-start.3
  6.7 3.0 %collective-permute-start.2 = (bf16[32,1280]{1,0:T(8,128)(2,1)}, bf16[32,1280]{1,0:T(8,128)(2,1)S(1)}, u32[]{:S(2)}, u32[]{:S(2)}) collective-permute-start(bf16[32,1280]{1,0:T(8,128)(2,1)} %param.13), channel_id=1, source_target_pairs={{0,64},{1,65},{16,80},{17,81},{32,96},{33,97},{48,112},{49,113},{4... | collective-permute-start | bytes 245768 | tf_op jit(solution)/shard_map/ppermute | solution.py:33
  9.8 0.0 collective-permute-start.4
  9.8 0.9 constant_dynamic-update-slice_fusion.1
  10.7 4.7 %shard_map.105.wm_ref = bf16[800,128]{1,0:T(8,128)(2,1)S(1)} custom-call(bf16[800,5120]{1,0:T(8,128)(2,1)} %f_ref.5), custom_call_target="tpu_custom_call" | custom-call | flops 1024 | bytes 16777216 | tf_op jit(solution)/shard_map/pallas_call | solution.py:53
  15.4 0.0 collective-permute-done.2
  15.5 1.9 %collective-permute-done.1.n2 = bf16[32,5120]{1,0:T(8,128)(2,1)S(1)} collective-permute-done((bf16[32,5120]{1,0:T(8,128)(2,1)S(1)}, bf16[32,5120]{1,0:T(8,128)(2,1)S(1)}, u32[]{:S(2)}, u32[]{:S(2)}) %collective-permute-start.1) | collective-permute-done | bytes 327712 | tf_op jit(solution)/shard_map/ppermute | solution.py:33
  17.3 1.8 %collective-permute-done.n1 = bf16[32,5120]{1,0:T(8,128)(2,1)S(1)} collective-permute-done((bf16[32,5120]{1,0:T(8,128)(2,1)S(1)}, bf16[32,5120]{1,0:T(8,128)(2,1)S(1)}, u32[]{:S(2)}, u32[]{:S(2)}) %collective-permute-start) | collective-permute-done | bytes 327712 | tf_op jit(solution)/shard_map/ppermute | solution.py:33
  19.1 3.7 %collective-permute-done.3.n3 = bf16[32,5120]{1,0:T(8,128)(2,1)S(1)} collective-permute-done((bf16[32,5120]{1,0:T(8,128)(2,1)S(1)}, bf16[32,5120]{1,0:T(8,128)(2,1)S(1)}, u32[]{:S(2)}, u32[]{:S(2)}) %collective-permute-start.3) | collective-permute-done | bytes 327712 | tf_op jit(solution)/shard_map/ppermute | solution.py:33
  22.8 1.0 shard_map.106
  23.8 0.0 collective-permute-start.7
  23.8 0.5 collective-permute-start.8
  24.3 2.8 %collective-permute-start.6 = (bf16[64,5120]{1,0:T(8,128)(2,1)}, bf16[64,5120]{1,0:T(8,128)(2,1)}, u32[]{:S(2)}, u32[]{:S(2)}) collective-permute-start(bf16[64,5120]{1,0:T(8,128)(2,1)} %get-tuple-element.37.l), channel_id=1, source_target_pairs={{0,66},{1,67},{16,82},{17,83},{32,98},{33,99},{48,114},{49,115},{4... | collective-permute-start | bytes 1966088 | tf_op jit(solution)/shard_map/ppermute | solution.py:33
  27.1 0.0 collective-permute-start.9
  27.1 0.8 copy-done.12
  27.9 0.0 collective-permute-done.4.v_ref
  27.9 3.2 %copy-done.1 = bf16[800,5120]{1,0:T(8,128)(2,1)} copy-done((bf16[800,5120]{1,0:T(8,128)(2,1)}, bf16[800,5120]{1,0:T(8,128)(2,1)S(1)}, u32[]{:S(2)}) %copy-start.1) | copy-done | bytes 8192024
  31.1 0.0 collective-permute-start.5
  31.1 0.1 pad_add_fusion.1.cols
  31.2 3.3 %copy-done = bf16[5120,800]{0,1:T(8,128)(2,1)S(1)} copy-done((bf16[5120,800]{0,1:T(8,128)(2,1)S(1)}, bf16[5120,800]{0,1:T(8,128)(2,1)}, u32[]{:S(2)}) %copy-start) | copy-done | bytes 8192024
  34.5 3.3 %copy-done.2 = bf16[800,5120]{1,0:T(8,128)(2,1)S(1)} copy-done((bf16[800,5120]{1,0:T(8,128)(2,1)S(1)}, bf16[800,5120]{1,0:T(8,128)(2,1)}, u32[]{:S(2)}) %copy-start.2) | copy-done | bytes 8192024
  37.8 2.0 %shard_map.107.w_ref = bf16[1600,5120]{1,0:T(8,128)(2,1)S(1)} custom-call(bf16[800,5120]{1,0:T(8,128)(2,1)S(1)} %bitcast.27, bf16[800,5120]{1,0:T(8,128)(2,1)S(1)} %copy-done.2), custom_call_target="tpu_custom_call" | custom-call | flops 1024 | bytes 33554432 | tf_op jit(solution)/shard_map/pallas_call | solution.py:53
  39.8 4.0 %shard_map.108.f_ref = bf16[1600,2560]{1,0:T(8,128)(2,1)S(1)} custom-call(s32[4]{0:T(128)S(1)} %pad_add_fusion.1.cols, bf16[800,5120]{1,0:T(8,128)(2,1)} %f_ref.5, bf16[800,5120]{1,0:T(8,128)(2,1)} %collective-permute-done.7.o_ref), custom_call_target="tpu_custom_call" | custom-call | flops 1024 | bytes 16777216 | tf_op jit(solution)/shard_map/pallas_call | solution.py:53
  43.9 0.9 collective-permute-done.9.a
  44.8 7.7 %shard_map.109 = (bf16[1600,256]{1,0:T(8,128)(2,1)S(1)}, f32[256,128]{1,0:T(8,128)S(1)}) custom-call(bf16[1600,5120]{1,0:T(8,128)(2,1)S(1)} %shard_map.107.w_ref, bf16[800,128]{1,0:T(8,128)(2,1)S(1)} %copy-done.11, bf16[800,128]{1,0:T(8,128)(2,1)} %collective-permute-done.5.vm_ref, bf16[64,5120]{1,0:T(8,128)(2,1)S(1)} %copy-done.13, ...), custom_call_target="tpu_custom_call" | custom-call | flops 1024 | bytes 1024 | tf_op jit(solution)/shard_map/pallas_call | solution.py:53
  52.5 4.0 %shard_map.111 = (bf16[2,128,640]{2,1,0:T(8,128)(2,1)}, bf16[2,128,640]{2,1,0:T(8,128)(2,1)}, bf16[2,128,640]{2,1,0:T(8,128)(2,1)}, bf16[2,128,640]{2,1,0:T(8,128)(2,1)}) custom-call(s32[4]{0:T(128)S(1)} %pad_add_fusion.1.cols, bf16[1600,256]{1,0:T(8,128)(2,1)S(1)} %get-tuple-element.41.h_ref, f32[256,128]{1,0:T(8,128)S(1)} %get-tuple-element.42.mean_ref, ...), custom_call_target="tpu_custom_call" | custom-call | flops 1024 | bytes 1024 | tf_op jit(solution)/shard_map/pallas_call | solution.py:53
  56.5 2.0 %collective-permute-start.17 = (bf16[64,1280]{1,0:T(8,128)(2,1)S(1)}, bf16[64,1280]{1,0:T(8,128)(2,1)S(1)}, u32[]{:S(2)}, u32[]{:S(2)}) collective-permute-start(bf16[64,1280]{1,0:T(8,128)(2,1)S(1)} %copy-done.18), channel_id=1, source_target_pairs={{0,16},{1,17},{16,0},{17,1},{32,48},{33,49},{48,32},{49,33},{4,20}... | collective-permute-start | bytes 491528 | tf_op jit(solution)/shard_map/ppermute | solution.py:33
  58.4 0.1 collective-permute-start.13
  58.6 3.1 %collective-permute-start.10 = (bf16[2,128,640]{2,1,0:T(8,128)(2,1)}, bf16[2,128,640]{2,1,0:T(8,128)(2,1)}, u32[]{:S(2)}, u32[]{:S(2)}) collective-permute-start(bf16[2,128,640]{2,1,0:T(8,128)(2,1)} %get-tuple-element.44), channel_id=1, source_target_pairs={{0,66},{1,67},{16,82},{17,83},{32,98},{33,99},{48,114},{49,115},{4... | collective-permute-start | bytes 983048 | tf_op jit(solution)/shard_map/ppermute | solution.py:33
  61.7 3.2 %collective-permute-start.12 = (bf16[2,128,640]{2,1,0:T(8,128)(2,1)}, bf16[2,128,640]{2,1,0:T(8,128)(2,1)}, u32[]{:S(2)}, u32[]{:S(2)}) collective-permute-start(bf16[2,128,640]{2,1,0:T(8,128)(2,1)} %get-tuple-element.46), channel_id=1, source_target_pairs={{0,66},{1,67},{16,82},{17,83},{32,98},{33,99},{48,114},{49,115},{4... | collective-permute-start | bytes 983048 | tf_op jit(solution)/shard_map/ppermute | solution.py:33
  64.9 0.8 pad_maximum_fusion.1
  65.7 3.6 %collective-permute-start.18 = (bf16[128,1280]{1,0:T(8,128)(2,1)}, bf16[128,1280]{1,0:T(8,128)(2,1)}, u32[]{:S(2)}, u32[]{:S(2)}) collective-permute-start(bf16[128,1280]{1,0:T(8,128)(2,1)} %pad_maximum_fusion.1), channel_id=1, source_target_pairs={{0,32},{1,33},{16,48},{17,49},{32,0},{33,1},{48,16},{49,17},{4,36}... | collective-permute-start | bytes 983048 | tf_op jit(solution)/shard_map/ppermute | solution.py:33
  69.3 0.1 pad_add_fusion.cols
  69.4 1.1 copy-done.5
  70.5 0.9 copy-done.15
  71.4 6.6 %shard_map.110.own_ref = f32[4,256,640]{2,1,0:T(8,128)S(1)} custom-call(s32[4]{0:T(128)S(1)} %pad_add_fusion.cols, bf16[1600,256]{1,0:T(8,128)(2,1)S(1)} %get-tuple-element.41.h_ref, f32[256,128]{1,0:T(8,128)S(1)} %copy-done.15, f32[32,5120]{1,0:T(8,128)S(1)} %copy-done.5, bf16[800,5120]{1,0:T(8,128)(2,1)} %f_ref.5, ...), custom_call_target="tpu_custom_call" | custom-call | flops 1024 | bytes 16777216 | tf_op jit(solution)/shard_map/pallas_call | solution.py:53
  78.0 0.0 copy-start.21
  78.0 0.0 copy-start.22
  78.1 2.0 %shard_map.112 = (bf16[256,640]{1,0:T(8,128)(2,1)}, bf16[256,640]{1,0:T(8,128)(2,1)}) custom-call(f32[4,256,640]{2,1,0:T(8,128)S(1)} %shard_map.110.own_ref, bf16[2,128,640]{2,1,0:T(8,128)(2,1)} %collective-permute-done.12.up_ref, bf16[2,128,640]{2,1,0:T(8,128)(2,1)} %collective-permute-done.13.low_ref), custom_call_target="tpu_custom_call" | custom-call | flops 1024 | bytes 1024 | tf_op jit(solution)/shard_map/pallas_call | solution.py:53
  80.1 1.9 %shard_map.113 = bf16[256,640]{1,0:T(8,128)(2,1)} custom-call(f32[4,256,640]{2,1,0:T(8,128)S(1)} %shard_map.110.own_ref, bf16[2,128,640]{2,1,0:T(8,128)(2,1)} %collective-permute-done.10.up_ref, bf16[2,128,640]{2,1,0:T(8,128)(2,1)} %collective-permute-done.11.low_ref), custom_call_target="tpu_custom_call" | custom-call | flops 1024 | bytes 1024 | tf_op jit(solution)/shard_map/pallas_call | solution.py:53
  82.0 2.0 %collective-permute-start.15 = (bf16[256,640]{1,0:T(8,128)(2,1)}, bf16[256,640]{1,0:T(8,128)(2,1)S(1)}, u32[]{:S(2)}, u32[]{:S(2)}) collective-permute-start(bf16[256,640]{1,0:T(8,128)(2,1)} %shard_map.113), channel_id=1, source_target_pairs={{0,8},{1,9},{16,24},{17,25},{32,40},{33,41},{48,56},{49,57},{4,12}... | collective-permute-start | bytes 983048 | tf_op jit(solution)/shard_map/ppermute | solution.py:33
  84.0 1.2 collective-permute-start.16
  85.2 0.1 copy.11.index_ref
  85.3 1.1 pad_maximum_fusion.pooled_ref
  86.5 0.0 copy-start.3
  86.5 2.1 %copy-done.3 = bf16[1280,1536]{1,0:T(8,128)(2,1)S(1)} copy-done((bf16[1280,1536]{1,0:T(8,128)(2,1)S(1)}, bf16[1280,1536]{1,0:T(8,128)(2,1)}, u32[]{:S(2)}) %copy-start.3) | copy-done | bytes 3932184
  88.6 1.3 %shard_map.114.text_ref = f32[32,1536]{1,0:T(8,128)S(1)} custom-call(s32[32,1]{1,0:T(8,128)S(1)} %copy.11.index_ref, bf16[256,1280]{1,0:T(8,128)(2,1)S(1)} %pad_maximum_fusion.pooled_ref, bf16[1280,1536]{1,0:T(8,128)(2,1)S(1)} %copy-done.3), custom_call_target="tpu_custom_call" | custom-call | flops 1024 | bytes 1024 | tf_op jit(solution)/shard_map/pallas_call | solution.py:53
  89.9 6.7 %collective-permute-done.14.t1 = bf16[256,640]{1,0:T(8,128)(2,1)S(1)} collective-permute-done((bf16[256,640]{1,0:T(8,128)(2,1)}, bf16[256,640]{1,0:T(8,128)(2,1)S(1)}, u32[]{:S(2)}, u32[]{:S(2)}) %collective-permute-start.14) | collective-permute-done | bytes 327712 | tf_op jit(solution)/shard_map/ppermute | solution.py:33
  96.6 2.6 %collective-permute-done.16.t3 = bf16[256,640]{1,0:T(8,128)(2,1)} collective-permute-done((bf16[256,640]{1,0:T(8,128)(2,1)}, bf16[256,640]{1,0:T(8,128)(2,1)}, u32[]{:S(2)}, u32[]{:S(2)}) %collective-permute-start.16) | collective-permute-done | bytes 327712 | tf_op jit(solution)/shard_map/ppermute | solution.py:33
  99.2 2.1 %shard_map.115 = (bf16[4,32,1664]{2,1,0:T(8,128)(2,1)S(1)}, bf16[64,1664]{1,0:T(8,128)(2,1)S(1)}, bf16[64,1664]{1,0:T(8,128)(2,1)S(1)}) custom-call(s32[1]{0:T(128)} %bitcast.core, f32[4,256,640]{2,1,0:T(8,128)S(1)} %shard_map.110.own_ref, bf16[2,128,640]{2,1,0:T(8,128)(2,1)} %collective-permute-done.10.up_ref, ...), custom_call_target="tpu_custom_call" | custom-call | flops 1024 | bytes 1024 | tf_op jit(solution)/shard_map/pallas_call | solution.py:53
  101.3 2.3 %collective-permute-start.19 = (bf16[64,1664]{1,0:T(8,128)(2,1)S(1)}, bf16[64,1664]{1,0:T(8,128)(2,1)S(1)}, u32[]{:S(2)}, u32[]{:S(2)}) collective-permute-start(bf16[64,1664]{1,0:T(8,128)(2,1)S(1)} %get-tuple-element.54), channel_id=1, source_target_pairs={{0,66},{1,67},{16,82},{17,83},{32,98},{33,99},{48,114},{49,115},{4... | collective-permute-start | bytes 638984 | tf_op jit(solution)/shard_map/ppermute | solution.py:33
  103.6 3.6 %collective-permute-done.19.r_ref = bf16[64,1664]{1,0:T(8,128)(2,1)S(1)} collective-permute-done((bf16[64,1664]{1,0:T(8,128)(2,1)S(1)}, bf16[64,1664]{1,0:T(8,128)(2,1)S(1)}, u32[]{:S(2)}, u32[]{:S(2)}) %collective-permute-start.19) | collective-permute-done | bytes 213024 | tf_op jit(solution)/shard_map/ppermute | solution.py:33
  107.2 3.4 %collective-permute-done.20.l_ref = bf16[64,1664]{1,0:T(8,128)(2,1)S(1)} collective-permute-done((bf16[64,1664]{1,0:T(8,128)(2,1)S(1)}, bf16[64,1664]{1,0:T(8,128)(2,1)S(1)}, u32[]{:S(2)}, u32[]{:S(2)}) %collective-permute-start.20) | collective-permute-done | bytes 213024 | tf_op jit(solution)/shard_map/ppermute | solution.py:33
  110.6 0.1 shard_map.116
  110.7 1.4 %collective-permute-start.21 = (bf16[32,1664]{1,0:T(8,128)(2,1)S(1)}, bf16[32,1664]{1,0:T(8,128)(2,1)S(1)}, u32[]{:S(2)}, u32[]{:S(2)}) collective-permute-start(bf16[32,1664]{1,0:T(8,128)(2,1)S(1)} %get-tuple-element.57), channel_id=1, source_target_pairs={{0,4},{1,5},{16,20},{17,21},{32,36},{33,37},{48,52},{49,53},{4,8},... | collective-permute-start | bytes 319496 | tf_op jit(solution)/shard_map/ppermute | solution.py:33
  112.1 3.2 %collective-permute-start.22 = (bf16[32,1664]{1,0:T(8,128)(2,1)S(1)}, bf16[32,1664]{1,0:T(8,128)(2,1)S(1)}, u32[]{:S(2)}, u32[]{:S(2)}) collective-permute-start(bf16[32,1664]{1,0:T(8,128)(2,1)S(1)} %get-tuple-element.58), channel_id=1, source_target_pairs={{0,8},{1,9},{16,24},{17,25},{32,40},{33,41},{48,56},{49,57},{4,12}... | collective-permute-start | bytes 319496 | tf_op jit(solution)/shard_map/ppermute | solution.py:33
  116.0 1.8 %collective-permute-done.21.s1 = bf16[32,1664]{1,0:T(8,128)(2,1)S(1)} collective-permute-done((bf16[32,1664]{1,0:T(8,128)(2,1)S(1)}, bf16[32,1664]{1,0:T(8,128)(2,1)S(1)}, u32[]{:S(2)}, u32[]{:S(2)}) %collective-permute-start.21) | collective-permute-done | bytes 106528 | tf_op jit(solution)/shard_map/ppermute | solution.py:33
  117.8 1.4 %collective-permute-done.22.s2 = bf16[32,1664]{1,0:T(8,128)(2,1)S(1)} collective-permute-done((bf16[32,1664]{1,0:T(8,128)(2,1)S(1)}, bf16[32,1664]{1,0:T(8,128)(2,1)S(1)}, u32[]{:S(2)}, u32[]{:S(2)}) %collective-permute-start.22) | collective-permute-done | bytes 106528 | tf_op jit(solution)/shard_map/ppermute | solution.py:33
  119.1 0.9 collective-permute-done.23.s3
  120.0 0.9 shard_map.117
  (52 shorter events, 0.1 us)
Async XLA Ops:
  0.6 1.0 copy-start.16
  1.9 50.6 %copy-start.4 = (f32[32,5120]{1,0:T(8,128)}, f32[32,5120]{1,0:T(8,128)S(1)}, u32[]{:S(2)}) copy-start(f32[32,5120]{1,0:T(8,128)S(1)} %get-tuple-element.43.res_ref) | copy-start | bytes 1966084
  2.0 17.2 %collective-permute-start = (bf16[32,5120]{1,0:T(8,128)(2,1)S(1)}, bf16[32,5120]{1,0:T(8,128)(2,1)S(1)}, u32[]{:S(2)}, u32[]{:S(2)}) collective-permute-start(bf16[32,5120]{1,0:T(8,128)(2,1)S(1)} %get-tuple-element.32.n0), channel_id=1, source_target_pairs={{0,12},{1,13},{16,28},{17,29},{32,44},{33,45},{48,60},{49,61},{4,0... | collective-permute-start | bytes 983048 | tf_op jit(solution)/shard_map/ppermute | solution.py:33
  5.1 12.2 %collective-permute-start.1 = (bf16[32,5120]{1,0:T(8,128)(2,1)S(1)}, bf16[32,5120]{1,0:T(8,128)(2,1)S(1)}, u32[]{:S(2)}, u32[]{:S(2)}) collective-permute-start(bf16[32,5120]{1,0:T(8,128)(2,1)S(1)} %get-tuple-element.32.n0), channel_id=1, source_target_pairs={{0,8},{1,9},{16,24},{17,25},{32,40},{33,41},{48,56},{49,57},{4,12}... | collective-permute-start | bytes 983048 | tf_op jit(solution)/shard_map/ppermute | solution.py:33
  5.8 17.1 %collective-permute-start.3 = (bf16[32,5120]{1,0:T(8,128)(2,1)S(1)}, bf16[32,5120]{1,0:T(8,128)(2,1)S(1)}, u32[]{:S(2)}, u32[]{:S(2)}) collective-permute-start(bf16[32,5120]{1,0:T(8,128)(2,1)S(1)} %get-tuple-element.32.n0), channel_id=1, source_target_pairs={{0,4},{1,5},{16,20},{17,21},{32,36},{33,37},{48,52},{49,53},{4,8},... | collective-permute-start | bytes 983048 | tf_op jit(solution)/shard_map/ppermute | solution.py:33
  6.7 8.7 %collective-permute-start.2 = (bf16[32,1280]{1,0:T(8,128)(2,1)}, bf16[32,1280]{1,0:T(8,128)(2,1)S(1)}, u32[]{:S(2)}, u32[]{:S(2)}) collective-permute-start(bf16[32,1280]{1,0:T(8,128)(2,1)} %param.13), channel_id=1, source_target_pairs={{0,64},{1,65},{16,80},{17,81},{32,96},{33,97},{48,112},{49,113},{4... | collective-permute-start | bytes 245768 | tf_op jit(solution)/shard_map/ppermute | solution.py:33
  9.8 18.2 %collective-permute-start.4 = (bf16[800,5120]{1,0:T(8,128)(2,1)}, bf16[800,5120]{1,0:T(8,128)(2,1)S(1)}, u32[]{:S(2)}, u32[]{:S(2)}) collective-permute-start(bf16[800,5120]{1,0:T(8,128)(2,1)} %bitcast.26), channel_id=1, source_target_pairs={{0,1},{1,0},{16,17},{17,16},{32,33},{33,32},{48,49},{49,48},{4,5},... | collective-permute-start | bytes 24576008 | tf_op jit(solution)/shard_map/ppermute | solution.py:33
  10.7 13.1 %copy-start.6 = (bf16[320,1536]{1,0:T(8,128)(2,1)S(1)}, bf16[320,1536]{1,0:T(8,128)(2,1)}, u32[]{:S(2)}) copy-start(bf16[320,1536]{1,0:T(8,128)(2,1)} %w_ref) | copy-start | bytes 2949124
  15.4 24.4 %copy-start.10 = (bf16[800,128]{1,0:T(8,128)(2,1)}, bf16[800,128]{1,0:T(8,128)(2,1)S(1)}, u32[]{:S(2)}) copy-start(bf16[800,128]{1,0:T(8,128)(2,1)S(1)} %shard_map.105.wm_ref) | copy-start | bytes 614404
  15.4 12.5 %copy-start.17 = (bf16[64,1280]{1,0:T(8,128)(2,1)}, bf16[64,1280]{1,0:T(8,128)(2,1)S(1)}, u32[]{:S(2)}) copy-start(bf16[64,1280]{1,0:T(8,128)(2,1)S(1)} %constant_dynamic-update-slice_fusion) | copy-start | bytes 491524
  23.8 16.0 %collective-permute-start.7 = (bf16[800,5120]{1,0:T(8,128)(2,1)}, bf16[800,5120]{1,0:T(8,128)(2,1)}, u32[]{:S(2)}, u32[]{:S(2)}) collective-permute-start(bf16[800,5120]{1,0:T(8,128)(2,1)} %f_ref.5), channel_id=1, source_target_pairs={{0,1},{1,0},{16,17},{17,16},{32,33},{33,32},{48,49},{49,48},{4,5},... | collective-permute-start | bytes 24576008 | tf_op jit(solution)/shard_map/ppermute | solution.py:33
  23.8 20.0 %collective-permute-start.8 = (bf16[320,1536]{1,0:T(8,128)(2,1)S(1)}, bf16[320,1536]{1,0:T(8,128)(2,1)S(1)}, u32[]{:S(2)}, u32[]{:S(2)}) collective-permute-start(bf16[320,1536]{1,0:T(8,128)(2,1)S(1)} %copy-done.6), channel_id=1, source_target_pairs={{0,1},{1,0},{16,17},{17,16},{32,33},{33,32},{48,49},{49,48},{4,5},... | collective-permute-start | bytes 2949128 | tf_op jit(solution)/shard_map/ppermute | solution.py:33
  24.3 19.5 %collective-permute-start.6 = (bf16[64,5120]{1,0:T(8,128)(2,1)}, bf16[64,5120]{1,0:T(8,128)(2,1)}, u32[]{:S(2)}, u32[]{:S(2)}) collective-permute-start(bf16[64,5120]{1,0:T(8,128)(2,1)} %get-tuple-element.37.l), channel_id=1, source_target_pairs={{0,66},{1,67},{16,82},{17,83},{32,98},{33,99},{48,114},{49,115},{4... | collective-permute-start | bytes 1966088 | tf_op jit(solution)/shard_map/ppermute | solution.py:33
  27.1 17.7 %collective-permute-start.9 = (bf16[64,5120]{1,0:T(8,128)(2,1)S(1)}, bf16[64,5120]{1,0:T(8,128)(2,1)}, u32[]{:S(2)}, u32[]{:S(2)}) collective-permute-start(bf16[64,5120]{1,0:T(8,128)(2,1)S(1)} %get-tuple-element.34.r), channel_id=1, source_target_pairs={{0,2},{1,3},{16,18},{17,19},{32,34},{33,35},{48,50},{49,51},{4,6},... | collective-permute-start | bytes 1966088 | tf_op jit(solution)/shard_map/ppermute | solution.py:33
  27.1 0.8 copy-start.12
  27.9 3.2 %copy-start.1 = (bf16[800,5120]{1,0:T(8,128)(2,1)}, bf16[800,5120]{1,0:T(8,128)(2,1)S(1)}, u32[]{:S(2)}) copy-start(bf16[800,5120]{1,0:T(8,128)(2,1)S(1)} %collective-permute-done.4.v_ref) | copy-start | bytes 24576004
  31.1 12.8 %collective-permute-start.5 = (bf16[800,128]{1,0:T(8,128)(2,1)S(1)}, bf16[800,128]{1,0:T(8,128)(2,1)}, u32[]{:S(2)}, u32[]{:S(2)}) collective-permute-start(bf16[800,128]{1,0:T(8,128)(2,1)S(1)} %shard_map.105.wm_ref), channel_id=1, source_target_pairs={{0,1},{1,0},{16,17},{17,16},{32,33},{33,32},{48,49},{49,48},{4,5},... | collective-permute-start | bytes 614408 | tf_op jit(solution)/shard_map/ppermute | solution.py:33
  31.2 3.3 %copy-start = (bf16[5120,800]{0,1:T(8,128)(2,1)S(1)}, bf16[5120,800]{0,1:T(8,128)(2,1)}, u32[]{:S(2)}) copy-start(bf16[5120,800]{0,1:T(8,128)(2,1)} %param.10) | copy-start | bytes 24576004
  34.5 3.3 %copy-start.2 = (bf16[800,5120]{1,0:T(8,128)(2,1)S(1)}, bf16[800,5120]{1,0:T(8,128)(2,1)}, u32[]{:S(2)}) copy-start(bf16[800,5120]{1,0:T(8,128)(2,1)} %copy-done.1) | copy-start | bytes 24576004
  39.8 5.0 %copy-start.13 = (bf16[64,5120]{1,0:T(8,128)(2,1)S(1)}, bf16[64,5120]{1,0:T(8,128)(2,1)}, u32[]{:S(2)}) copy-start(bf16[64,5120]{1,0:T(8,128)(2,1)} %copy-done.12) | copy-start | bytes 1966084
  39.8 5.0 %copy-start.11 = (bf16[800,128]{1,0:T(8,128)(2,1)S(1)}, bf16[800,128]{1,0:T(8,128)(2,1)}, u32[]{:S(2)}) copy-start(bf16[800,128]{1,0:T(8,128)(2,1)} %copy-done.10) | copy-start | bytes 614404
  43.9 8.6 %copy-start.8 = (bf16[320,1536]{1,0:T(8,128)(2,1)}, bf16[320,1536]{1,0:T(8,128)(2,1)S(1)}, u32[]{:S(2)}) copy-start(bf16[320,1536]{1,0:T(8,128)(2,1)S(1)} %collective-permute-done.8.o_ref) | copy-start | bytes 2949124
  52.5 4.0 %copy-start.14 = (f32[256,128]{1,0:T(8,128)}, f32[256,128]{1,0:T(8,128)S(1)}, u32[]{:S(2)}) copy-start(f32[256,128]{1,0:T(8,128)S(1)} %get-tuple-element.42.mean_ref) | copy-start | bytes 393220
  52.5 4.0 %copy-start.18 = (bf16[64,1280]{1,0:T(8,128)(2,1)S(1)}, bf16[64,1280]{1,0:T(8,128)(2,1)}, u32[]{:S(2)}) copy-start(bf16[64,1280]{1,0:T(8,128)(2,1)} %copy-done.17) | copy-start | bytes 491524
  56.5 8.4 %collective-permute-start.17 = (bf16[64,1280]{1,0:T(8,128)(2,1)S(1)}, bf16[64,1280]{1,0:T(8,128)(2,1)S(1)}, u32[]{:S(2)}, u32[]{:S(2)}) collective-permute-start(bf16[64,1280]{1,0:T(8,128)(2,1)S(1)} %copy-done.18), channel_id=1, source_target_pairs={{0,16},{1,17},{16,0},{17,1},{32,48},{33,49},{48,32},{49,33},{4,20}... | collective-permute-start | bytes 491528 | tf_op jit(solution)/shard_map/ppermute | solution.py:33
  58.4 19.6 %collective-permute-start.13 = (bf16[2,128,640]{2,1,0:T(8,128)(2,1)}, bf16[2,128,640]{2,1,0:T(8,128)(2,1)}, u32[]{:S(2)}, u32[]{:S(2)}) collective-permute-start(bf16[2,128,640]{2,1,0:T(8,128)(2,1)} %get-tuple-element.47), channel_id=1, source_target_pairs={{0,2},{1,3},{16,18},{17,19},{32,34},{33,35},{48,50},{49,51},{4,6},... | collective-permute-start | bytes 983048 | tf_op jit(solution)/shard_map/ppermute | solution.py:33
  58.6 21.5 %collective-permute-start.10 = (bf16[2,128,640]{2,1,0:T(8,128)(2,1)}, bf16[2,128,640]{2,1,0:T(8,128)(2,1)}, u32[]{:S(2)}, u32[]{:S(2)}) collective-permute-start(bf16[2,128,640]{2,1,0:T(8,128)(2,1)} %get-tuple-element.44), channel_id=1, source_target_pairs={{0,66},{1,67},{16,82},{17,83},{32,98},{33,99},{48,114},{49,115},{4... | collective-permute-start | bytes 983048 | tf_op jit(solution)/shard_map/ppermute | solution.py:33
  61.7 18.4 %collective-permute-start.11 = (bf16[2,128,640]{2,1,0:T(8,128)(2,1)}, bf16[2,128,640]{2,1,0:T(8,128)(2,1)}, u32[]{:S(2)}, u32[]{:S(2)}) collective-permute-start(bf16[2,128,640]{2,1,0:T(8,128)(2,1)} %get-tuple-element.45), channel_id=1, source_target_pairs={{0,2},{1,3},{16,18},{17,19},{32,34},{33,35},{48,50},{49,51},{4,6},... | collective-permute-start | bytes 983048 | tf_op jit(solution)/shard_map/ppermute | solution.py:33
  61.7 16.4 %collective-permute-start.12 = (bf16[2,128,640]{2,1,0:T(8,128)(2,1)}, bf16[2,128,640]{2,1,0:T(8,128)(2,1)}, u32[]{:S(2)}, u32[]{:S(2)}) collective-permute-start(bf16[2,128,640]{2,1,0:T(8,128)(2,1)} %get-tuple-element.46), channel_id=1, source_target_pairs={{0,66},{1,67},{16,82},{17,83},{32,98},{33,99},{48,114},{49,115},{4... | collective-permute-start | bytes 983048 | tf_op jit(solution)/shard_map/ppermute | solution.py:33
  64.9 4.5 %copy-start.20 = (bf16[64,1280]{1,0:T(8,128)(2,1)}, bf16[64,1280]{1,0:T(8,128)(2,1)S(1)}, u32[]{:S(2)}) copy-start(bf16[64,1280]{1,0:T(8,128)(2,1)S(1)} %collective-permute-done.17) | copy-start | bytes 491524
  65.7 19.6 %collective-permute-start.18 = (bf16[128,1280]{1,0:T(8,128)(2,1)}, bf16[128,1280]{1,0:T(8,128)(2,1)}, u32[]{:S(2)}, u32[]{:S(2)}) collective-permute-start(bf16[128,1280]{1,0:T(8,128)(2,1)} %pad_maximum_fusion.1), channel_id=1, source_target_pairs={{0,32},{1,33},{16,48},{17,49},{32,0},{33,1},{48,16},{49,17},{4,36}... | collective-permute-start | bytes 983048 | tf_op jit(solution)/shard_map/ppermute | solution.py:33
  69.4 1.1 copy-start.5
  70.5 0.9 copy-start.15
  78.0 7.2 %copy-start.21 = (s32[32]{0:T(128)S(1)}, s32[32]{0:T(128)}, u32[]{:S(2)}) copy-start(s32[32]{0:T(128)} %param.16) | copy-start | bytes 388
  78.0 7.2 %copy-start.22 = (s32[32,1]{0,1:T(1,128)S(1)}, s32[32,1]{0,1:T(1,128)}, u32[]{:S(2)}) copy-start(s32[32,1]{0,1:T(1,128)} %param.15) | copy-start | bytes 388
  78.0 7.3 %copy-start.19 = (bf16[64,1280]{1,0:T(8,128)(2,1)S(1)}, bf16[64,1280]{1,0:T(8,128)(2,1)}, u32[]{:S(2)}) copy-start(bf16[64,1280]{1,0:T(8,128)(2,1)} %copy-done.17) | copy-start | bytes 491524
  80.1 16.5 %collective-permute-start.14 = (bf16[256,640]{1,0:T(8,128)(2,1)}, bf16[256,640]{1,0:T(8,128)(2,1)S(1)}, u32[]{:S(2)}, u32[]{:S(2)}) collective-permute-start(bf16[256,640]{1,0:T(8,128)(2,1)} %get-tuple-element.48), channel_id=1, source_target_pairs={{0,4},{1,5},{16,20},{17,21},{32,36},{33,37},{48,52},{49,53},{4,8},... | collective-permute-start | bytes 983048 | tf_op jit(solution)/shard_map/ppermute | solution.py:33
  82.0 14.6 %collective-permute-start.15 = (bf16[256,640]{1,0:T(8,128)(2,1)}, bf16[256,640]{1,0:T(8,128)(2,1)S(1)}, u32[]{:S(2)}, u32[]{:S(2)}) collective-permute-start(bf16[256,640]{1,0:T(8,128)(2,1)} %shard_map.113), channel_id=1, source_target_pairs={{0,8},{1,9},{16,24},{17,25},{32,40},{33,41},{48,56},{49,57},{4,12}... | collective-permute-start | bytes 983048 | tf_op jit(solution)/shard_map/ppermute | solution.py:33
  84.0 15.2 %collective-permute-start.16 = (bf16[256,640]{1,0:T(8,128)(2,1)}, bf16[256,640]{1,0:T(8,128)(2,1)}, u32[]{:S(2)}, u32[]{:S(2)}) collective-permute-start(bf16[256,640]{1,0:T(8,128)(2,1)} %get-tuple-element.49), channel_id=1, source_target_pairs={{0,12},{1,13},{16,28},{17,29},{32,44},{33,45},{48,60},{49,61},{4,0... | collective-permute-start | bytes 983048 | tf_op jit(solution)/shard_map/ppermute | solution.py:33
  85.3 13.9 %copy-start.7 = (bf16[320,1536]{1,0:T(8,128)(2,1)S(1)}, bf16[320,1536]{1,0:T(8,128)(2,1)}, u32[]{:S(2)}) copy-start(bf16[320,1536]{1,0:T(8,128)(2,1)} %w_ref) | copy-start | bytes 2949124
  86.5 2.1 %copy-start.3 = (bf16[1280,1536]{1,0:T(8,128)(2,1)S(1)}, bf16[1280,1536]{1,0:T(8,128)(2,1)}, u32[]{:S(2)}) copy-start(bf16[1280,1536]{1,0:T(8,128)(2,1)} %proj_ref.1) | copy-start | bytes 11796484
  88.6 10.6 %copy-start.9 = (bf16[320,1536]{1,0:T(8,128)(2,1)S(1)}, bf16[320,1536]{1,0:T(8,128)(2,1)}, u32[]{:S(2)}) copy-start(bf16[320,1536]{1,0:T(8,128)(2,1)} %copy-done.8) | copy-start | bytes 2949124
  101.3 5.9 %collective-permute-start.19 = (bf16[64,1664]{1,0:T(8,128)(2,1)S(1)}, bf16[64,1664]{1,0:T(8,128)(2,1)S(1)}, u32[]{:S(2)}, u32[]{:S(2)}) collective-permute-start(bf16[64,1664]{1,0:T(8,128)(2,1)S(1)} %get-tuple-element.54), channel_id=1, source_target_pairs={{0,66},{1,67},{16,82},{17,83},{32,98},{33,99},{48,114},{49,115},{4... | collective-permute-start | bytes 638984 | tf_op jit(solution)/shard_map/ppermute | solution.py:33
  103.6 7.1 %collective-permute-start.20 = (bf16[64,1664]{1,0:T(8,128)(2,1)S(1)}, bf16[64,1664]{1,0:T(8,128)(2,1)S(1)}, u32[]{:S(2)}, u32[]{:S(2)}) collective-permute-start(bf16[64,1664]{1,0:T(8,128)(2,1)S(1)} %get-tuple-element.55), channel_id=1, source_target_pairs={{0,2},{1,3},{16,18},{17,19},{32,34},{33,35},{48,50},{49,51},{4,6},... | collective-permute-start | bytes 638984 | tf_op jit(solution)/shard_map/ppermute | solution.py:33
  110.7 7.0 %collective-permute-start.21 = (bf16[32,1664]{1,0:T(8,128)(2,1)S(1)}, bf16[32,1664]{1,0:T(8,128)(2,1)S(1)}, u32[]{:S(2)}, u32[]{:S(2)}) collective-permute-start(bf16[32,1664]{1,0:T(8,128)(2,1)S(1)} %get-tuple-element.57), channel_id=1, source_target_pairs={{0,4},{1,5},{16,20},{17,21},{32,36},{33,37},{48,52},{49,53},{4,8},... | collective-permute-start | bytes 319496 | tf_op jit(solution)/shard_map/ppermute | solution.py:33
  112.1 7.0 %collective-permute-start.22 = (bf16[32,1664]{1,0:T(8,128)(2,1)S(1)}, bf16[32,1664]{1,0:T(8,128)(2,1)S(1)}, u32[]{:S(2)}, u32[]{:S(2)}) collective-permute-start(bf16[32,1664]{1,0:T(8,128)(2,1)S(1)} %get-tuple-element.58), channel_id=1, source_target_pairs={{0,8},{1,9},{16,24},{17,25},{32,40},{33,41},{48,56},{49,57},{4,12}... | collective-permute-start | bytes 319496 | tf_op jit(solution)/shard_map/ppermute | solution.py:33
  115.3 4.7 %collective-permute-start.23 = (bf16[32,1664]{1,0:T(8,128)(2,1)S(1)}, bf16[32,1664]{1,0:T(8,128)(2,1)S(1)}, u32[]{:S(2)}, u32[]{:S(2)}) collective-permute-start(bf16[32,1664]{1,0:T(8,128)(2,1)S(1)} %get-tuple-element.59), channel_id=1, source_target_pairs={{0,12},{1,13},{16,28},{17,29},{32,44},{33,45},{48,60},{49,61},{4,0... | collective-permute-start | bytes 319496 | tf_op jit(solution)/shard_map/ppermute | solution.py:33

commit v3 on v2

--- a/solution.py
+++ b/solution.py
@@ -187,7 +187,7 @@
 
 def away_call(cols, h, h_mean, centred, f):
     outs = (struct((2, 128, BLK), bf16),) * 4
-    return call(away_kernel, (cols,), (h, h_mean, centred, f), outs, limit=20)
+    return call(away_kernel, (cols,), (h, h_mean, centred, f), outs, limit=8)
 
 
 def own_kernel(cols, h_ref, mean_ref, res_ref, f_ref, o_ref, own_ref, buf, sems):
@@ -215,7 +215,7 @@
         (struct((4, 256, BLK), f32),),
         scratch=[pltpu.VMEM((1600, 4 * BLK), bf16), pltpu.SemaphoreType.DMA((8,))],
         remote=2,
-        limit=29,
+        limit=14,
         size=16 * 1024 * 1024,
     )[0]
 
@@ -337,8 +337,10 @@
     r, l = halves_call(normed, n1, after(n2, w_mean, pooled), n3)
     a, b = shift(r, dx=1), shift(l, dx=-1)
     fc2_other = shift(after(fc2_weight, r), flip=True)
-    v_mean = shift(after(w_mean, r), flip=True)
-    proj_other = shift(after(proj_weight, r), flip=True)
+    v_mean = shift(w_mean, flip=True)
+    pooled = after(pooled, r)
+    pooled = jnp.concatenate([pooled, shift(pooled, mz=1)])
+    pooled_far = shift(pooled, mz=2)
     fc1_both = stage_call(after(fc1_rows, r), fc1_other)
 
     def blocks(parity, *ks):
@@ -346,13 +348,12 @@
 
     cols = blocks(1 - x_lo, 1, 3, 2, 0)
     fc2_both = columns_call(cols, fc2_weight, fc2_other)
-    h, h_mean = fc1_call((r, after(b, fc2_both, proj_other), a, l), fc1_both, w_mean, v_mean)
-    to_r, to_l, to_r2, to_l2 = away_call(cols, h, h_mean, centred, fc2_both)
+    h, h_mean = fc1_call((r, after(b, fc2_both), a, l), fc1_both, w_mean, v_mean)
+    pooled = jnp.concatenate([pooled, after(pooled_far, h)])
+    to_r, to_l, to_r2, to_l2 = away_call(cols, h, h_mean, after(centred, pooled), fc2_both)
     got_r, got_l = shift(to_l, dx=-1), shift(to_r, dx=1)
     got_r2, got_l2 = shift(to_l2, dx=-1), shift(to_r2, dx=1)
-    pooled = after(pooled, to_r)
-    pooled = jnp.concatenate([pooled, shift(pooled, mz=1)])
-    pooled = jnp.concatenate([pooled, shift(pooled, mz=2)])
+    proj_other = shift(after(proj_weight, to_r), flip=True)
     own = own_call(blocks(x_lo, 1, 3, 2, 0), h, h_mean, centred, fc2_weight, fc2_other)
     s1, s3 = add_call(0, 2, own, got_r, got_l)
     t1, t3 = shift(s1, dy=1), shift(s3, dy=-1)

time: 121 us -> 116 us (0.959)
  local copies, waits for them, and re-layouts: 16.8 us -> 10.6 us
  waiting for transfers between devices: 28.7 us -> 32.5 us
  other arithmetic: 2.1 us -> 0.19 us
    unnamed x47 -> x25, local copies, waits for them, and re-layouts: 16.7 us -> 10.4 us
    ppermute x24, waiting for transfers between devices: 28.7 us -> 32.5 us  [shift(): return lax.ppermute(value, AXES, moves(**step))]
  transfers between devices with their start and end apart: 24 -> 24, of which waited for: 11 -> 14; matrix products, arithmetic and copies ran while one was open for 3% -> 1% of each run, Pallas kernels for 19% -> 27%
where the time goes in v3:
time: 116 us
  Pallas kernels  38.9 us (34%)
  waiting for transfers between devices  32.5 us (28%)
  starting transfers between devices  32 us (28%)
  local copies, waits for them, and re-layouts  10.6 us (9%)
  between operations  1.51 us (1%)
    pallas_call x14, Pallas kernels, call(): pl.pallas_call(body, in_specs=[SM] * len(scalars) + [VM] * inside + [HB]...  38.9 us
    ppermute x24, waiting for transfers between devices, shift(): return lax.ppermute(value, AXES, moves(**step))  32.5 us
    ppermute x24, starting transfers between devices, shift(): return lax.ppermute(value, AXES, moves(**step))  32 us
    unnamed x25, local copies, waits for them, and re-layouts  10.4 us
  transfers between devices with their start and end apart: 24, of which 14 were waited for; matrix products, arithmetic and copies ran while one was open for 1% of the time, Pallas kernels for 27%

profile of v3, /device:TPU:0, one launch (start us, length us, event | category | flops | bytes accessed | tf_op | source)
XLA Modules:
  0.0 115.7 jit_solution(1469679629966777867)
XLA Ops:
  0.6 1.0 copy-done.8
  1.6 0.3 shard_map.104
  2.0 3.2 %collective-permute-start = (bf16[32,5120]{1,0:T(8,128)(2,1)S(1)}, bf16[32,5120]{1,0:T(8,128)(2,1)S(1)}, u32[]{:S(2)}, u32[]{:S(2)}) collective-permute-start(bf16[32,5120]{1,0:T(8,128)(2,1)S(1)} %get-tuple-element.33.n0), channel_id=1, source_target_pairs={{0,12},{1,13},{16,28},{17,29},{32,44},{33,45},{48,60},{49,61},{4,0... | collective-permute-start | bytes 983048 | tf_op jit(solution)/shard_map/ppermute | solution.py:33
  5.1 0.6 collective-permute-start.1
  5.8 1.0 collective-permute-start.3
  6.7 3.0 %collective-permute-start.2 = (bf16[32,1280]{1,0:T(8,128)(2,1)}, bf16[32,1280]{1,0:T(8,128)(2,1)S(1)}, u32[]{:S(2)}, u32[]{:S(2)}) collective-permute-start(bf16[32,1280]{1,0:T(8,128)(2,1)} %param.13), channel_id=1, source_target_pairs={{0,64},{1,65},{16,80},{17,81},{32,96},{33,97},{48,112},{49,113},{4... | collective-permute-start | bytes 245768 | tf_op jit(solution)/shard_map/ppermute | solution.py:33
  9.8 0.9 constant_dynamic-update-slice_fusion.1
  10.7 4.7 %shard_map.105.wm_ref = bf16[800,128]{1,0:T(8,128)(2,1)S(1)} custom-call(bf16[800,5120]{1,0:T(8,128)(2,1)} %f_ref.5), custom_call_target="tpu_custom_call" | custom-call | flops 1024 | bytes 16777216 | tf_op jit(solution)/shard_map/pallas_call | solution.py:53
  15.3 0.0 collective-permute-done.2
  15.3 2.0 %collective-permute-done.1.n2 = bf16[32,5120]{1,0:T(8,128)(2,1)S(1)} collective-permute-done((bf16[32,5120]{1,0:T(8,128)(2,1)S(1)}, bf16[32,5120]{1,0:T(8,128)(2,1)S(1)}, u32[]{:S(2)}, u32[]{:S(2)}) %collective-permute-start.1) | collective-permute-done | bytes 327712 | tf_op jit(solution)/shard_map/ppermute | solution.py:33
  17.3 1.8 %collective-permute-done.n1 = bf16[32,5120]{1,0:T(8,128)(2,1)S(1)} collective-permute-done((bf16[32,5120]{1,0:T(8,128)(2,1)S(1)}, bf16[32,5120]{1,0:T(8,128)(2,1)S(1)}, u32[]{:S(2)}, u32[]{:S(2)}) %collective-permute-start) | collective-permute-done | bytes 327712 | tf_op jit(solution)/shard_map/ppermute | solution.py:33
  19.1 3.7 %collective-permute-done.3.n3 = bf16[32,5120]{1,0:T(8,128)(2,1)S(1)} collective-permute-done((bf16[32,5120]{1,0:T(8,128)(2,1)S(1)}, bf16[32,5120]{1,0:T(8,128)(2,1)S(1)}, u32[]{:S(2)}, u32[]{:S(2)}) %collective-permute-start.3) | collective-permute-done | bytes 327712 | tf_op jit(solution)/shard_map/ppermute | solution.py:33
  22.8 0.1 shard_map.106
  22.9 0.1 collective-permute-start.7
  23.0 2.0 %collective-permute-start.9 = (bf16[64,1280]{1,0:T(8,128)(2,1)S(1)}, bf16[64,1280]{1,0:T(8,128)(2,1)S(1)}, u32[]{:S(2)}, u32[]{:S(2)}) collective-permute-start(bf16[64,1280]{1,0:T(8,128)(2,1)S(1)} %constant_dynamic-update-slice_fusion), channel_id=1, source_target_pairs={{0,16},{1,17},{16,0},{17,1},{32,48},{33,49},{48,32},{49,33},{4,20}... | collective-permute-start | bytes 491528 | tf_op jit(solution)/shard_map/ppermute | solution.py:33
  25.0 0.1 pad_add_fusion.1.cols
  25.1 1.5 %collective-permute-start.8 = (bf16[64,5120]{1,0:T(8,128)(2,1)S(1)}, bf16[64,5120]{1,0:T(8,128)(2,1)S(1)}, u32[]{:S(2)}, u32[]{:S(2)}) collective-permute-start(bf16[64,5120]{1,0:T(8,128)(2,1)S(1)} %get-tuple-element.35.r), channel_id=1, source_target_pairs={{0,2},{1,3},{16,18},{17,19},{32,34},{33,35},{48,50},{49,51},{4,6},... | collective-permute-start | bytes 1966088 | tf_op jit(solution)/shard_map/ppermute | solution.py:33
  26.6 1.7 %collective-permute-start.6 = (bf16[64,5120]{1,0:T(8,128)(2,1)S(1)}, bf16[64,5120]{1,0:T(8,128)(2,1)S(1)}, u32[]{:S(2)}, u32[]{:S(2)}) collective-permute-start(bf16[64,5120]{1,0:T(8,128)(2,1)S(1)} %get-tuple-element.37.l), channel_id=1, source_target_pairs={{0,66},{1,67},{16,82},{17,83},{32,98},{33,99},{48,114},{49,115},{4... | collective-permute-start | bytes 1966088 | tf_op jit(solution)/shard_map/ppermute | solution.py:33
  28.3 1.5 %collective-permute-done.9 = bf16[64,1280]{1,0:T(8,128)(2,1)S(1)} collective-permute-done((bf16[64,1280]{1,0:T(8,128)(2,1)S(1)}, bf16[64,1280]{1,0:T(8,128)(2,1)S(1)}, u32[]{:S(2)}, u32[]{:S(2)}) %collective-permute-start.9) | collective-permute-done | bytes 163872 | tf_op jit(solution)/shard_map/ppermute | solution.py:33
  29.8 3.8 %collective-permute-start.10 = (bf16[128,1280]{1,0:T(8,128)(2,1)S(1)}, bf16[128,1280]{1,0:T(8,128)(2,1)S(1)}, u32[]{:S(2)}, u32[]{:S(2)}) collective-permute-start(bf16[128,1280]{1,0:T(8,128)(2,1)S(1)} %pad_maximum_fusion), channel_id=1, source_target_pairs={{0,32},{1,33},{16,48},{17,49},{32,0},{33,1},{48,16},{49,17},{4,36}... | collective-permute-start | bytes 983048 | tf_op jit(solution)/shard_map/ppermute | solution.py:33
  33.6 0.1 collective-permute-start.5
  33.7 0.0 copy-start
  33.8 3.3 %copy-done = bf16[5120,800]{0,1:T(8,128)(2,1)S(1)} copy-done((bf16[5120,800]{0,1:T(8,128)(2,1)S(1)}, bf16[5120,800]{0,1:T(8,128)(2,1)}, u32[]{:S(2)}) %copy-start) | copy-done | bytes 8192024
  37.1 4.4 %shard_map.107.w_ref = bf16[1600,5120]{1,0:T(8,128)(2,1)S(1)} custom-call(bf16[800,5120]{1,0:T(8,128)(2,1)S(1)} %bitcast.27, bf16[800,5120]{1,0:T(8,128)(2,1)} %collective-permute-done.4.v_ref), custom_call_target="tpu_custom_call" | custom-call | flops 1024 | bytes 33554432 | tf_op jit(solution)/shard_map/pallas_call | solution.py:53
  41.5 0.0 collective-permute-done.7.o_ref
  41.5 4.0 %shard_map.108.f_ref = bf16[1600,2560]{1,0:T(8,128)(2,1)S(1)} custom-call(s32[4]{0:T(128)S(1)} %pad_add_fusion.1.cols, bf16[800,5120]{1,0:T(8,128)(2,1)} %f_ref.5, bf16[800,5120]{1,0:T(8,128)(2,1)} %collective-permute-done.7.o_ref), custom_call_target="tpu_custom_call" | custom-call | flops 1024 | bytes 16777216 | tf_op jit(solution)/shard_map/pallas_call | solution.py:53
  45.5 0.0 collective-permute-done.6.b
  45.5 0.0 collective-permute-done.8.a
  45.5 5.9 %shard_map.109 = (bf16[1600,256]{1,0:T(8,128)(2,1)S(1)}, f32[256,128]{1,0:T(8,128)S(1)}) custom-call(bf16[1600,5120]{1,0:T(8,128)(2,1)S(1)} %shard_map.107.w_ref, bf16[800,128]{1,0:T(8,128)(2,1)S(1)} %shard_map.105.wm_ref, bf16[800,128]{1,0:T(8,128)(2,1)S(1)} %collective-permute-done.5.vm_ref, bf16[64,5120]{1,0:T(8,128)(2,1)S(1)} %get-tuple-element.35.r, ...), custom_call_target="tpu_custom_call" | custom-call | flops 1024 | bytes 1024 | tf_op jit(solution)/shard_map/pallas_call | solution.py:53
  51.6 4.0 %shard_map.111 = (bf16[2,128,640]{2,1,0:T(8,128)(2,1)}, bf16[2,128,640]{2,1,0:T(8,128)(2,1)}, bf16[2,128,640]{2,1,0:T(8,128)(2,1)}, bf16[2,128,640]{2,1,0:T(8,128)(2,1)}) custom-call(s32[4]{0:T(128)S(1)} %pad_add_fusion.1.cols, bf16[1600,256]{1,0:T(8,128)(2,1)S(1)} %get-tuple-element.40.h_ref, f32[256,128]{1,0:T(8,128)S(1)} %get-tuple-element.41.mean_ref, ...), custom_call_target="tpu_custom_call" | custom-call | flops 1024 | bytes 1024 | tf_op jit(solution)/shard_map/pallas_call | solution.py:53
  55.5 0.5 collective-permute-start.18
  56.1 2.7 %collective-permute-start.13 = (bf16[2,128,640]{2,1,0:T(8,128)(2,1)}, bf16[2,128,640]{2,1,0:T(8,128)(2,1)}, u32[]{:S(2)}, u32[]{:S(2)}) collective-permute-start(bf16[2,128,640]{2,1,0:T(8,128)(2,1)} %get-tuple-element.48), channel_id=1, source_target_pairs={{0,66},{1,67},{16,82},{17,83},{32,98},{33,99},{48,114},{49,115},{4... | collective-permute-start | bytes 983048 | tf_op jit(solution)/shard_map/ppermute | solution.py:33
  58.8 0.0 collective-permute-start.14
  58.8 3.2 %collective-permute-start.11 = (bf16[2,128,640]{2,1,0:T(8,128)(2,1)}, bf16[2,128,640]{2,1,0:T(8,128)(2,1)}, u32[]{:S(2)}, u32[]{:S(2)}) collective-permute-start(bf16[2,128,640]{2,1,0:T(8,128)(2,1)} %get-tuple-element.46), channel_id=1, source_target_pairs={{0,66},{1,67},{16,82},{17,83},{32,98},{33,99},{48,114},{49,115},{4... | collective-permute-start | bytes 983048 | tf_op jit(solution)/shard_map/ppermute | solution.py:33
  62.0 0.0 collective-permute-start.12
  62.0 0.1 pad_add_fusion.cols
  62.1 1.1 copy-done.3
  63.2 0.9 copy-done.7
  64.1 6.6 %shard_map.110.own_ref = f32[4,256,640]{2,1,0:T(8,128)S(1)} custom-call(s32[4]{0:T(128)S(1)} %pad_add_fusion.cols, bf16[1600,256]{1,0:T(8,128)(2,1)S(1)} %get-tuple-element.40.h_ref, f32[256,128]{1,0:T(8,128)S(1)} %copy-done.7, f32[32,5120]{1,0:T(8,128)S(1)} %copy-done.3, bf16[800,5120]{1,0:T(8,128)(2,1)} %f_ref.5, ...), custom_call_target="tpu_custom_call" | custom-call | flops 1024 | bytes 16777216 | tf_op jit(solution)/shard_map/pallas_call | solution.py:53
  70.7 0.2 collective-permute-done.14.low_ref
  70.9 2.0 %shard_map.112 = (bf16[256,640]{1,0:T(8,128)(2,1)}, bf16[256,640]{1,0:T(8,128)(2,1)}) custom-call(f32[4,256,640]{2,1,0:T(8,128)S(1)} %shard_map.110.own_ref, bf16[2,128,640]{2,1,0:T(8,128)(2,1)} %collective-permute-done.13.up_ref, bf16[2,128,640]{2,1,0:T(8,128)(2,1)} %collective-permute-done.14.low_ref), custom_call_target="tpu_custom_call" | custom-call | flops 1024 | bytes 1024 | tf_op jit(solution)/shard_map/pallas_call | solution.py:53
  72.9 0.5 collective-permute-done.11.up_ref
  73.4 3.4 %collective-permute-done.12.low_ref = bf16[2,128,640]{2,1,0:T(8,128)(2,1)} collective-permute-done((bf16[2,128,640]{2,1,0:T(8,128)(2,1)}, bf16[2,128,640]{2,1,0:T(8,128)(2,1)}, u32[]{:S(2)}, u32[]{:S(2)}) %collective-permute-start.12) | collective-permute-done | bytes 327712 | tf_op jit(solution)/shard_map/ppermute | solution.py:33
  76.8 1.9 %shard_map.113 = bf16[256,640]{1,0:T(8,128)(2,1)} custom-call(f32[4,256,640]{2,1,0:T(8,128)S(1)} %shard_map.110.own_ref, bf16[2,128,640]{2,1,0:T(8,128)(2,1)} %collective-permute-done.11.up_ref, bf16[2,128,640]{2,1,0:T(8,128)(2,1)} %collective-permute-done.12.low_ref), custom_call_target="tpu_custom_call" | custom-call | flops 1024 | bytes 1024 | tf_op jit(solution)/shard_map/pallas_call | solution.py:53
  78.6 0.6 collective-permute-start.16
  79.2 1.2 %collective-permute-start.17 = (bf16[256,640]{1,0:T(8,128)(2,1)}, bf16[256,640]{1,0:T(8,128)(2,1)}, u32[]{:S(2)}, u32[]{:S(2)}) collective-permute-start(bf16[256,640]{1,0:T(8,128)(2,1)} %get-tuple-element.51), channel_id=1, source_target_pairs={{0,12},{1,13},{16,28},{17,29},{32,44},{33,45},{48,60},{49,61},{4,0... | collective-permute-start | bytes 983048 | tf_op jit(solution)/shard_map/ppermute | solution.py:33
  80.5 0.1 copy.11.index_ref
  80.6 2.1 %copy-done.1 = bf16[1280,1536]{1,0:T(8,128)(2,1)S(1)} copy-done((bf16[1280,1536]{1,0:T(8,128)(2,1)S(1)}, bf16[1280,1536]{1,0:T(8,128)(2,1)}, u32[]{:S(2)}) %copy-start.1) | copy-done | bytes 3932184
  82.7 1.1 copy-done.5
  83.8 1.3 %shard_map.114.text_ref = f32[32,1536]{1,0:T(8,128)S(1)} custom-call(s32[32,1]{1,0:T(8,128)S(1)} %copy.11.index_ref, bf16[256,1280]{1,0:T(8,128)(2,1)S(1)} %copy-done.5, bf16[1280,1536]{1,0:T(8,128)(2,1)S(1)} %copy-done.1), custom_call_target="tpu_custom_call" | custom-call | flops 1024 | bytes 1024 | tf_op jit(solution)/shard_map/pallas_call | solution.py:53
  85.1 4.9 %collective-permute-done.15.t1 = bf16[256,640]{1,0:T(8,128)(2,1)S(1)} collective-permute-done((bf16[256,640]{1,0:T(8,128)(2,1)}, bf16[256,640]{1,0:T(8,128)(2,1)S(1)}, u32[]{:S(2)}, u32[]{:S(2)}) %collective-permute-start.15) | collective-permute-done | bytes 327712 | tf_op jit(solution)/shard_map/ppermute | solution.py:33
  90.0 4.0 %collective-permute-done.17.t3 = bf16[256,640]{1,0:T(8,128)(2,1)} collective-permute-done((bf16[256,640]{1,0:T(8,128)(2,1)}, bf16[256,640]{1,0:T(8,128)(2,1)}, u32[]{:S(2)}, u32[]{:S(2)}) %collective-permute-start.17) | collective-permute-done | bytes 327712 | tf_op jit(solution)/shard_map/ppermute | solution.py:33
  94.0 2.7 %shard_map.115 = (bf16[4,32,1664]{2,1,0:T(8,128)(2,1)S(1)}, bf16[64,1664]{1,0:T(8,128)(2,1)S(1)}, bf16[64,1664]{1,0:T(8,128)(2,1)S(1)}) custom-call(s32[1]{0:T(128)} %bitcast.core, f32[4,256,640]{2,1,0:T(8,128)S(1)} %shard_map.110.own_ref, bf16[2,128,640]{2,1,0:T(8,128)(2,1)} %collective-permute-done.11.up_ref, ...), custom_call_target="tpu_custom_call" | custom-call | flops 1024 | bytes 1024 | tf_op jit(solution)/shard_map/pallas_call | solution.py:53
  96.7 1.6 %collective-permute-start.19 = (bf16[64,1664]{1,0:T(8,128)(2,1)S(1)}, bf16[64,1664]{1,0:T(8,128)(2,1)S(1)}, u32[]{:S(2)}, u32[]{:S(2)}) collective-permute-start(bf16[64,1664]{1,0:T(8,128)(2,1)S(1)} %get-tuple-element.56), channel_id=1, source_target_pairs={{0,66},{1,67},{16,82},{17,83},{32,98},{33,99},{48,114},{49,115},{4... | collective-permute-start | bytes 638984 | tf_op jit(solution)/shard_map/ppermute | solution.py:33
  98.4 0.4 collective-permute-start.20
  98.8 4.1 %collective-permute-done.19.r_ref = bf16[64,1664]{1,0:T(8,128)(2,1)S(1)} collective-permute-done((bf16[64,1664]{1,0:T(8,128)(2,1)S(1)}, bf16[64,1664]{1,0:T(8,128)(2,1)S(1)}, u32[]{:S(2)}, u32[]{:S(2)}) %collective-permute-start.19) | collective-permute-done | bytes 213024 | tf_op jit(solution)/shard_map/ppermute | solution.py:33
  102.9 2.5 %collective-permute-done.20.l_ref = bf16[64,1664]{1,0:T(8,128)(2,1)S(1)} collective-permute-done((bf16[64,1664]{1,0:T(8,128)(2,1)S(1)}, bf16[64,1664]{1,0:T(8,128)(2,1)S(1)}, u32[]{:S(2)}, u32[]{:S(2)}) %collective-permute-start.20) | collective-permute-done | bytes 213024 | tf_op jit(solution)/shard_map/ppermute | solution.py:33
  105.4 0.1 shard_map.116
  105.5 1.4 %collective-permute-start.21 = (bf16[32,1664]{1,0:T(8,128)(2,1)S(1)}, bf16[32,1664]{1,0:T(8,128)(2,1)S(1)}, u32[]{:S(2)}, u32[]{:S(2)}) collective-permute-start(bf16[32,1664]{1,0:T(8,128)(2,1)S(1)} %get-tuple-element.59), channel_id=1, source_target_pairs={{0,4},{1,5},{16,20},{17,21},{32,36},{33,37},{48,52},{49,53},{4,8},... | collective-permute-start | bytes 319496 | tf_op jit(solution)/shard_map/ppermute | solution.py:33
  106.9 3.2 %collective-permute-start.22 = (bf16[32,1664]{1,0:T(8,128)(2,1)S(1)}, bf16[32,1664]{1,0:T(8,128)(2,1)S(1)}, u32[]{:S(2)}, u32[]{:S(2)}) collective-permute-start(bf16[32,1664]{1,0:T(8,128)(2,1)S(1)} %get-tuple-element.60), channel_id=1, source_target_pairs={{0,8},{1,9},{16,24},{17,25},{32,40},{33,41},{48,56},{49,57},{4,12}... | collective-permute-start | bytes 319496 | tf_op jit(solution)/shard_map/ppermute | solution.py:33
  110.7 1.8 %collective-permute-done.21.s1 = bf16[32,1664]{1,0:T(8,128)(2,1)S(1)} collective-permute-done((bf16[32,1664]{1,0:T(8,128)(2,1)S(1)}, bf16[32,1664]{1,0:T(8,128)(2,1)S(1)}, u32[]{:S(2)}, u32[]{:S(2)}) %collective-permute-start.21) | collective-permute-done | bytes 106528 | tf_op jit(solution)/shard_map/ppermute | solution.py:33
  112.5 1.4 %collective-permute-done.22.s2 = bf16[32,1664]{1,0:T(8,128)(2,1)S(1)} collective-permute-done((bf16[32,1664]{1,0:T(8,128)(2,1)S(1)}, bf16[32,1664]{1,0:T(8,128)(2,1)S(1)}, u32[]{:S(2)}, u32[]{:S(2)}) %collective-permute-start.22) | collective-permute-done | bytes 106528 | tf_op jit(solution)/shard_map/ppermute | solution.py:33
  113.9 0.9 collective-permute-done.23.s3
  114.8 0.9 shard_map.117
  (30 shorter events, 0.1 us)
Async XLA Ops:
  0.6 1.0 copy-start.8
  1.9 49.6 %copy-start.2 = (f32[32,5120]{1,0:T(8,128)}, f32[32,5120]{1,0:T(8,128)S(1)}, u32[]{:S(2)}) copy-start(f32[32,5120]{1,0:T(8,128)S(1)} %get-tuple-element.45.res_ref) | copy-start | bytes 1966084
  2.0 17.2 %collective-permute-start = (bf16[32,5120]{1,0:T(8,128)(2,1)S(1)}, bf16[32,5120]{1,0:T(8,128)(2,1)S(1)}, u32[]{:S(2)}, u32[]{:S(2)}) collective-permute-start(bf16[32,5120]{1,0:T(8,128)(2,1)S(1)} %get-tuple-element.33.n0), channel_id=1, source_target_pairs={{0,12},{1,13},{16,28},{17,29},{32,44},{33,45},{48,60},{49,61},{4,0... | collective-permute-start | bytes 983048 | tf_op jit(solution)/shard_map/ppermute | solution.py:33
  5.1 12.2 %collective-permute-start.1 = (bf16[32,5120]{1,0:T(8,128)(2,1)S(1)}, bf16[32,5120]{1,0:T(8,128)(2,1)S(1)}, u32[]{:S(2)}, u32[]{:S(2)}) collective-permute-start(bf16[32,5120]{1,0:T(8,128)(2,1)S(1)} %get-tuple-element.33.n0), channel_id=1, source_target_pairs={{0,8},{1,9},{16,24},{17,25},{32,40},{33,41},{48,56},{49,57},{4,12}... | collective-permute-start | bytes 983048 | tf_op jit(solution)/shard_map/ppermute | solution.py:33
  5.8 17.1 %collective-permute-start.3 = (bf16[32,5120]{1,0:T(8,128)(2,1)S(1)}, bf16[32,5120]{1,0:T(8,128)(2,1)S(1)}, u32[]{:S(2)}, u32[]{:S(2)}) collective-permute-start(bf16[32,5120]{1,0:T(8,128)(2,1)S(1)} %get-tuple-element.33.n0), channel_id=1, source_target_pairs={{0,4},{1,5},{16,20},{17,21},{32,36},{33,37},{48,52},{49,53},{4,8},... | collective-permute-start | bytes 983048 | tf_op jit(solution)/shard_map/ppermute | solution.py:33
  6.7 8.6 %collective-permute-start.2 = (bf16[32,1280]{1,0:T(8,128)(2,1)}, bf16[32,1280]{1,0:T(8,128)(2,1)S(1)}, u32[]{:S(2)}, u32[]{:S(2)}) collective-permute-start(bf16[32,1280]{1,0:T(8,128)(2,1)} %param.13), channel_id=1, source_target_pairs={{0,64},{1,65},{16,80},{17,81},{32,96},{33,97},{48,112},{49,113},{4... | collective-permute-start | bytes 245768 | tf_op jit(solution)/shard_map/ppermute | solution.py:33
  9.8 23.9 %collective-permute-start.4 = (bf16[800,5120]{1,0:T(8,128)(2,1)}, bf16[800,5120]{1,0:T(8,128)(2,1)}, u32[]{:S(2)}, u32[]{:S(2)}) collective-permute-start(bf16[800,5120]{1,0:T(8,128)(2,1)} %bitcast.26), channel_id=1, source_target_pairs={{0,1},{1,0},{16,17},{17,16},{32,33},{33,32},{48,49},{49,48},{4,5},... | collective-permute-start | bytes 24576008 | tf_op jit(solution)/shard_map/ppermute | solution.py:33
  22.9 18.6 %collective-permute-start.7 = (bf16[800,5120]{1,0:T(8,128)(2,1)}, bf16[800,5120]{1,0:T(8,128)(2,1)}, u32[]{:S(2)}, u32[]{:S(2)}) collective-permute-start(bf16[800,5120]{1,0:T(8,128)(2,1)} %f_ref.5), channel_id=1, source_target_pairs={{0,1},{1,0},{16,17},{17,16},{32,33},{33,32},{48,49},{49,48},{4,5},... | collective-permute-start | bytes 24576008 | tf_op jit(solution)/shard_map/ppermute | solution.py:33
  23.0 6.8 %collective-permute-start.9 = (bf16[64,1280]{1,0:T(8,128)(2,1)S(1)}, bf16[64,1280]{1,0:T(8,128)(2,1)S(1)}, u32[]{:S(2)}, u32[]{:S(2)}) collective-permute-start(bf16[64,1280]{1,0:T(8,128)(2,1)S(1)} %constant_dynamic-update-slice_fusion), channel_id=1, source_target_pairs={{0,16},{1,17},{16,0},{17,1},{32,48},{33,49},{48,32},{49,33},{4,20}... | collective-permute-start | bytes 491528 | tf_op jit(solution)/shard_map/ppermute | solution.py:33
  25.1 20.4 %collective-permute-start.8 = (bf16[64,5120]{1,0:T(8,128)(2,1)S(1)}, bf16[64,5120]{1,0:T(8,128)(2,1)S(1)}, u32[]{:S(2)}, u32[]{:S(2)}) collective-permute-start(bf16[64,5120]{1,0:T(8,128)(2,1)S(1)} %get-tuple-element.35.r), channel_id=1, source_target_pairs={{0,2},{1,3},{16,18},{17,19},{32,34},{33,35},{48,50},{49,51},{4,6},... | collective-permute-start | bytes 1966088 | tf_op jit(solution)/shard_map/ppermute | solution.py:33
  26.6 18.9 %collective-permute-start.6 = (bf16[64,5120]{1,0:T(8,128)(2,1)S(1)}, bf16[64,5120]{1,0:T(8,128)(2,1)S(1)}, u32[]{:S(2)}, u32[]{:S(2)}) collective-permute-start(bf16[64,5120]{1,0:T(8,128)(2,1)S(1)} %get-tuple-element.37.l), channel_id=1, source_target_pairs={{0,66},{1,67},{16,82},{17,83},{32,98},{33,99},{48,114},{49,115},{4... | collective-permute-start | bytes 1966088 | tf_op jit(solution)/shard_map/ppermute | solution.py:33
  29.8 21.7 %collective-permute-start.10 = (bf16[128,1280]{1,0:T(8,128)(2,1)S(1)}, bf16[128,1280]{1,0:T(8,128)(2,1)S(1)}, u32[]{:S(2)}, u32[]{:S(2)}) collective-permute-start(bf16[128,1280]{1,0:T(8,128)(2,1)S(1)} %pad_maximum_fusion), channel_id=1, source_target_pairs={{0,32},{1,33},{16,48},{17,49},{32,0},{33,1},{48,16},{49,17},{4,36}... | collective-permute-start | bytes 983048 | tf_op jit(solution)/shard_map/ppermute | solution.py:33
  33.6 11.9 %collective-permute-start.5 = (bf16[800,128]{1,0:T(8,128)(2,1)S(1)}, bf16[800,128]{1,0:T(8,128)(2,1)S(1)}, u32[]{:S(2)}, u32[]{:S(2)}) collective-permute-start(bf16[800,128]{1,0:T(8,128)(2,1)S(1)} %shard_map.105.wm_ref), channel_id=1, source_target_pairs={{0,1},{1,0},{16,17},{17,16},{32,33},{33,32},{48,49},{49,48},{4,5},... | collective-permute-start | bytes 614408 | tf_op jit(solution)/shard_map/ppermute | solution.py:33
  33.7 3.3 %copy-start = (bf16[5120,800]{0,1:T(8,128)(2,1)S(1)}, bf16[5120,800]{0,1:T(8,128)(2,1)}, u32[]{:S(2)}) copy-start(bf16[5120,800]{0,1:T(8,128)(2,1)} %param.10) | copy-start | bytes 24576004
  51.5 4.0 %copy-start.6 = (f32[256,128]{1,0:T(8,128)}, f32[256,128]{1,0:T(8,128)S(1)}, u32[]{:S(2)}) copy-start(f32[256,128]{1,0:T(8,128)S(1)} %get-tuple-element.41.mean_ref) | copy-start | bytes 393220
  51.5 4.0 %copy-start.4 = (bf16[256,1280]{1,0:T(8,128)(2,1)}, bf16[256,1280]{1,0:T(8,128)(2,1)S(1)}, u32[]{:S(2)}) copy-start(bf16[256,1280]{1,0:T(8,128)(2,1)S(1)} %constant_dynamic-update-slice_fusion.2.pooled_ref) | copy-start | bytes 1966084
  55.5 38.4 %collective-permute-start.18 = (bf16[320,1536]{1,0:T(8,128)(2,1)}, bf16[320,1536]{1,0:T(8,128)(2,1)}, u32[]{:S(2)}, u32[]{:S(2)}) collective-permute-start(bf16[320,1536]{1,0:T(8,128)(2,1)} %w_ref), channel_id=1, source_target_pairs={{0,1},{1,0},{16,17},{17,16},{32,33},{33,32},{48,49},{49,48},{4,5},... | collective-permute-start | bytes 2949128 | tf_op jit(solution)/shard_map/ppermute | solution.py:33
  56.1 14.7 %collective-permute-start.13 = (bf16[2,128,640]{2,1,0:T(8,128)(2,1)}, bf16[2,128,640]{2,1,0:T(8,128)(2,1)}, u32[]{:S(2)}, u32[]{:S(2)}) collective-permute-start(bf16[2,128,640]{2,1,0:T(8,128)(2,1)} %get-tuple-element.48), channel_id=1, source_target_pairs={{0,66},{1,67},{16,82},{17,83},{32,98},{33,99},{48,114},{49,115},{4... | collective-permute-start | bytes 983048 | tf_op jit(solution)/shard_map/ppermute | solution.py:33
  58.8 12.1 %collective-permute-start.14 = (bf16[2,128,640]{2,1,0:T(8,128)(2,1)}, bf16[2,128,640]{2,1,0:T(8,128)(2,1)}, u32[]{:S(2)}, u32[]{:S(2)}) collective-permute-start(bf16[2,128,640]{2,1,0:T(8,128)(2,1)} %get-tuple-element.49), channel_id=1, source_target_pairs={{0,2},{1,3},{16,18},{17,19},{32,34},{33,35},{48,50},{49,51},{4,6},... | collective-permute-start | bytes 983048 | tf_op jit(solution)/shard_map/ppermute | solution.py:33
  58.8 14.6 %collective-permute-start.11 = (bf16[2,128,640]{2,1,0:T(8,128)(2,1)}, bf16[2,128,640]{2,1,0:T(8,128)(2,1)}, u32[]{:S(2)}, u32[]{:S(2)}) collective-permute-start(bf16[2,128,640]{2,1,0:T(8,128)(2,1)} %get-tuple-element.46), channel_id=1, source_target_pairs={{0,66},{1,67},{16,82},{17,83},{32,98},{33,99},{48,114},{49,115},{4... | collective-permute-start | bytes 983048 | tf_op jit(solution)/shard_map/ppermute | solution.py:33
  62.0 14.7 %collective-permute-start.12 = (bf16[2,128,640]{2,1,0:T(8,128)(2,1)}, bf16[2,128,640]{2,1,0:T(8,128)(2,1)}, u32[]{:S(2)}, u32[]{:S(2)}) collective-permute-start(bf16[2,128,640]{2,1,0:T(8,128)(2,1)} %get-tuple-element.47), channel_id=1, source_target_pairs={{0,2},{1,3},{16,18},{17,19},{32,34},{33,35},{48,50},{49,51},{4,6},... | collective-permute-start | bytes 983048 | tf_op jit(solution)/shard_map/ppermute | solution.py:33
  62.1 1.1 copy-start.3
  63.2 0.9 copy-start.7
  64.1 16.4 %copy-start.9 = (s32[32]{0:T(128)S(1)}, s32[32]{0:T(128)}, u32[]{:S(2)}) copy-start(s32[32]{0:T(128)} %param.16) | copy-start | bytes 388
  64.1 16.4 %copy-start.10 = (s32[32,1]{0,1:T(1,128)S(1)}, s32[32,1]{0,1:T(1,128)}, u32[]{:S(2)}) copy-start(s32[32,1]{0,1:T(1,128)} %param.15) | copy-start | bytes 388
  72.9 17.1 %collective-permute-start.15 = (bf16[256,640]{1,0:T(8,128)(2,1)}, bf16[256,640]{1,0:T(8,128)(2,1)S(1)}, u32[]{:S(2)}, u32[]{:S(2)}) collective-permute-start(bf16[256,640]{1,0:T(8,128)(2,1)} %get-tuple-element.50), channel_id=1, source_target_pairs={{0,4},{1,5},{16,20},{17,21},{32,36},{33,37},{48,52},{49,53},{4,8},... | collective-permute-start | bytes 983048 | tf_op jit(solution)/shard_map/ppermute | solution.py:33
  78.6 11.4 %collective-permute-start.16 = (bf16[256,640]{1,0:T(8,128)(2,1)}, bf16[256,640]{1,0:T(8,128)(2,1)S(1)}, u32[]{:S(2)}, u32[]{:S(2)}) collective-permute-start(bf16[256,640]{1,0:T(8,128)(2,1)} %shard_map.113), channel_id=1, source_target_pairs={{0,8},{1,9},{16,24},{17,25},{32,40},{33,41},{48,56},{49,57},{4,12}... | collective-permute-start | bytes 983048 | tf_op jit(solution)/shard_map/ppermute | solution.py:33
  79.2 14.7 %collective-permute-start.17 = (bf16[256,640]{1,0:T(8,128)(2,1)}, bf16[256,640]{1,0:T(8,128)(2,1)}, u32[]{:S(2)}, u32[]{:S(2)}) collective-permute-start(bf16[256,640]{1,0:T(8,128)(2,1)} %get-tuple-element.51), channel_id=1, source_target_pairs={{0,12},{1,13},{16,28},{17,29},{32,44},{33,45},{48,60},{49,61},{4,0... | collective-permute-start | bytes 983048 | tf_op jit(solution)/shard_map/ppermute | solution.py:33
  80.6 2.1 %copy-start.1 = (bf16[1280,1536]{1,0:T(8,128)(2,1)S(1)}, bf16[1280,1536]{1,0:T(8,128)(2,1)}, u32[]{:S(2)}) copy-start(bf16[1280,1536]{1,0:T(8,128)(2,1)} %proj_ref.1) | copy-start | bytes 11796484
  82.7 1.1 copy-start.5
  96.7 6.2 %collective-permute-start.19 = (bf16[64,1664]{1,0:T(8,128)(2,1)S(1)}, bf16[64,1664]{1,0:T(8,128)(2,1)S(1)}, u32[]{:S(2)}, u32[]{:S(2)}) collective-permute-start(bf16[64,1664]{1,0:T(8,128)(2,1)S(1)} %get-tuple-element.56), channel_id=1, source_target_pairs={{0,66},{1,67},{16,82},{17,83},{32,98},{33,99},{48,114},{49,115},{4... | collective-permute-start | bytes 638984 | tf_op jit(solution)/shard_map/ppermute | solution.py:33
  98.4 7.1 %collective-permute-start.20 = (bf16[64,1664]{1,0:T(8,128)(2,1)S(1)}, bf16[64,1664]{1,0:T(8,128)(2,1)S(1)}, u32[]{:S(2)}, u32[]{:S(2)}) collective-permute-start(bf16[64,1664]{1,0:T(8,128)(2,1)S(1)} %get-tuple-element.57), channel_id=1, source_target_pairs={{0,2},{1,3},{16,18},{17,19},{32,34},{33,35},{48,50},{49,51},{4,6},... | collective-permute-start | bytes 638984 | tf_op jit(solution)/shard_map/ppermute | solution.py:33
  105.5 7.0 %collective-permute-start.21 = (bf16[32,1664]{1,0:T(8,128)(2,1)S(1)}, bf16[32,1664]{1,0:T(8,128)(2,1)S(1)}, u32[]{:S(2)}, u32[]{:S(2)}) collective-permute-start(bf16[32,1664]{1,0:T(8,128)(2,1)S(1)} %get-tuple-element.59), channel_id=1, source_target_pairs={{0,4},{1,5},{16,20},{17,21},{32,36},{33,37},{48,52},{49,53},{4,8},... | collective-permute-start | bytes 319496 | tf_op jit(solution)/shard_map/ppermute | solution.py:33
  106.9 7.0 %collective-permute-start.22 = (bf16[32,1664]{1,0:T(8,128)(2,1)S(1)}, bf16[32,1664]{1,0:T(8,128)(2,1)S(1)}, u32[]{:S(2)}, u32[]{:S(2)}) collective-permute-start(bf16[32,1664]{1,0:T(8,128)(2,1)S(1)} %get-tuple-element.60), channel_id=1, source_target_pairs={{0,8},{1,9},{16,24},{17,25},{32,40},{33,41},{48,56},{49,57},{4,12}... | collective-permute-start | bytes 319496 | tf_op jit(solution)/shard_map/ppermute | solution.py:33
  110.1 4.7 %collective-permute-start.23 = (bf16[32,1664]{1,0:T(8,128)(2,1)S(1)}, bf16[32,1664]{1,0:T(8,128)(2,1)S(1)}, u32[]{:S(2)}, u32[]{:S(2)}) collective-permute-start(bf16[32,1664]{1,0:T(8,128)(2,1)S(1)} %get-tuple-element.61), channel_id=1, source_target_pairs={{0,12},{1,13},{16,28},{17,29},{32,44},{33,45},{48,60},{49,61},{4,0... | collective-permute-start | bytes 319496 | tf_op jit(solution)/shard_map/ppermute | solution.py:33

commit v4 on v3

--- a/solution.py
+++ b/solution.py
@@ -106,20 +106,18 @@
         copy.wait()
 
 
-def stage_kernel(w_ref, v_ref, out_ref, sems):
+def stage_kernel(w_ref, out_ref, sems):
     copies = [
-        pltpu.make_async_copy(ref.at[pl.ds(at, 400)], out_ref.at[pl.ds(base + at, 400)], sems.at[(base + at) // 400])
-        for base, ref in ((0, w_ref), (800, v_ref))
-        for at in (0, 400)
+        pltpu.make_async_copy(w_ref.at[pl.ds(at, 400)], out_ref.at[pl.ds(at, 400)], sems.at[at // 400]) for at in (0, 400)
     ]
     start(copies)
     wait(copies)
 
 
-def stage_call(w, v):
-    outs = (struct((1600, w.shape[1]), bf16),)
-    return call(
-        stage_kernel, (), (w, v), outs, [pltpu.SemaphoreType.DMA((4,))], remote=2, limit=4, size=32 * 1024 * 1024
+def stage_call(w):
+    outs = (struct(w.shape, bf16),)
+    return call(
+        stage_kernel, (), (w,), outs, [pltpu.SemaphoreType.DMA((2,))], remote=1, limit=4, size=16 * 1024 * 1024
     )[0]
 
 
@@ -151,12 +149,12 @@
         yield q, upper, lower
 
 
-def fc1_kernel(w_ref, wm_ref, vm_ref, r, b, a, l, h_ref, mean_ref, rows, sems):
-    parts = [pltpu.make_async_copy(ref, rows.at[pl.ds(64 * k, 64)], sems.at[k]) for k, ref in enumerate((r, b, a, l))]
-    start(parts)
-    wait(parts)
+def fc1_kernel(w_ref, v_ref, wm_ref, vm_ref, r, b, a, l, h_ref, mean_ref, rows):
+    for k, ref in enumerate((r, b, a, l)):
+        rows[64 * k : 64 * k + 64] = ref[...]
     for at in range(0, 1600, 400):
-        z = lax.dot_general(w_ref[at : at + 400], rows[...], NT, preferred_element_type=f32)
+        ref = w_ref if at < 800 else v_ref
+        z = lax.dot_general(ref[at % 800 : at % 800 + 400], rows[...], NT, preferred_element_type=f32)
         act = 0.5 * z * (1.0 + lax.erf(z * (0.5**0.5)))
         h_ref[at : at + 400] = act.astype(bf16)
     means = lax.dot_general(h_ref[0:800], wm_ref[...], TN, preferred_element_type=f32) + lax.dot_general(
@@ -165,15 +163,14 @@
     mean_ref[...] = jnp.broadcast_to(jnp.sum(means, axis=-1, keepdims=True), mean_ref.shape)
 
 
-def fc1_call(rows, w, w_mean, v_mean):
+def fc1_call(rows, w, v, w_mean, v_mean):
     outs = (struct((1600, 256), bf16), struct((256, 128), f32))
     return call(
         fc1_kernel,
         (),
-        (w, w_mean, v_mean, *rows),
+        (w, v, w_mean, v_mean, *rows),
         outs,
-        scratch=[pltpu.VMEM((256, w.shape[1]), bf16), pltpu.SemaphoreType.DMA((4,))],
-        remote=4,
+        scratch=[pltpu.VMEM((256, w.shape[1]), bf16)],
         limit=10,
     )
 
@@ -334,21 +331,22 @@
     n1, n3, n2 = shift(normed, dy=-1), shift(normed, dy=1), shift(normed, dy=2)
     pooled = jnp.concatenate([text_pooled, shift(text_pooled, dx=2)])
     w_mean = mean_call(fc2_weight)
-    r, l = halves_call(normed, n1, after(n2, w_mean, pooled), n3)
+    fc1_near = stage_call(after(fc1_rows, w_mean))
+    r, l = halves_call(normed, n1, after(n2, w_mean, pooled, fc1_near), n3)
     a, b = shift(r, dx=1), shift(l, dx=-1)
     fc2_other = shift(after(fc2_weight, r), flip=True)
     v_mean = shift(w_mean, flip=True)
     pooled = after(pooled, r)
     pooled = jnp.concatenate([pooled, shift(pooled, mz=1)])
     pooled_far = shift(pooled, mz=2)
-    fc1_both = stage_call(after(fc1_rows, r), fc1_other)
+    fc1_far = stage_call(fc1_other)
 
     def blocks(parity, *ks):
         return jnp.stack([2 * ((y + k) % 4) + parity for k in ks]).astype(jnp.int32)
 
     cols = blocks(1 - x_lo, 1, 3, 2, 0)
     fc2_both = columns_call(cols, fc2_weight, fc2_other)
-    h, h_mean = fc1_call((r, after(b, fc2_both), a, l), fc1_both, w_mean, v_mean)
+    h, h_mean = fc1_call((r, after(b, fc2_both), a, l), fc1_near, fc1_far, w_mean, v_mean)
     pooled = jnp.concatenate([pooled, after(pooled_far, h)])
     to_r, to_l, to_r2, to_l2 = away_call(cols, h, h_mean, after(centred, pooled), fc2_both)
     got_r, got_l = shift(to_l, dx=-1), shift(to_r, dx=1)

time: 116 us -> 114 us (0.983)
  waiting for transfers between devices: 32.5 us -> 30.1 us
    ppermute x24, waiting for transfers between devices: 32.5 us -> 30.1 us  [shift(): return lax.ppermute(value, AXES, moves(**step))]
    pallas_call x14 -> x15, Pallas kernels: 38.9 us -> 38.5 us  [call(): pl.pallas_call(body, in_specs=[SM] * len(scalars) + [VM] * inside + [HB]...]
    unnamed x25 -> x31, local copies, waits for them, and re-layouts: 10.4 us -> 10.4 us
  transfers between devices with their start and end apart: 24 -> 24, of which waited for: 14 -> 13; matrix products, arithmetic and copies ran while one was open for 1% -> 1% of each run, Pallas kernels for 27% -> 27%
where the time goes in v4:
time: 114 us; the launch traced here: 113 us
  Pallas kernels  38.5 us (34%)
  starting transfers between devices  32.4 us (28%)
  waiting for transfers between devices  30.1 us (26%)
  local copies, waits for them, and re-layouts  10.6 us (9%)
  between operations  1.56 us (1%)
    pallas_call x15, Pallas kernels, call(): pl.pallas_call(body, in_specs=[SM] * len(scalars) + [VM] * inside + [HB]...  38.5 us
    ppermute x24, starting transfers between devices, shift(): return lax.ppermute(value, AXES, moves(**step))  32.4 us
    ppermute x24, waiting for transfers between devices, shift(): return lax.ppermute(value, AXES, moves(**step))  30.1 us
    unnamed x31, local copies, waits for them, and re-layouts  10.4 us
  transfers between devices with their start and end apart: 24, of which 13 were waited for; matrix products, arithmetic and copies ran while one was open for 1% of the time, Pallas kernels for 27%

profile of v4, /device:TPU:0, one launch (start us, length us, event | category | flops | bytes accessed | tf_op | source)
XLA Modules:
  0.0 113.4 jit_solution(6283049269056592019)
XLA Ops:
  0.6 0.0 copy-start.1
  0.7 1.1 copy-done.9
  1.8 0.3 shard_map.107
  2.1 3.2 %collective-permute-start.2 = (bf16[32,5120]{1,0:T(8,128)(2,1)S(1)}, bf16[32,5120]{1,0:T(8,128)(2,1)S(1)}, u32[]{:S(2)}, u32[]{:S(2)}) collective-permute-start(bf16[32,5120]{1,0:T(8,128)(2,1)S(1)} %get-tuple-element.34.n0), channel_id=1, source_target_pairs={{0,12},{1,13},{16,28},{17,29},{32,44},{33,45},{48,60},{49,61},{4,0... | collective-permute-start | bytes 983048 | tf_op jit(solution)/shard_map/ppermute | solution.py:33
  5.3 0.6 collective-permute-start.3
  5.9 1.0 collective-permute-start.5
  6.9 0.0 collective-permute-start
  6.9 3.0 %collective-permute-start.4 = (bf16[32,1280]{1,0:T(8,128)(2,1)}, bf16[32,1280]{1,0:T(8,128)(2,1)S(1)}, u32[]{:S(2)}, u32[]{:S(2)}) collective-permute-start(bf16[32,1280]{1,0:T(8,128)(2,1)} %param.13), channel_id=1, source_target_pairs={{0,64},{1,65},{16,80},{17,81},{32,96},{33,97},{48,112},{49,113},{4... | collective-permute-start | bytes 245768 | tf_op jit(solution)/shard_map/ppermute | solution.py:33
  9.9 0.9 constant_dynamic-update-slice_fusion.1
  10.8 4.7 %shard_map.104.wm_ref = bf16[800,128]{1,0:T(8,128)(2,1)S(1)} custom-call(bf16[800,5120]{1,0:T(8,128)(2,1)} %f_ref.5), custom_call_target="tpu_custom_call" | custom-call | flops 1024 | bytes 16777216 | tf_op jit(solution)/shard_map/pallas_call | solution.py:53
  15.5 1.0 shard_map.105.w_ref
  16.5 3.1 %copy-done = bf16[800,5120]{1,0:T(8,128)(2,1)} copy-done((bf16[800,5120]{1,0:T(8,128)(2,1)}, bf16[800,5120]{1,0:T(8,128)(2,1)S(1)}, u32[]{:S(2)}) %copy-start) | copy-done | bytes 8192024
  19.7 0.0 collective-permute-done.3.n2
  19.7 3.3 %collective-permute-done.5.n3 = bf16[32,5120]{1,0:T(8,128)(2,1)S(1)} collective-permute-done((bf16[32,5120]{1,0:T(8,128)(2,1)S(1)}, bf16[32,5120]{1,0:T(8,128)(2,1)S(1)}, u32[]{:S(2)}, u32[]{:S(2)}) %collective-permute-start.5) | collective-permute-done | bytes 327712 | tf_op jit(solution)/shard_map/ppermute | solution.py:33
  23.0 0.1 shard_map.108
  23.1 0.1 collective-permute-start.7
  23.2 2.0 %collective-permute-start.9 = (bf16[64,1280]{1,0:T(8,128)(2,1)S(1)}, bf16[64,1280]{1,0:T(8,128)(2,1)S(1)}, u32[]{:S(2)}, u32[]{:S(2)}) collective-permute-start(bf16[64,1280]{1,0:T(8,128)(2,1)S(1)} %constant_dynamic-update-slice_fusion), channel_id=1, source_target_pairs={{0,16},{1,17},{16,0},{17,1},{32,48},{33,49},{48,32},{49,33},{4,20}... | collective-permute-start | bytes 491528 | tf_op jit(solution)/shard_map/ppermute | solution.py:33
  25.2 0.1 pad_add_fusion.1.cols
  25.2 1.5 %collective-permute-start.8 = (bf16[64,5120]{1,0:T(8,128)(2,1)S(1)}, bf16[64,5120]{1,0:T(8,128)(2,1)S(1)}, u32[]{:S(2)}, u32[]{:S(2)}) collective-permute-start(bf16[64,5120]{1,0:T(8,128)(2,1)S(1)} %get-tuple-element.36.r), channel_id=1, source_target_pairs={{0,2},{1,3},{16,18},{17,19},{32,34},{33,35},{48,50},{49,51},{4,6},... | collective-permute-start | bytes 1966088 | tf_op jit(solution)/shard_map/ppermute | solution.py:33
  26.7 1.7 %collective-permute-start.6 = (bf16[64,5120]{1,0:T(8,128)(2,1)S(1)}, bf16[64,5120]{1,0:T(8,128)(2,1)S(1)}, u32[]{:S(2)}, u32[]{:S(2)}) collective-permute-start(bf16[64,5120]{1,0:T(8,128)(2,1)S(1)} %get-tuple-element.37.l), channel_id=1, source_target_pairs={{0,66},{1,67},{16,82},{17,83},{32,98},{33,99},{48,114},{49,115},{4... | collective-permute-start | bytes 1966088 | tf_op jit(solution)/shard_map/ppermute | solution.py:33
  28.5 1.5 %collective-permute-done.9 = bf16[64,1280]{1,0:T(8,128)(2,1)S(1)} collective-permute-done((bf16[64,1280]{1,0:T(8,128)(2,1)S(1)}, bf16[64,1280]{1,0:T(8,128)(2,1)S(1)}, u32[]{:S(2)}, u32[]{:S(2)}) %collective-permute-start.9) | collective-permute-done | bytes 163872 | tf_op jit(solution)/shard_map/ppermute | solution.py:33
  30.0 3.8 %collective-permute-start.10 = (bf16[128,1280]{1,0:T(8,128)(2,1)S(1)}, bf16[128,1280]{1,0:T(8,128)(2,1)S(1)}, u32[]{:S(2)}, u32[]{:S(2)}) collective-permute-start(bf16[128,1280]{1,0:T(8,128)(2,1)S(1)} %pad_maximum_fusion), channel_id=1, source_target_pairs={{0,32},{1,33},{16,48},{17,49},{32,0},{33,1},{48,16},{49,17},{4,36}... | collective-permute-start | bytes 983048 | tf_op jit(solution)/shard_map/ppermute | solution.py:33
  33.8 0.0 collective-permute-done.w_ref
  33.8 0.1 collective-permute-start.1
  33.9 0.0 slice-start
  33.9 3.6 %shard_map.106.v_ref = bf16[800,5120]{1,0:T(8,128)(2,1)S(1)} custom-call(bf16[800,5120]{1,0:T(8,128)(2,1)} %collective-permute-done.w_ref), custom_call_target="tpu_custom_call" | custom-call | flops 1024 | bytes 16777216 | tf_op jit(solution)/shard_map/pallas_call | solution.py:53
  37.5 0.0 slice-start.1
  37.5 4.3 %shard_map.109.f_ref = bf16[1600,2560]{1,0:T(8,128)(2,1)S(1)} custom-call(s32[4]{0:T(128)S(1)} %pad_add_fusion.1.cols, bf16[800,5120]{1,0:T(8,128)(2,1)} %f_ref.5, bf16[800,5120]{1,0:T(8,128)(2,1)} %collective-permute-done.7.o_ref), custom_call_target="tpu_custom_call" | custom-call | flops 1024 | bytes 16777216 | tf_op jit(solution)/shard_map/pallas_call | solution.py:53
  41.8 1.4 %collective-permute-done.6.b = bf16[64,5120]{1,0:T(8,128)(2,1)S(1)} collective-permute-done((bf16[64,5120]{1,0:T(8,128)(2,1)S(1)}, bf16[64,5120]{1,0:T(8,128)(2,1)S(1)}, u32[]{:S(2)}, u32[]{:S(2)}) %collective-permute-start.6) | collective-permute-done | bytes 655392 | tf_op jit(solution)/shard_map/ppermute | solution.py:33
  43.3 5.1 %shard_map.110 = (bf16[1600,256]{1,0:T(8,128)(2,1)S(1)}, f32[256,128]{1,0:T(8,128)S(1)}) custom-call(bf16[800,5120]{1,0:T(8,128)(2,1)S(1)} %bitcast.27, bf16[800,5120]{1,0:T(8,128)(2,1)S(1)} %shard_map.106.v_ref, bf16[800,128]{1,0:T(8,128)(2,1)S(1)} %shard_map.104.wm_ref, bf16[800,128]{1,0:T(8,128)(2,1)S(1)} %collective-permute-done.1.vm_ref, ...), custom_call_target="tpu_custom_call" | custom-call | flops 1024 | bytes 1024 | tf_op jit(solution)/shard_map/pallas_call | solution.py:53
  48.4 4.0 %shard_map.112 = (bf16[2,128,640]{2,1,0:T(8,128)(2,1)}, bf16[2,128,640]{2,1,0:T(8,128)(2,1)}, bf16[2,128,640]{2,1,0:T(8,128)(2,1)}, bf16[2,128,640]{2,1,0:T(8,128)(2,1)}) custom-call(s32[4]{0:T(128)S(1)} %pad_add_fusion.1.cols, bf16[1600,256]{1,0:T(8,128)(2,1)S(1)} %get-tuple-element.40.h_ref, f32[256,128]{1,0:T(8,128)S(1)} %get-tuple-element.41.mean_ref, ...), custom_call_target="tpu_custom_call" | custom-call | flops 1024 | bytes 1024 | tf_op jit(solution)/shard_map/pallas_call | solution.py:53
  52.4 0.0 collective-permute-start.18
  52.4 3.0 %collective-permute-start.13 = (bf16[2,128,640]{2,1,0:T(8,128)(2,1)}, bf16[2,128,640]{2,1,0:T(8,128)(2,1)}, u32[]{:S(2)}, u32[]{:S(2)}) collective-permute-start(bf16[2,128,640]{2,1,0:T(8,128)(2,1)} %get-tuple-element.48), channel_id=1, source_target_pairs={{0,66},{1,67},{16,82},{17,83},{32,98},{33,99},{48,114},{49,115},{4... | collective-permute-start | bytes 983048 | tf_op jit(solution)/shard_map/ppermute | solution.py:33
  55.4 0.0 collective-permute-start.14
  55.4 3.2 %collective-permute-start.11 = (bf16[2,128,640]{2,1,0:T(8,128)(2,1)}, bf16[2,128,640]{2,1,0:T(8,128)(2,1)}, u32[]{:S(2)}, u32[]{:S(2)}) collective-permute-start(bf16[2,128,640]{2,1,0:T(8,128)(2,1)} %get-tuple-element.46), channel_id=1, source_target_pairs={{0,66},{1,67},{16,82},{17,83},{32,98},{33,99},{48,114},{49,115},{4... | collective-permute-start | bytes 983048 | tf_op jit(solution)/shard_map/ppermute | solution.py:33
  58.7 0.1 pad_add_fusion.cols
  58.8 1.1 copy-done.4
  59.9 0.9 copy-done.8
  60.8 6.6 %shard_map.111.own_ref = f32[4,256,640]{2,1,0:T(8,128)S(1)} custom-call(s32[4]{0:T(128)S(1)} %pad_add_fusion.cols, bf16[1600,256]{1,0:T(8,128)(2,1)S(1)} %get-tuple-element.40.h_ref, f32[256,128]{1,0:T(8,128)S(1)} %copy-done.8, f32[32,5120]{1,0:T(8,128)S(1)} %copy-done.4, bf16[800,5120]{1,0:T(8,128)(2,1)} %f_ref.5, ...), custom_call_target="tpu_custom_call" | custom-call | flops 1024 | bytes 16777216 | tf_op jit(solution)/shard_map/pallas_call | solution.py:53
  67.4 0.1 collective-permute-done.14.low_ref
  67.5 2.0 %shard_map.113 = (bf16[256,640]{1,0:T(8,128)(2,1)}, bf16[256,640]{1,0:T(8,128)(2,1)}) custom-call(f32[4,256,640]{2,1,0:T(8,128)S(1)} %shard_map.111.own_ref, bf16[2,128,640]{2,1,0:T(8,128)(2,1)} %collective-permute-done.13.up_ref, bf16[2,128,640]{2,1,0:T(8,128)(2,1)} %collective-permute-done.14.low_ref), custom_call_target="tpu_custom_call" | custom-call | flops 1024 | bytes 1024 | tf_op jit(solution)/shard_map/pallas_call | solution.py:53
  69.5 0.8 collective-permute-done.11.up_ref
  70.4 3.4 %collective-permute-done.12.low_ref = bf16[2,128,640]{2,1,0:T(8,128)(2,1)} collective-permute-done((bf16[2,128,640]{2,1,0:T(8,128)(2,1)}, bf16[2,128,640]{2,1,0:T(8,128)(2,1)}, u32[]{:S(2)}, u32[]{:S(2)}) %collective-permute-start.12) | collective-permute-done | bytes 327712 | tf_op jit(solution)/shard_map/ppermute | solution.py:33
  73.8 1.9 %shard_map.114 = bf16[256,640]{1,0:T(8,128)(2,1)} custom-call(f32[4,256,640]{2,1,0:T(8,128)S(1)} %shard_map.111.own_ref, bf16[2,128,640]{2,1,0:T(8,128)(2,1)} %collective-permute-done.11.up_ref, bf16[2,128,640]{2,1,0:T(8,128)(2,1)} %collective-permute-done.12.low_ref), custom_call_target="tpu_custom_call" | custom-call | flops 1024 | bytes 1024 | tf_op jit(solution)/shard_map/pallas_call | solution.py:53
  75.6 0.6 collective-permute-start.16
  76.3 1.2 %collective-permute-start.17 = (bf16[256,640]{1,0:T(8,128)(2,1)}, bf16[256,640]{1,0:T(8,128)(2,1)}, u32[]{:S(2)}, u32[]{:S(2)}) collective-permute-start(bf16[256,640]{1,0:T(8,128)(2,1)} %get-tuple-element.51), channel_id=1, source_target_pairs={{0,12},{1,13},{16,28},{17,29},{32,44},{33,45},{48,60},{49,61},{4,0... | collective-permute-start | bytes 983048 | tf_op jit(solution)/shard_map/ppermute | solution.py:33
  77.5 0.1 copy.11.index_ref
  77.6 2.1 %copy-done.2 = bf16[1280,1536]{1,0:T(8,128)(2,1)S(1)} copy-done((bf16[1280,1536]{1,0:T(8,128)(2,1)S(1)}, bf16[1280,1536]{1,0:T(8,128)(2,1)}, u32[]{:S(2)}) %copy-start.2) | copy-done | bytes 3932184
  79.7 1.1 copy-done.6
  80.8 1.3 %shard_map.115.text_ref = f32[32,1536]{1,0:T(8,128)S(1)} custom-call(s32[32,1]{1,0:T(8,128)S(1)} %copy.11.index_ref, bf16[256,1280]{1,0:T(8,128)(2,1)S(1)} %copy-done.6, bf16[1280,1536]{1,0:T(8,128)(2,1)S(1)} %copy-done.2), custom_call_target="tpu_custom_call" | custom-call | flops 1024 | bytes 1024 | tf_op jit(solution)/shard_map/pallas_call | solution.py:53
  82.1 4.9 %collective-permute-done.15.t1 = bf16[256,640]{1,0:T(8,128)(2,1)S(1)} collective-permute-done((bf16[256,640]{1,0:T(8,128)(2,1)}, bf16[256,640]{1,0:T(8,128)(2,1)S(1)}, u32[]{:S(2)}, u32[]{:S(2)}) %collective-permute-start.15) | collective-permute-done | bytes 327712 | tf_op jit(solution)/shard_map/ppermute | solution.py:33
  87.1 4.4 %collective-permute-done.17.t3 = bf16[256,640]{1,0:T(8,128)(2,1)} collective-permute-done((bf16[256,640]{1,0:T(8,128)(2,1)}, bf16[256,640]{1,0:T(8,128)(2,1)}, u32[]{:S(2)}, u32[]{:S(2)}) %collective-permute-start.17) | collective-permute-done | bytes 327712 | tf_op jit(solution)/shard_map/ppermute | solution.py:33
  91.4 2.7 %shard_map.116 = (bf16[4,32,1664]{2,1,0:T(8,128)(2,1)S(1)}, bf16[64,1664]{1,0:T(8,128)(2,1)S(1)}, bf16[64,1664]{1,0:T(8,128)(2,1)S(1)}) custom-call(s32[1]{0:T(128)} %bitcast.core, f32[4,256,640]{2,1,0:T(8,128)S(1)} %shard_map.111.own_ref, bf16[2,128,640]{2,1,0:T(8,128)(2,1)} %collective-permute-done.11.up_ref, ...), custom_call_target="tpu_custom_call" | custom-call | flops 1024 | bytes 1024 | tf_op jit(solution)/shard_map/pallas_call | solution.py:53
  94.1 1.2 %collective-permute-start.19 = (bf16[64,1664]{1,0:T(8,128)(2,1)S(1)}, bf16[64,1664]{1,0:T(8,128)(2,1)S(1)}, u32[]{:S(2)}, u32[]{:S(2)}) collective-permute-start(bf16[64,1664]{1,0:T(8,128)(2,1)S(1)} %get-tuple-element.56), channel_id=1, source_target_pairs={{0,66},{1,67},{16,82},{17,83},{32,98},{33,99},{48,114},{49,115},{4... | collective-permute-start | bytes 638984 | tf_op jit(solution)/shard_map/ppermute | solution.py:33
  95.4 0.8 collective-permute-start.20
  96.2 4.1 %collective-permute-done.19.r_ref = bf16[64,1664]{1,0:T(8,128)(2,1)S(1)} collective-permute-done((bf16[64,1664]{1,0:T(8,128)(2,1)S(1)}, bf16[64,1664]{1,0:T(8,128)(2,1)S(1)}, u32[]{:S(2)}, u32[]{:S(2)}) %collective-permute-start.19) | collective-permute-done | bytes 213024 | tf_op jit(solution)/shard_map/ppermute | solution.py:33
  100.3 2.1 %collective-permute-done.20.l_ref = bf16[64,1664]{1,0:T(8,128)(2,1)S(1)} collective-permute-done((bf16[64,1664]{1,0:T(8,128)(2,1)S(1)}, bf16[64,1664]{1,0:T(8,128)(2,1)S(1)}, u32[]{:S(2)}, u32[]{:S(2)}) %collective-permute-start.20) | collective-permute-done | bytes 213024 | tf_op jit(solution)/shard_map/ppermute | solution.py:33
  102.4 0.1 shard_map.117
  102.5 1.7 %collective-permute-start.21 = (bf16[32,1664]{1,0:T(8,128)(2,1)S(1)}, bf16[32,1664]{1,0:T(8,128)(2,1)S(1)}, u32[]{:S(2)}, u32[]{:S(2)}) collective-permute-start(bf16[32,1664]{1,0:T(8,128)(2,1)S(1)} %get-tuple-element.59), channel_id=1, source_target_pairs={{0,4},{1,5},{16,20},{17,21},{32,36},{33,37},{48,52},{49,53},{4,8},... | collective-permute-start | bytes 319496 | tf_op jit(solution)/shard_map/ppermute | solution.py:33
  104.3 3.5 %collective-permute-start.22 = (bf16[32,1664]{1,0:T(8,128)(2,1)S(1)}, bf16[32,1664]{1,0:T(8,128)(2,1)S(1)}, u32[]{:S(2)}, u32[]{:S(2)}) collective-permute-start(bf16[32,1664]{1,0:T(8,128)(2,1)S(1)} %get-tuple-element.60), channel_id=1, source_target_pairs={{0,8},{1,9},{16,24},{17,25},{32,40},{33,41},{48,56},{49,57},{4,12}... | collective-permute-start | bytes 319496 | tf_op jit(solution)/shard_map/ppermute | solution.py:33
  108.4 1.7 %collective-permute-done.21.s1 = bf16[32,1664]{1,0:T(8,128)(2,1)S(1)} collective-permute-done((bf16[32,1664]{1,0:T(8,128)(2,1)S(1)}, bf16[32,1664]{1,0:T(8,128)(2,1)S(1)}, u32[]{:S(2)}, u32[]{:S(2)}) %collective-permute-start.21) | collective-permute-done | bytes 106528 | tf_op jit(solution)/shard_map/ppermute | solution.py:33
  110.1 1.7 %collective-permute-done.22.s2 = bf16[32,1664]{1,0:T(8,128)(2,1)S(1)} collective-permute-done((bf16[32,1664]{1,0:T(8,128)(2,1)S(1)}, bf16[32,1664]{1,0:T(8,128)(2,1)S(1)}, u32[]{:S(2)}, u32[]{:S(2)}) %collective-permute-start.22) | collective-permute-done | bytes 106528 | tf_op jit(solution)/shard_map/ppermute | solution.py:33
  111.8 0.7 collective-permute-done.23.s3
  112.5 0.9 shard_map.118
  (38 shorter events, 0.2 us)
Async XLA Ops:
  0.6 14.9 %copy-start.1 = (bf16[5120,800]{0,1:T(8,128)(2,1)S(1)}, bf16[5120,800]{0,1:T(8,128)(2,1)}, u32[]{:S(2)}) copy-start(bf16[5120,800]{0,1:T(8,128)(2,1)} %param.10) | copy-start | bytes 24576004
  0.6 1.1 copy-start.9
  2.1 46.3 %copy-start.3 = (f32[32,5120]{1,0:T(8,128)}, f32[32,5120]{1,0:T(8,128)S(1)}, u32[]{:S(2)}) copy-start(f32[32,5120]{1,0:T(8,128)S(1)} %get-tuple-element.45.res_ref) | copy-start | bytes 1966084
  2.1 17.5 %collective-permute-start.2 = (bf16[32,5120]{1,0:T(8,128)(2,1)S(1)}, bf16[32,5120]{1,0:T(8,128)(2,1)S(1)}, u32[]{:S(2)}, u32[]{:S(2)}) collective-permute-start(bf16[32,5120]{1,0:T(8,128)(2,1)S(1)} %get-tuple-element.34.n0), channel_id=1, source_target_pairs={{0,12},{1,13},{16,28},{17,29},{32,44},{33,45},{48,60},{49,61},{4,0... | collective-permute-start | bytes 983048 | tf_op jit(solution)/shard_map/ppermute | solution.py:33
  5.3 14.4 %collective-permute-start.3 = (bf16[32,5120]{1,0:T(8,128)(2,1)S(1)}, bf16[32,5120]{1,0:T(8,128)(2,1)S(1)}, u32[]{:S(2)}, u32[]{:S(2)}) collective-permute-start(bf16[32,5120]{1,0:T(8,128)(2,1)S(1)} %get-tuple-element.34.n0), channel_id=1, source_target_pairs={{0,8},{1,9},{16,24},{17,25},{32,40},{33,41},{48,56},{49,57},{4,12}... | collective-permute-start | bytes 983048 | tf_op jit(solution)/shard_map/ppermute | solution.py:33
  5.9 17.1 %collective-permute-start.5 = (bf16[32,5120]{1,0:T(8,128)(2,1)S(1)}, bf16[32,5120]{1,0:T(8,128)(2,1)S(1)}, u32[]{:S(2)}, u32[]{:S(2)}) collective-permute-start(bf16[32,5120]{1,0:T(8,128)(2,1)S(1)} %get-tuple-element.34.n0), channel_id=1, source_target_pairs={{0,4},{1,5},{16,20},{17,21},{32,36},{33,37},{48,52},{49,53},{4,8},... | collective-permute-start | bytes 983048 | tf_op jit(solution)/shard_map/ppermute | solution.py:33
  6.9 26.9 %collective-permute-start = (bf16[800,5120]{1,0:T(8,128)(2,1)}, bf16[800,5120]{1,0:T(8,128)(2,1)}, u32[]{:S(2)}, u32[]{:S(2)}) collective-permute-start(bf16[800,5120]{1,0:T(8,128)(2,1)} %bitcast.28), channel_id=1, source_target_pairs={{0,1},{1,0},{16,17},{17,16},{32,33},{33,32},{48,49},{49,48},{4,5},... | collective-permute-start | bytes 24576008 | tf_op jit(solution)/shard_map/ppermute | solution.py:33
  6.9 12.8 %collective-permute-start.4 = (bf16[32,1280]{1,0:T(8,128)(2,1)}, bf16[32,1280]{1,0:T(8,128)(2,1)S(1)}, u32[]{:S(2)}, u32[]{:S(2)}) collective-permute-start(bf16[32,1280]{1,0:T(8,128)(2,1)} %param.13), channel_id=1, source_target_pairs={{0,64},{1,65},{16,80},{17,81},{32,96},{33,97},{48,112},{49,113},{4... | collective-permute-start | bytes 245768 | tf_op jit(solution)/shard_map/ppermute | solution.py:33
  16.5 3.2 %copy-start = (bf16[800,5120]{1,0:T(8,128)(2,1)}, bf16[800,5120]{1,0:T(8,128)(2,1)S(1)}, u32[]{:S(2)}) copy-start(bf16[800,5120]{1,0:T(8,128)(2,1)S(1)} %shard_map.105.w_ref) | copy-start | bytes 24576004
  23.1 14.4 %collective-permute-start.7 = (bf16[800,5120]{1,0:T(8,128)(2,1)}, bf16[800,5120]{1,0:T(8,128)(2,1)}, u32[]{:S(2)}, u32[]{:S(2)}) collective-permute-start(bf16[800,5120]{1,0:T(8,128)(2,1)} %f_ref.5), channel_id=1, source_target_pairs={{0,1},{1,0},{16,17},{17,16},{32,33},{33,32},{48,49},{49,48},{4,5},... | collective-permute-start | bytes 24576008 | tf_op jit(solution)/shard_map/ppermute | solution.py:33
  23.2 6.8 %collective-permute-start.9 = (bf16[64,1280]{1,0:T(8,128)(2,1)S(1)}, bf16[64,1280]{1,0:T(8,128)(2,1)S(1)}, u32[]{:S(2)}, u32[]{:S(2)}) collective-permute-start(bf16[64,1280]{1,0:T(8,128)(2,1)S(1)} %constant_dynamic-update-slice_fusion), channel_id=1, source_target_pairs={{0,16},{1,17},{16,0},{17,1},{32,48},{33,49},{48,32},{49,33},{4,20}... | collective-permute-start | bytes 491528 | tf_op jit(solution)/shard_map/ppermute | solution.py:33
  25.2 18.0 %collective-permute-start.8 = (bf16[64,5120]{1,0:T(8,128)(2,1)S(1)}, bf16[64,5120]{1,0:T(8,128)(2,1)S(1)}, u32[]{:S(2)}, u32[]{:S(2)}) collective-permute-start(bf16[64,5120]{1,0:T(8,128)(2,1)S(1)} %get-tuple-element.36.r), channel_id=1, source_target_pairs={{0,2},{1,3},{16,18},{17,19},{32,34},{33,35},{48,50},{49,51},{4,6},... | collective-permute-start | bytes 1966088 | tf_op jit(solution)/shard_map/ppermute | solution.py:33
  26.7 16.5 %collective-permute-start.6 = (bf16[64,5120]{1,0:T(8,128)(2,1)S(1)}, bf16[64,5120]{1,0:T(8,128)(2,1)S(1)}, u32[]{:S(2)}, u32[]{:S(2)}) collective-permute-start(bf16[64,5120]{1,0:T(8,128)(2,1)S(1)} %get-tuple-element.37.l), channel_id=1, source_target_pairs={{0,66},{1,67},{16,82},{17,83},{32,98},{33,99},{48,114},{49,115},{4... | collective-permute-start | bytes 1966088 | tf_op jit(solution)/shard_map/ppermute | solution.py:33
  30.0 18.4 %collective-permute-start.10 = (bf16[128,1280]{1,0:T(8,128)(2,1)S(1)}, bf16[128,1280]{1,0:T(8,128)(2,1)S(1)}, u32[]{:S(2)}, u32[]{:S(2)}) collective-permute-start(bf16[128,1280]{1,0:T(8,128)(2,1)S(1)} %pad_maximum_fusion), channel_id=1, source_target_pairs={{0,32},{1,33},{16,48},{17,49},{32,0},{33,1},{48,16},{49,17},{4,36}... | collective-permute-start | bytes 983048 | tf_op jit(solution)/shard_map/ppermute | solution.py:33
  33.8 9.5 %collective-permute-start.1 = (bf16[800,128]{1,0:T(8,128)(2,1)S(1)}, bf16[800,128]{1,0:T(8,128)(2,1)S(1)}, u32[]{:S(2)}, u32[]{:S(2)}) collective-permute-start(bf16[800,128]{1,0:T(8,128)(2,1)S(1)} %shard_map.104.wm_ref), channel_id=1, source_target_pairs={{0,1},{1,0},{16,17},{17,16},{32,33},{33,32},{48,49},{49,48},{4,5},... | collective-permute-start | bytes 614408 | tf_op jit(solution)/shard_map/ppermute | solution.py:33
  33.9 9.3 %slice-start = ((s8[8192000]{0:T(1024)(128)(4,1)}), s8[4194304]{0:T(1024)(128)(4,1)S(1)}, s32[]{:S(2)}) async-start(s8[8192000]{0:T(1024)(128)(4,1)} %bitcast.26), calls=%async_computation | async-start | bytes 8388608
  37.5 5.8 %slice-start.1 = ((s8[8192000]{0:T(1024)(128)(4,1)}), s8[3997696]{0:T(1024)(128)(4,1)S(1)}, s32[]{:S(2)}) async-start(s8[8192000]{0:T(1024)(128)(4,1)} %bitcast.26), calls=%async_computation.1 | async-start | bytes 7995392
  48.4 4.0 %copy-start.7 = (f32[256,128]{1,0:T(8,128)}, f32[256,128]{1,0:T(8,128)S(1)}, u32[]{:S(2)}) copy-start(f32[256,128]{1,0:T(8,128)S(1)} %get-tuple-element.41.mean_ref) | copy-start | bytes 393220
  48.4 4.0 %copy-start.5 = (bf16[256,1280]{1,0:T(8,128)(2,1)}, bf16[256,1280]{1,0:T(8,128)(2,1)S(1)}, u32[]{:S(2)}) copy-start(bf16[256,1280]{1,0:T(8,128)(2,1)S(1)} %constant_dynamic-update-slice_fusion.2.pooled_ref) | copy-start | bytes 1966084
  52.4 39.0 %collective-permute-start.18 = (bf16[320,1536]{1,0:T(8,128)(2,1)}, bf16[320,1536]{1,0:T(8,128)(2,1)}, u32[]{:S(2)}, u32[]{:S(2)}) collective-permute-start(bf16[320,1536]{1,0:T(8,128)(2,1)} %w_ref), channel_id=1, source_target_pairs={{0,1},{1,0},{16,17},{17,16},{32,33},{33,32},{48,49},{49,48},{4,5},... | collective-permute-start | bytes 2949128 | tf_op jit(solution)/shard_map/ppermute | solution.py:33
  52.4 15.0 %collective-permute-start.13 = (bf16[2,128,640]{2,1,0:T(8,128)(2,1)}, bf16[2,128,640]{2,1,0:T(8,128)(2,1)}, u32[]{:S(2)}, u32[]{:S(2)}) collective-permute-start(bf16[2,128,640]{2,1,0:T(8,128)(2,1)} %get-tuple-element.48), channel_id=1, source_target_pairs={{0,66},{1,67},{16,82},{17,83},{32,98},{33,99},{48,114},{49,115},{4... | collective-permute-start | bytes 983048 | tf_op jit(solution)/shard_map/ppermute | solution.py:33
  55.4 12.1 %collective-permute-start.14 = (bf16[2,128,640]{2,1,0:T(8,128)(2,1)}, bf16[2,128,640]{2,1,0:T(8,128)(2,1)}, u32[]{:S(2)}, u32[]{:S(2)}) collective-permute-start(bf16[2,128,640]{2,1,0:T(8,128)(2,1)} %get-tuple-element.49), channel_id=1, source_target_pairs={{0,2},{1,3},{16,18},{17,19},{32,34},{33,35},{48,50},{49,51},{4,6},... | collective-permute-start | bytes 983048 | tf_op jit(solution)/shard_map/ppermute | solution.py:33
  55.4 14.9 %collective-permute-start.11 = (bf16[2,128,640]{2,1,0:T(8,128)(2,1)}, bf16[2,128,640]{2,1,0:T(8,128)(2,1)}, u32[]{:S(2)}, u32[]{:S(2)}) collective-permute-start(bf16[2,128,640]{2,1,0:T(8,128)(2,1)} %get-tuple-element.46), channel_id=1, source_target_pairs={{0,66},{1,67},{16,82},{17,83},{32,98},{33,99},{48,114},{49,115},{4... | collective-permute-start | bytes 983048 | tf_op jit(solution)/shard_map/ppermute | solution.py:33
  58.7 15.1 %collective-permute-start.12 = (bf16[2,128,640]{2,1,0:T(8,128)(2,1)}, bf16[2,128,640]{2,1,0:T(8,128)(2,1)}, u32[]{:S(2)}, u32[]{:S(2)}) collective-permute-start(bf16[2,128,640]{2,1,0:T(8,128)(2,1)} %get-tuple-element.47), channel_id=1, source_target_pairs={{0,2},{1,3},{16,18},{17,19},{32,34},{33,35},{48,50},{49,51},{4,6},... | collective-permute-start | bytes 983048 | tf_op jit(solution)/shard_map/ppermute | solution.py:33
  58.8 1.1 copy-start.4
  59.9 0.9 copy-start.8
  60.8 16.7 %copy-start.10 = (s32[32]{0:T(128)S(1)}, s32[32]{0:T(128)}, u32[]{:S(2)}) copy-start(s32[32]{0:T(128)} %param.16) | copy-start | bytes 388
  60.8 16.7 %copy-start.11 = (s32[32,1]{0,1:T(1,128)S(1)}, s32[32,1]{0,1:T(1,128)}, u32[]{:S(2)}) copy-start(s32[32,1]{0,1:T(1,128)} %param.15) | copy-start | bytes 388
  69.5 17.5 %collective-permute-start.15 = (bf16[256,640]{1,0:T(8,128)(2,1)}, bf16[256,640]{1,0:T(8,128)(2,1)S(1)}, u32[]{:S(2)}, u32[]{:S(2)}) collective-permute-start(bf16[256,640]{1,0:T(8,128)(2,1)} %get-tuple-element.50), channel_id=1, source_target_pairs={{0,4},{1,5},{16,20},{17,21},{32,36},{33,37},{48,52},{49,53},{4,8},... | collective-permute-start | bytes 983048 | tf_op jit(solution)/shard_map/ppermute | solution.py:33
  75.6 11.4 %collective-permute-start.16 = (bf16[256,640]{1,0:T(8,128)(2,1)}, bf16[256,640]{1,0:T(8,128)(2,1)S(1)}, u32[]{:S(2)}, u32[]{:S(2)}) collective-permute-start(bf16[256,640]{1,0:T(8,128)(2,1)} %shard_map.114), channel_id=1, source_target_pairs={{0,8},{1,9},{16,24},{17,25},{32,40},{33,41},{48,56},{49,57},{4,12}... | collective-permute-start | bytes 983048 | tf_op jit(solution)/shard_map/ppermute | solution.py:33
  76.3 15.1 %collective-permute-start.17 = (bf16[256,640]{1,0:T(8,128)(2,1)}, bf16[256,640]{1,0:T(8,128)(2,1)}, u32[]{:S(2)}, u32[]{:S(2)}) collective-permute-start(bf16[256,640]{1,0:T(8,128)(2,1)} %get-tuple-element.51), channel_id=1, source_target_pairs={{0,12},{1,13},{16,28},{17,29},{32,44},{33,45},{48,60},{49,61},{4,0... | collective-permute-start | bytes 983048 | tf_op jit(solution)/shard_map/ppermute | solution.py:33
  77.6 2.1 %copy-start.2 = (bf16[1280,1536]{1,0:T(8,128)(2,1)S(1)}, bf16[1280,1536]{1,0:T(8,128)(2,1)}, u32[]{:S(2)}) copy-start(bf16[1280,1536]{1,0:T(8,128)(2,1)} %proj_ref.1) | copy-start | bytes 11796484
  79.7 1.1 copy-start.6
  94.1 6.2 %collective-permute-start.19 = (bf16[64,1664]{1,0:T(8,128)(2,1)S(1)}, bf16[64,1664]{1,0:T(8,128)(2,1)S(1)}, u32[]{:S(2)}, u32[]{:S(2)}) collective-permute-start(bf16[64,1664]{1,0:T(8,128)(2,1)S(1)} %get-tuple-element.56), channel_id=1, source_target_pairs={{0,66},{1,67},{16,82},{17,83},{32,98},{33,99},{48,114},{49,115},{4... | collective-permute-start | bytes 638984 | tf_op jit(solution)/shard_map/ppermute | solution.py:33
  95.4 7.1 %collective-permute-start.20 = (bf16[64,1664]{1,0:T(8,128)(2,1)S(1)}, bf16[64,1664]{1,0:T(8,128)(2,1)S(1)}, u32[]{:S(2)}, u32[]{:S(2)}) collective-permute-start(bf16[64,1664]{1,0:T(8,128)(2,1)S(1)} %get-tuple-element.57), channel_id=1, source_target_pairs={{0,2},{1,3},{16,18},{17,19},{32,34},{33,35},{48,50},{49,51},{4,6},... | collective-permute-start | bytes 638984 | tf_op jit(solution)/shard_map/ppermute | solution.py:33
  102.5 7.6 %collective-permute-start.21 = (bf16[32,1664]{1,0:T(8,128)(2,1)S(1)}, bf16[32,1664]{1,0:T(8,128)(2,1)S(1)}, u32[]{:S(2)}, u32[]{:S(2)}) collective-permute-start(bf16[32,1664]{1,0:T(8,128)(2,1)S(1)} %get-tuple-element.59), channel_id=1, source_target_pairs={{0,4},{1,5},{16,20},{17,21},{32,36},{33,37},{48,52},{49,53},{4,8},... | collective-permute-start | bytes 319496 | tf_op jit(solution)/shard_map/ppermute | solution.py:33
  104.3 7.5 %collective-permute-start.22 = (bf16[32,1664]{1,0:T(8,128)(2,1)S(1)}, bf16[32,1664]{1,0:T(8,128)(2,1)S(1)}, u32[]{:S(2)}, u32[]{:S(2)}) collective-permute-start(bf16[32,1664]{1,0:T(8,128)(2,1)S(1)} %get-tuple-element.60), channel_id=1, source_target_pairs={{0,8},{1,9},{16,24},{17,25},{32,40},{33,41},{48,56},{49,57},{4,12}... | collective-permute-start | bytes 319496 | tf_op jit(solution)/shard_map/ppermute | solution.py:33
  107.8 4.7 %collective-permute-start.23 = (bf16[32,1664]{1,0:T(8,128)(2,1)S(1)}, bf16[32,1664]{1,0:T(8,128)(2,1)S(1)}, u32[]{:S(2)}, u32[]{:S(2)}) collective-permute-start(bf16[32,1664]{1,0:T(8,128)(2,1)S(1)} %get-tuple-element.61), channel_id=1, source_target_pairs={{0,12},{1,13},{16,28},{17,29},{32,44},{33,45},{48,60},{49,61},{4,0... | collective-permute-start | bytes 319496 | tf_op jit(solution)/shard_map/ppermute | solution.py:33

commit v5 on v4

--- a/solution.py
+++ b/solution.py
@@ -187,7 +187,12 @@
     return call(away_kernel, (cols,), (h, h_mean, centred, f), outs, limit=8)
 
 
-def own_kernel(cols, h_ref, mean_ref, res_ref, f_ref, o_ref, own_ref, buf, sems):
+def own_kernel(cols, h_ref, mean_in, res_in, f_ref, o_ref, own_ref, buf, mean_ref, res_ref, sems):
+    small = [
+        pltpu.make_async_copy(mean_in, mean_ref, sems.at[8]),
+        pltpu.make_async_copy(res_in, res_ref, sems.at[9]),
+    ]
+    start(small)
     loads = []
     for q in range(4):
         at = pl.ds(pl.multiple_of(cols[q] * BLK, 128), BLK)
@@ -195,6 +200,7 @@
             to = buf.at[pl.ds(800 * k, 800), pl.ds(BLK * q, BLK)]
             loads.append(pltpu.make_async_copy(ref.at[:, at], to, sems.at[2 * q + k]))
     start(loads[:4])
+    wait(small)
     for k in range(2):
         wait(loads[4 * k : 4 * k + 4])
         if k == 0:
@@ -210,8 +216,13 @@
         (cols,),
         (h, h_mean, centred, f, o),
         (struct((4, 256, BLK), f32),),
-        scratch=[pltpu.VMEM((1600, 4 * BLK), bf16), pltpu.SemaphoreType.DMA((8,))],
-        remote=2,
+        scratch=[
+            pltpu.VMEM((1600, 4 * BLK), bf16),
+            pltpu.VMEM(h_mean.shape, f32),
+            pltpu.VMEM(centred.shape, f32),
+            pltpu.SemaphoreType.DMA((10,)),
+        ],
+        remote=4,
         limit=14,
         size=16 * 1024 * 1024,
     )[0]

time: 114 us -> 114 us (level)
  transfers between devices with their start and end apart: 24 -> 24, of which waited for: 13 -> 12; matrix products, arithmetic and copies ran while one was open for 1% -> 1% of each run, Pallas kernels for 27% -> 27%
where the time goes in v5:
time: 114 us; the launch traced here: 113 us
  Pallas kernels  38.9 us (34%)
  starting transfers between devices  31.8 us (28%)
  waiting for transfers between devices  30.1 us (26%)
  local copies, waits for them, and re-layouts  10.6 us (9%)
  between operations  1.57 us (1%)
    pallas_call x15, Pallas kernels, call(): pl.pallas_call(body, in_specs=[SM] * len(scalars) + [VM] * inside + [HB]...  38.9 us
    ppermute x24, starting transfers between devices, shift(): return lax.ppermute(value, AXES, moves(**step))  31.8 us
    ppermute x24, waiting for transfers between devices, shift(): return lax.ppermute(value, AXES, moves(**step))  30.1 us
    unnamed x31, local copies, waits for them, and re-layouts  10.4 us
  transfers between devices with their start and end apart: 24, of which 12 were waited for; matrix products, arithmetic and copies ran while one was open for 1% of the time, Pallas kernels for 27%

profile of v5, /device:TPU:0, one launch (start us, length us, event | category | flops | bytes accessed | tf_op | source)
XLA Modules:
  0.0 113.2 jit_solution(7875739128398606389)
XLA Ops:
  0.6 0.0 copy-start.1
  0.7 1.1 copy-done.9
  1.8 0.3 shard_map.107
  2.1 3.2 %collective-permute-start.2 = (bf16[32,5120]{1,0:T(8,128)(2,1)S(1)}, bf16[32,5120]{1,0:T(8,128)(2,1)S(1)}, u32[]{:S(2)}, u32[]{:S(2)}) collective-permute-start(bf16[32,5120]{1,0:T(8,128)(2,1)S(1)} %get-tuple-element.34.n0), channel_id=1, source_target_pairs={{0,12},{1,13},{16,28},{17,29},{32,44},{33,45},{48,60},{49,61},{4,0... | collective-permute-start | bytes 983048 | tf_op jit(solution)/shard_map/ppermute | solution.py:33
  5.3 0.6 collective-permute-start.3
  5.9 1.0 collective-permute-start.5
  6.9 0.0 collective-permute-start
  6.9 3.0 %collective-permute-start.4 = (bf16[32,1280]{1,0:T(8,128)(2,1)}, bf16[32,1280]{1,0:T(8,128)(2,1)S(1)}, u32[]{:S(2)}, u32[]{:S(2)}) collective-permute-start(bf16[32,1280]{1,0:T(8,128)(2,1)} %param.13), channel_id=1, source_target_pairs={{0,64},{1,65},{16,80},{17,81},{32,96},{33,97},{48,112},{49,113},{4... | collective-permute-start | bytes 245768 | tf_op jit(solution)/shard_map/ppermute | solution.py:33
  9.9 0.9 constant_dynamic-update-slice_fusion.1
  10.8 4.7 %shard_map.104.wm_ref = bf16[800,128]{1,0:T(8,128)(2,1)S(1)} custom-call(bf16[800,5120]{1,0:T(8,128)(2,1)} %f_ref.5), custom_call_target="tpu_custom_call" | custom-call | flops 1024 | bytes 16777216 | tf_op jit(solution)/shard_map/pallas_call | solution.py:53
  15.5 1.0 shard_map.105.w_ref
  16.5 3.1 %copy-done = bf16[800,5120]{1,0:T(8,128)(2,1)} copy-done((bf16[800,5120]{1,0:T(8,128)(2,1)}, bf16[800,5120]{1,0:T(8,128)(2,1)S(1)}, u32[]{:S(2)}) %copy-start) | copy-done | bytes 8192024
  19.7 0.0 collective-permute-done.3.n2
  19.7 3.3 %collective-permute-done.5.n3 = bf16[32,5120]{1,0:T(8,128)(2,1)S(1)} collective-permute-done((bf16[32,5120]{1,0:T(8,128)(2,1)S(1)}, bf16[32,5120]{1,0:T(8,128)(2,1)S(1)}, u32[]{:S(2)}, u32[]{:S(2)}) %collective-permute-start.5) | collective-permute-done | bytes 327712 | tf_op jit(solution)/shard_map/ppermute | solution.py:33
  23.0 0.1 shard_map.108
  23.1 0.1 collective-permute-start.7
  23.2 2.0 %collective-permute-start.9 = (bf16[64,1280]{1,0:T(8,128)(2,1)S(1)}, bf16[64,1280]{1,0:T(8,128)(2,1)S(1)}, u32[]{:S(2)}, u32[]{:S(2)}) collective-permute-start(bf16[64,1280]{1,0:T(8,128)(2,1)S(1)} %constant_dynamic-update-slice_fusion), channel_id=1, source_target_pairs={{0,16},{1,17},{16,0},{17,1},{32,48},{33,49},{48,32},{49,33},{4,20}... | collective-permute-start | bytes 491528 | tf_op jit(solution)/shard_map/ppermute | solution.py:33
  25.2 0.1 pad_add_fusion.1.cols
  25.2 1.5 %collective-permute-start.8 = (bf16[64,5120]{1,0:T(8,128)(2,1)S(1)}, bf16[64,5120]{1,0:T(8,128)(2,1)S(1)}, u32[]{:S(2)}, u32[]{:S(2)}) collective-permute-start(bf16[64,5120]{1,0:T(8,128)(2,1)S(1)} %get-tuple-element.36.r), channel_id=1, source_target_pairs={{0,2},{1,3},{16,18},{17,19},{32,34},{33,35},{48,50},{49,51},{4,6},... | collective-permute-start | bytes 1966088 | tf_op jit(solution)/shard_map/ppermute | solution.py:33
  26.7 1.7 %collective-permute-start.6 = (bf16[64,5120]{1,0:T(8,128)(2,1)S(1)}, bf16[64,5120]{1,0:T(8,128)(2,1)S(1)}, u32[]{:S(2)}, u32[]{:S(2)}) collective-permute-start(bf16[64,5120]{1,0:T(8,128)(2,1)S(1)} %get-tuple-element.37.l), channel_id=1, source_target_pairs={{0,66},{1,67},{16,82},{17,83},{32,98},{33,99},{48,114},{49,115},{4... | collective-permute-start | bytes 1966088 | tf_op jit(solution)/shard_map/ppermute | solution.py:33
  28.5 1.5 %collective-permute-done.9 = bf16[64,1280]{1,0:T(8,128)(2,1)S(1)} collective-permute-done((bf16[64,1280]{1,0:T(8,128)(2,1)S(1)}, bf16[64,1280]{1,0:T(8,128)(2,1)S(1)}, u32[]{:S(2)}, u32[]{:S(2)}) %collective-permute-start.9) | collective-permute-done | bytes 163872 | tf_op jit(solution)/shard_map/ppermute | solution.py:33
  30.0 3.8 %collective-permute-start.10 = (bf16[128,1280]{1,0:T(8,128)(2,1)S(1)}, bf16[128,1280]{1,0:T(8,128)(2,1)S(1)}, u32[]{:S(2)}, u32[]{:S(2)}) collective-permute-start(bf16[128,1280]{1,0:T(8,128)(2,1)S(1)} %pad_maximum_fusion), channel_id=1, source_target_pairs={{0,32},{1,33},{16,48},{17,49},{32,0},{33,1},{48,16},{49,17},{4,36}... | collective-permute-start | bytes 983048 | tf_op jit(solution)/shard_map/ppermute | solution.py:33
  33.8 0.0 collective-permute-done.w_ref
  33.8 0.1 collective-permute-start.1
  33.9 0.0 slice-start
  33.9 3.6 %shard_map.106.v_ref = bf16[800,5120]{1,0:T(8,128)(2,1)S(1)} custom-call(bf16[800,5120]{1,0:T(8,128)(2,1)} %collective-permute-done.w_ref), custom_call_target="tpu_custom_call" | custom-call | flops 1024 | bytes 16777216 | tf_op jit(solution)/shard_map/pallas_call | solution.py:53
  37.5 0.0 slice-start.1
  37.5 4.3 %shard_map.109.f_ref = bf16[1600,2560]{1,0:T(8,128)(2,1)S(1)} custom-call(s32[4]{0:T(128)S(1)} %pad_add_fusion.1.cols, bf16[800,5120]{1,0:T(8,128)(2,1)} %f_ref.5, bf16[800,5120]{1,0:T(8,128)(2,1)} %collective-permute-done.7.o_ref), custom_call_target="tpu_custom_call" | custom-call | flops 1024 | bytes 16777216 | tf_op jit(solution)/shard_map/pallas_call | solution.py:53
  41.8 1.4 %collective-permute-done.6.b = bf16[64,5120]{1,0:T(8,128)(2,1)S(1)} collective-permute-done((bf16[64,5120]{1,0:T(8,128)(2,1)S(1)}, bf16[64,5120]{1,0:T(8,128)(2,1)S(1)}, u32[]{:S(2)}, u32[]{:S(2)}) %collective-permute-start.6) | collective-permute-done | bytes 655392 | tf_op jit(solution)/shard_map/ppermute | solution.py:33
  43.2 0.0 collective-permute-done.1.vm_ref
  43.3 5.1 %shard_map.110 = (bf16[1600,256]{1,0:T(8,128)(2,1)S(1)}, f32[256,128]{1,0:T(8,128)S(1)}) custom-call(bf16[800,5120]{1,0:T(8,128)(2,1)S(1)} %bitcast.27, bf16[800,5120]{1,0:T(8,128)(2,1)S(1)} %shard_map.106.v_ref, bf16[800,128]{1,0:T(8,128)(2,1)S(1)} %shard_map.104.wm_ref, bf16[800,128]{1,0:T(8,128)(2,1)S(1)} %collective-permute-done.1.vm_ref, ...), custom_call_target="tpu_custom_call" | custom-call | flops 1024 | bytes 1024 | tf_op jit(solution)/shard_map/pallas_call | solution.py:53
  48.4 4.0 %shard_map.112 = (bf16[2,128,640]{2,1,0:T(8,128)(2,1)}, bf16[2,128,640]{2,1,0:T(8,128)(2,1)}, bf16[2,128,640]{2,1,0:T(8,128)(2,1)}, bf16[2,128,640]{2,1,0:T(8,128)(2,1)}) custom-call(s32[4]{0:T(128)S(1)} %pad_add_fusion.1.cols, bf16[1600,256]{1,0:T(8,128)(2,1)S(1)} %get-tuple-element.40.h_ref, f32[256,128]{1,0:T(8,128)S(1)} %get-tuple-element.41.mean_in.mean_ref, ...), custom_call_target="tpu_custom_call" | custom-call | flops 1024 | bytes 1024 | tf_op jit(solution)/shard_map/pallas_call | solution.py:53
  52.4 0.0 collective-permute-start.18
  52.4 3.0 %collective-permute-start.13 = (bf16[2,128,640]{2,1,0:T(8,128)(2,1)}, bf16[2,128,640]{2,1,0:T(8,128)(2,1)}, u32[]{:S(2)}, u32[]{:S(2)}) collective-permute-start(bf16[2,128,640]{2,1,0:T(8,128)(2,1)} %get-tuple-element.48), channel_id=1, source_target_pairs={{0,66},{1,67},{16,82},{17,83},{32,98},{33,99},{48,114},{49,115},{4... | collective-permute-start | bytes 983048 | tf_op jit(solution)/shard_map/ppermute | solution.py:33
  55.4 0.0 collective-permute-start.14
  55.4 3.2 %collective-permute-start.11 = (bf16[2,128,640]{2,1,0:T(8,128)(2,1)}, bf16[2,128,640]{2,1,0:T(8,128)(2,1)}, u32[]{:S(2)}, u32[]{:S(2)}) collective-permute-start(bf16[2,128,640]{2,1,0:T(8,128)(2,1)} %get-tuple-element.46), channel_id=1, source_target_pairs={{0,66},{1,67},{16,82},{17,83},{32,98},{33,99},{48,114},{49,115},{4... | collective-permute-start | bytes 983048 | tf_op jit(solution)/shard_map/ppermute | solution.py:33
  58.7 0.1 pad_add_fusion.cols
  58.8 1.1 copy-done.4
  59.9 0.9 copy-done.8
  60.8 7.0 %shard_map.111.own_ref = f32[4,256,640]{2,1,0:T(8,128)S(1)} custom-call(s32[4]{0:T(128)S(1)} %pad_add_fusion.cols, bf16[1600,256]{1,0:T(8,128)(2,1)S(1)} %get-tuple-element.40.h_ref, f32[256,128]{1,0:T(8,128)S(1)} %copy-done.8, f32[32,5120]{1,0:T(8,128)S(1)} %copy-done.4, bf16[800,5120]{1,0:T(8,128)(2,1)} %f_ref.5, ...), custom_call_target="tpu_custom_call" | custom-call | flops 1024 | bytes 16777216 | tf_op jit(solution)/shard_map/pallas_call | solution.py:53
  67.8 2.0 %shard_map.113 = (bf16[256,640]{1,0:T(8,128)(2,1)}, bf16[256,640]{1,0:T(8,128)(2,1)}) custom-call(f32[4,256,640]{2,1,0:T(8,128)S(1)} %shard_map.111.own_ref, bf16[2,128,640]{2,1,0:T(8,128)(2,1)} %collective-permute-done.13.up_ref, bf16[2,128,640]{2,1,0:T(8,128)(2,1)} %collective-permute-done.14.low_ref), custom_call_target="tpu_custom_call" | custom-call | flops 1024 | bytes 1024 | tf_op jit(solution)/shard_map/pallas_call | solution.py:53
  69.8 0.6 collective-permute-done.11.up_ref
  70.4 3.4 %collective-permute-done.12.low_ref = bf16[2,128,640]{2,1,0:T(8,128)(2,1)} collective-permute-done((bf16[2,128,640]{2,1,0:T(8,128)(2,1)}, bf16[2,128,640]{2,1,0:T(8,128)(2,1)}, u32[]{:S(2)}, u32[]{:S(2)}) %collective-permute-start.12) | collective-permute-done | bytes 327712 | tf_op jit(solution)/shard_map/ppermute | solution.py:33
  73.8 1.9 %shard_map.114 = bf16[256,640]{1,0:T(8,128)(2,1)} custom-call(f32[4,256,640]{2,1,0:T(8,128)S(1)} %shard_map.111.own_ref, bf16[2,128,640]{2,1,0:T(8,128)(2,1)} %collective-permute-done.11.up_ref, bf16[2,128,640]{2,1,0:T(8,128)(2,1)} %collective-permute-done.12.low_ref), custom_call_target="tpu_custom_call" | custom-call | flops 1024 | bytes 1024 | tf_op jit(solution)/shard_map/pallas_call | solution.py:53
  75.6 0.6 collective-permute-start.16
  76.3 1.2 %collective-permute-start.17 = (bf16[256,640]{1,0:T(8,128)(2,1)}, bf16[256,640]{1,0:T(8,128)(2,1)}, u32[]{:S(2)}, u32[]{:S(2)}) collective-permute-start(bf16[256,640]{1,0:T(8,128)(2,1)} %get-tuple-element.51), channel_id=1, source_target_pairs={{0,12},{1,13},{16,28},{17,29},{32,44},{33,45},{48,60},{49,61},{4,0... | collective-permute-start | bytes 983048 | tf_op jit(solution)/shard_map/ppermute | solution.py:33
  77.5 0.1 copy.11.index_ref
  77.6 2.1 %copy-done.2 = bf16[1280,1536]{1,0:T(8,128)(2,1)S(1)} copy-done((bf16[1280,1536]{1,0:T(8,128)(2,1)S(1)}, bf16[1280,1536]{1,0:T(8,128)(2,1)}, u32[]{:S(2)}) %copy-start.2) | copy-done | bytes 3932184
  79.7 1.1 copy-done.6
  80.8 1.3 %shard_map.115.text_ref = f32[32,1536]{1,0:T(8,128)S(1)} custom-call(s32[32,1]{1,0:T(8,128)S(1)} %copy.11.index_ref, bf16[256,1280]{1,0:T(8,128)(2,1)S(1)} %copy-done.6, bf16[1280,1536]{1,0:T(8,128)(2,1)S(1)} %copy-done.2), custom_call_target="tpu_custom_call" | custom-call | flops 1024 | bytes 1024 | tf_op jit(solution)/shard_map/pallas_call | solution.py:53
  82.1 5.3 %collective-permute-done.15.t1 = bf16[256,640]{1,0:T(8,128)(2,1)S(1)} collective-permute-done((bf16[256,640]{1,0:T(8,128)(2,1)}, bf16[256,640]{1,0:T(8,128)(2,1)S(1)}, u32[]{:S(2)}, u32[]{:S(2)}) %collective-permute-start.15) | collective-permute-done | bytes 327712 | tf_op jit(solution)/shard_map/ppermute | solution.py:33
  87.4 4.0 %collective-permute-done.17.t3 = bf16[256,640]{1,0:T(8,128)(2,1)} collective-permute-done((bf16[256,640]{1,0:T(8,128)(2,1)}, bf16[256,640]{1,0:T(8,128)(2,1)}, u32[]{:S(2)}, u32[]{:S(2)}) %collective-permute-start.17) | collective-permute-done | bytes 327712 | tf_op jit(solution)/shard_map/ppermute | solution.py:33
  91.4 2.7 %shard_map.116 = (bf16[4,32,1664]{2,1,0:T(8,128)(2,1)S(1)}, bf16[64,1664]{1,0:T(8,128)(2,1)S(1)}, bf16[64,1664]{1,0:T(8,128)(2,1)S(1)}) custom-call(s32[1]{0:T(128)} %bitcast.core, f32[4,256,640]{2,1,0:T(8,128)S(1)} %shard_map.111.own_ref, bf16[2,128,640]{2,1,0:T(8,128)(2,1)} %collective-permute-done.11.up_ref, ...), custom_call_target="tpu_custom_call" | custom-call | flops 1024 | bytes 1024 | tf_op jit(solution)/shard_map/pallas_call | solution.py:53
  94.1 1.6 %collective-permute-start.19 = (bf16[64,1664]{1,0:T(8,128)(2,1)S(1)}, bf16[64,1664]{1,0:T(8,128)(2,1)S(1)}, u32[]{:S(2)}, u32[]{:S(2)}) collective-permute-start(bf16[64,1664]{1,0:T(8,128)(2,1)S(1)} %get-tuple-element.56), channel_id=1, source_target_pairs={{0,66},{1,67},{16,82},{17,83},{32,98},{33,99},{48,114},{49,115},{4... | collective-permute-start | bytes 638984 | tf_op jit(solution)/shard_map/ppermute | solution.py:33
  95.8 0.5 collective-permute-start.20
  96.2 4.1 %collective-permute-done.19.r_ref = bf16[64,1664]{1,0:T(8,128)(2,1)S(1)} collective-permute-done((bf16[64,1664]{1,0:T(8,128)(2,1)S(1)}, bf16[64,1664]{1,0:T(8,128)(2,1)S(1)}, u32[]{:S(2)}, u32[]{:S(2)}) %collective-permute-start.19) | collective-permute-done | bytes 213024 | tf_op jit(solution)/shard_map/ppermute | solution.py:33
  100.3 2.5 %collective-permute-done.20.l_ref = bf16[64,1664]{1,0:T(8,128)(2,1)S(1)} collective-permute-done((bf16[64,1664]{1,0:T(8,128)(2,1)S(1)}, bf16[64,1664]{1,0:T(8,128)(2,1)S(1)}, u32[]{:S(2)}, u32[]{:S(2)}) %collective-permute-start.20) | collective-permute-done | bytes 213024 | tf_op jit(solution)/shard_map/ppermute | solution.py:33
  102.8 0.1 shard_map.117
  102.9 1.4 %collective-permute-start.21 = (bf16[32,1664]{1,0:T(8,128)(2,1)S(1)}, bf16[32,1664]{1,0:T(8,128)(2,1)S(1)}, u32[]{:S(2)}, u32[]{:S(2)}) collective-permute-start(bf16[32,1664]{1,0:T(8,128)(2,1)S(1)} %get-tuple-element.59), channel_id=1, source_target_pairs={{0,4},{1,5},{16,20},{17,21},{32,36},{33,37},{48,52},{49,53},{4,8},... | collective-permute-start | bytes 319496 | tf_op jit(solution)/shard_map/ppermute | solution.py:33
  104.3 3.2 %collective-permute-start.22 = (bf16[32,1664]{1,0:T(8,128)(2,1)S(1)}, bf16[32,1664]{1,0:T(8,128)(2,1)S(1)}, u32[]{:S(2)}, u32[]{:S(2)}) collective-permute-start(bf16[32,1664]{1,0:T(8,128)(2,1)S(1)} %get-tuple-element.60), channel_id=1, source_target_pairs={{0,8},{1,9},{16,24},{17,25},{32,40},{33,41},{48,56},{49,57},{4,12}... | collective-permute-start | bytes 319496 | tf_op jit(solution)/shard_map/ppermute | solution.py:33
  108.2 1.8 %collective-permute-done.21.s1 = bf16[32,1664]{1,0:T(8,128)(2,1)S(1)} collective-permute-done((bf16[32,1664]{1,0:T(8,128)(2,1)S(1)}, bf16[32,1664]{1,0:T(8,128)(2,1)S(1)}, u32[]{:S(2)}, u32[]{:S(2)}) %collective-permute-start.21) | collective-permute-done | bytes 106528 | tf_op jit(solution)/shard_map/ppermute | solution.py:33
  110.0 1.4 %collective-permute-done.22.s2 = bf16[32,1664]{1,0:T(8,128)(2,1)S(1)} collective-permute-done((bf16[32,1664]{1,0:T(8,128)(2,1)S(1)}, bf16[32,1664]{1,0:T(8,128)(2,1)S(1)}, u32[]{:S(2)}, u32[]{:S(2)}) %collective-permute-start.22) | collective-permute-done | bytes 106528 | tf_op jit(solution)/shard_map/ppermute | solution.py:33
  111.3 0.9 collective-permute-done.23.s3
  112.2 0.9 shard_map.118
  (38 shorter events, 0.2 us)
Async XLA Ops:
  0.6 14.9 %copy-start.1 = (bf16[5120,800]{0,1:T(8,128)(2,1)S(1)}, bf16[5120,800]{0,1:T(8,128)(2,1)}, u32[]{:S(2)}) copy-start(bf16[5120,800]{0,1:T(8,128)(2,1)} %param.10) | copy-start | bytes 24576004
  0.6 1.1 copy-start.9
  2.1 46.3 %copy-start.3 = (f32[32,5120]{1,0:T(8,128)}, f32[32,5120]{1,0:T(8,128)S(1)}, u32[]{:S(2)}) copy-start(f32[32,5120]{1,0:T(8,128)S(1)} %get-tuple-element.45.res_in.res_ref) | copy-start | bytes 1966084
  2.1 17.5 %collective-permute-start.2 = (bf16[32,5120]{1,0:T(8,128)(2,1)S(1)}, bf16[32,5120]{1,0:T(8,128)(2,1)S(1)}, u32[]{:S(2)}, u32[]{:S(2)}) collective-permute-start(bf16[32,5120]{1,0:T(8,128)(2,1)S(1)} %get-tuple-element.34.n0), channel_id=1, source_target_pairs={{0,12},{1,13},{16,28},{17,29},{32,44},{33,45},{48,60},{49,61},{4,0... | collective-permute-start | bytes 983048 | tf_op jit(solution)/shard_map/ppermute | solution.py:33
  5.3 14.4 %collective-permute-start.3 = (bf16[32,5120]{1,0:T(8,128)(2,1)S(1)}, bf16[32,5120]{1,0:T(8,128)(2,1)S(1)}, u32[]{:S(2)}, u32[]{:S(2)}) collective-permute-start(bf16[32,5120]{1,0:T(8,128)(2,1)S(1)} %get-tuple-element.34.n0), channel_id=1, source_target_pairs={{0,8},{1,9},{16,24},{17,25},{32,40},{33,41},{48,56},{49,57},{4,12}... | collective-permute-start | bytes 983048 | tf_op jit(solution)/shard_map/ppermute | solution.py:33
  5.9 17.1 %collective-permute-start.5 = (bf16[32,5120]{1,0:T(8,128)(2,1)S(1)}, bf16[32,5120]{1,0:T(8,128)(2,1)S(1)}, u32[]{:S(2)}, u32[]{:S(2)}) collective-permute-start(bf16[32,5120]{1,0:T(8,128)(2,1)S(1)} %get-tuple-element.34.n0), channel_id=1, source_target_pairs={{0,4},{1,5},{16,20},{17,21},{32,36},{33,37},{48,52},{49,53},{4,8},... | collective-permute-start | bytes 983048 | tf_op jit(solution)/shard_map/ppermute | solution.py:33
  6.9 26.9 %collective-permute-start = (bf16[800,5120]{1,0:T(8,128)(2,1)}, bf16[800,5120]{1,0:T(8,128)(2,1)}, u32[]{:S(2)}, u32[]{:S(2)}) collective-permute-start(bf16[800,5120]{1,0:T(8,128)(2,1)} %bitcast.28), channel_id=1, source_target_pairs={{0,1},{1,0},{16,17},{17,16},{32,33},{33,32},{48,49},{49,48},{4,5},... | collective-permute-start | bytes 24576008 | tf_op jit(solution)/shard_map/ppermute | solution.py:33
  6.9 12.8 %collective-permute-start.4 = (bf16[32,1280]{1,0:T(8,128)(2,1)}, bf16[32,1280]{1,0:T(8,128)(2,1)S(1)}, u32[]{:S(2)}, u32[]{:S(2)}) collective-permute-start(bf16[32,1280]{1,0:T(8,128)(2,1)} %param.13), channel_id=1, source_target_pairs={{0,64},{1,65},{16,80},{17,81},{32,96},{33,97},{48,112},{49,113},{4... | collective-permute-start | bytes 245768 | tf_op jit(solution)/shard_map/ppermute | solution.py:33
  16.5 3.2 %copy-start = (bf16[800,5120]{1,0:T(8,128)(2,1)}, bf16[800,5120]{1,0:T(8,128)(2,1)S(1)}, u32[]{:S(2)}) copy-start(bf16[800,5120]{1,0:T(8,128)(2,1)S(1)} %shard_map.105.w_ref) | copy-start | bytes 24576004
  23.1 14.4 %collective-permute-start.7 = (bf16[800,5120]{1,0:T(8,128)(2,1)}, bf16[800,5120]{1,0:T(8,128)(2,1)}, u32[]{:S(2)}, u32[]{:S(2)}) collective-permute-start(bf16[800,5120]{1,0:T(8,128)(2,1)} %f_ref.5), channel_id=1, source_target_pairs={{0,1},{1,0},{16,17},{17,16},{32,33},{33,32},{48,49},{49,48},{4,5},... | collective-permute-start | bytes 24576008 | tf_op jit(solution)/shard_map/ppermute | solution.py:33
  23.2 6.8 %collective-permute-start.9 = (bf16[64,1280]{1,0:T(8,128)(2,1)S(1)}, bf16[64,1280]{1,0:T(8,128)(2,1)S(1)}, u32[]{:S(2)}, u32[]{:S(2)}) collective-permute-start(bf16[64,1280]{1,0:T(8,128)(2,1)S(1)} %constant_dynamic-update-slice_fusion), channel_id=1, source_target_pairs={{0,16},{1,17},{16,0},{17,1},{32,48},{33,49},{48,32},{49,33},{4,20}... | collective-permute-start | bytes 491528 | tf_op jit(solution)/shard_map/ppermute | solution.py:33
  25.2 18.0 %collective-permute-start.8 = (bf16[64,5120]{1,0:T(8,128)(2,1)S(1)}, bf16[64,5120]{1,0:T(8,128)(2,1)S(1)}, u32[]{:S(2)}, u32[]{:S(2)}) collective-permute-start(bf16[64,5120]{1,0:T(8,128)(2,1)S(1)} %get-tuple-element.36.r), channel_id=1, source_target_pairs={{0,2},{1,3},{16,18},{17,19},{32,34},{33,35},{48,50},{49,51},{4,6},... | collective-permute-start | bytes 1966088 | tf_op jit(solution)/shard_map/ppermute | solution.py:33
  26.7 16.5 %collective-permute-start.6 = (bf16[64,5120]{1,0:T(8,128)(2,1)S(1)}, bf16[64,5120]{1,0:T(8,128)(2,1)S(1)}, u32[]{:S(2)}, u32[]{:S(2)}) collective-permute-start(bf16[64,5120]{1,0:T(8,128)(2,1)S(1)} %get-tuple-element.37.l), channel_id=1, source_target_pairs={{0,66},{1,67},{16,82},{17,83},{32,98},{33,99},{48,114},{49,115},{4... | collective-permute-start | bytes 1966088 | tf_op jit(solution)/shard_map/ppermute | solution.py:33
  30.0 18.4 %collective-permute-start.10 = (bf16[128,1280]{1,0:T(8,128)(2,1)S(1)}, bf16[128,1280]{1,0:T(8,128)(2,1)S(1)}, u32[]{:S(2)}, u32[]{:S(2)}) collective-permute-start(bf16[128,1280]{1,0:T(8,128)(2,1)S(1)} %pad_maximum_fusion), channel_id=1, source_target_pairs={{0,32},{1,33},{16,48},{17,49},{32,0},{33,1},{48,16},{49,17},{4,36}... | collective-permute-start | bytes 983048 | tf_op jit(solution)/shard_map/ppermute | solution.py:33
  33.8 9.5 %collective-permute-start.1 = (bf16[800,128]{1,0:T(8,128)(2,1)S(1)}, bf16[800,128]{1,0:T(8,128)(2,1)S(1)}, u32[]{:S(2)}, u32[]{:S(2)}) collective-permute-start(bf16[800,128]{1,0:T(8,128)(2,1)S(1)} %shard_map.104.wm_ref), channel_id=1, source_target_pairs={{0,1},{1,0},{16,17},{17,16},{32,33},{33,32},{48,49},{49,48},{4,5},... | collective-permute-start | bytes 614408 | tf_op jit(solution)/shard_map/ppermute | solution.py:33
  33.9 9.3 %slice-start = ((s8[8192000]{0:T(1024)(128)(4,1)}), s8[4194304]{0:T(1024)(128)(4,1)S(1)}, s32[]{:S(2)}) async-start(s8[8192000]{0:T(1024)(128)(4,1)} %bitcast.26), calls=%async_computation | async-start | bytes 8388608
  37.5 5.8 %slice-start.1 = ((s8[8192000]{0:T(1024)(128)(4,1)}), s8[3997696]{0:T(1024)(128)(4,1)S(1)}, s32[]{:S(2)}) async-start(s8[8192000]{0:T(1024)(128)(4,1)} %bitcast.26), calls=%async_computation.1 | async-start | bytes 7995392
  48.4 4.0 %copy-start.7 = (f32[256,128]{1,0:T(8,128)}, f32[256,128]{1,0:T(8,128)S(1)}, u32[]{:S(2)}) copy-start(f32[256,128]{1,0:T(8,128)S(1)} %get-tuple-element.41.mean_in.mean_ref) | copy-start | bytes 393220
  48.4 4.0 %copy-start.5 = (bf16[256,1280]{1,0:T(8,128)(2,1)}, bf16[256,1280]{1,0:T(8,128)(2,1)S(1)}, u32[]{:S(2)}) copy-start(bf16[256,1280]{1,0:T(8,128)(2,1)S(1)} %constant_dynamic-update-slice_fusion.2.pooled_ref) | copy-start | bytes 1966084
  52.4 39.0 %collective-permute-start.18 = (bf16[320,1536]{1,0:T(8,128)(2,1)}, bf16[320,1536]{1,0:T(8,128)(2,1)}, u32[]{:S(2)}, u32[]{:S(2)}) collective-permute-start(bf16[320,1536]{1,0:T(8,128)(2,1)} %w_ref), channel_id=1, source_target_pairs={{0,1},{1,0},{16,17},{17,16},{32,33},{33,32},{48,49},{49,48},{4,5},... | collective-permute-start | bytes 2949128 | tf_op jit(solution)/shard_map/ppermute | solution.py:33
  52.4 15.3 %collective-permute-start.13 = (bf16[2,128,640]{2,1,0:T(8,128)(2,1)}, bf16[2,128,640]{2,1,0:T(8,128)(2,1)}, u32[]{:S(2)}, u32[]{:S(2)}) collective-permute-start(bf16[2,128,640]{2,1,0:T(8,128)(2,1)} %get-tuple-element.48), channel_id=1, source_target_pairs={{0,66},{1,67},{16,82},{17,83},{32,98},{33,99},{48,114},{49,115},{4... | collective-permute-start | bytes 983048 | tf_op jit(solution)/shard_map/ppermute | solution.py:33
  55.4 12.3 %collective-permute-start.14 = (bf16[2,128,640]{2,1,0:T(8,128)(2,1)}, bf16[2,128,640]{2,1,0:T(8,128)(2,1)}, u32[]{:S(2)}, u32[]{:S(2)}) collective-permute-start(bf16[2,128,640]{2,1,0:T(8,128)(2,1)} %get-tuple-element.49), channel_id=1, source_target_pairs={{0,2},{1,3},{16,18},{17,19},{32,34},{33,35},{48,50},{49,51},{4,6},... | collective-permute-start | bytes 983048 | tf_op jit(solution)/shard_map/ppermute | solution.py:33
  55.4 14.9 %collective-permute-start.11 = (bf16[2,128,640]{2,1,0:T(8,128)(2,1)}, bf16[2,128,640]{2,1,0:T(8,128)(2,1)}, u32[]{:S(2)}, u32[]{:S(2)}) collective-permute-start(bf16[2,128,640]{2,1,0:T(8,128)(2,1)} %get-tuple-element.46), channel_id=1, source_target_pairs={{0,66},{1,67},{16,82},{17,83},{32,98},{33,99},{48,114},{49,115},{4... | collective-permute-start | bytes 983048 | tf_op jit(solution)/shard_map/ppermute | solution.py:33
  58.7 15.1 %collective-permute-start.12 = (bf16[2,128,640]{2,1,0:T(8,128)(2,1)}, bf16[2,128,640]{2,1,0:T(8,128)(2,1)}, u32[]{:S(2)}, u32[]{:S(2)}) collective-permute-start(bf16[2,128,640]{2,1,0:T(8,128)(2,1)} %get-tuple-element.47), channel_id=1, source_target_pairs={{0,2},{1,3},{16,18},{17,19},{32,34},{33,35},{48,50},{49,51},{4,6},... | collective-permute-start | bytes 983048 | tf_op jit(solution)/shard_map/ppermute | solution.py:33
  58.8 1.1 copy-start.4
  59.9 0.9 copy-start.8
  60.8 16.7 %copy-start.10 = (s32[32]{0:T(128)S(1)}, s32[32]{0:T(128)}, u32[]{:S(2)}) copy-start(s32[32]{0:T(128)} %param.16) | copy-start | bytes 388
  60.8 16.7 %copy-start.11 = (s32[32,1]{0,1:T(1,128)S(1)}, s32[32,1]{0,1:T(1,128)}, u32[]{:S(2)}) copy-start(s32[32,1]{0,1:T(1,128)} %param.15) | copy-start | bytes 388
  69.8 17.7 %collective-permute-start.15 = (bf16[256,640]{1,0:T(8,128)(2,1)}, bf16[256,640]{1,0:T(8,128)(2,1)S(1)}, u32[]{:S(2)}, u32[]{:S(2)}) collective-permute-start(bf16[256,640]{1,0:T(8,128)(2,1)} %get-tuple-element.50), channel_id=1, source_target_pairs={{0,4},{1,5},{16,20},{17,21},{32,36},{33,37},{48,52},{49,53},{4,8},... | collective-permute-start | bytes 983048 | tf_op jit(solution)/shard_map/ppermute | solution.py:33
  75.6 11.8 %collective-permute-start.16 = (bf16[256,640]{1,0:T(8,128)(2,1)}, bf16[256,640]{1,0:T(8,128)(2,1)S(1)}, u32[]{:S(2)}, u32[]{:S(2)}) collective-permute-start(bf16[256,640]{1,0:T(8,128)(2,1)} %shard_map.114), channel_id=1, source_target_pairs={{0,8},{1,9},{16,24},{17,25},{32,40},{33,41},{48,56},{49,57},{4,12}... | collective-permute-start | bytes 983048 | tf_op jit(solution)/shard_map/ppermute | solution.py:33
  76.3 15.1 %collective-permute-start.17 = (bf16[256,640]{1,0:T(8,128)(2,1)}, bf16[256,640]{1,0:T(8,128)(2,1)}, u32[]{:S(2)}, u32[]{:S(2)}) collective-permute-start(bf16[256,640]{1,0:T(8,128)(2,1)} %get-tuple-element.51), channel_id=1, source_target_pairs={{0,12},{1,13},{16,28},{17,29},{32,44},{33,45},{48,60},{49,61},{4,0... | collective-permute-start | bytes 983048 | tf_op jit(solution)/shard_map/ppermute | solution.py:33
  77.6 2.1 %copy-start.2 = (bf16[1280,1536]{1,0:T(8,128)(2,1)S(1)}, bf16[1280,1536]{1,0:T(8,128)(2,1)}, u32[]{:S(2)}) copy-start(bf16[1280,1536]{1,0:T(8,128)(2,1)} %proj_ref.1) | copy-start | bytes 11796484
  79.7 1.1 copy-start.6
  94.1 6.2 %collective-permute-start.19 = (bf16[64,1664]{1,0:T(8,128)(2,1)S(1)}, bf16[64,1664]{1,0:T(8,128)(2,1)S(1)}, u32[]{:S(2)}, u32[]{:S(2)}) collective-permute-start(bf16[64,1664]{1,0:T(8,128)(2,1)S(1)} %get-tuple-element.56), channel_id=1, source_target_pairs={{0,66},{1,67},{16,82},{17,83},{32,98},{33,99},{48,114},{49,115},{4... | collective-permute-start | bytes 638984 | tf_op jit(solution)/shard_map/ppermute | solution.py:33
  95.8 7.1 %collective-permute-start.20 = (bf16[64,1664]{1,0:T(8,128)(2,1)S(1)}, bf16[64,1664]{1,0:T(8,128)(2,1)S(1)}, u32[]{:S(2)}, u32[]{:S(2)}) collective-permute-start(bf16[64,1664]{1,0:T(8,128)(2,1)S(1)} %get-tuple-element.57), channel_id=1, source_target_pairs={{0,2},{1,3},{16,18},{17,19},{32,34},{33,35},{48,50},{49,51},{4,6},... | collective-permute-start | bytes 638984 | tf_op jit(solution)/shard_map/ppermute | solution.py:33
  102.9 7.0 %collective-permute-start.21 = (bf16[32,1664]{1,0:T(8,128)(2,1)S(1)}, bf16[32,1664]{1,0:T(8,128)(2,1)S(1)}, u32[]{:S(2)}, u32[]{:S(2)}) collective-permute-start(bf16[32,1664]{1,0:T(8,128)(2,1)S(1)} %get-tuple-element.59), channel_id=1, source_target_pairs={{0,4},{1,5},{16,20},{17,21},{32,36},{33,37},{48,52},{49,53},{4,8},... | collective-permute-start | bytes 319496 | tf_op jit(solution)/shard_map/ppermute | solution.py:33
  104.3 7.0 %collective-permute-start.22 = (bf16[32,1664]{1,0:T(8,128)(2,1)S(1)}, bf16[32,1664]{1,0:T(8,128)(2,1)S(1)}, u32[]{:S(2)}, u32[]{:S(2)}) collective-permute-start(bf16[32,1664]{1,0:T(8,128)(2,1)S(1)} %get-tuple-element.60), channel_id=1, source_target_pairs={{0,8},{1,9},{16,24},{17,25},{32,40},{33,41},{48,56},{49,57},{4,12}... | collective-permute-start | bytes 319496 | tf_op jit(solution)/shard_map/ppermute | solution.py:33
  107.5 4.7 %collective-permute-start.23 = (bf16[32,1664]{1,0:T(8,128)(2,1)S(1)}, bf16[32,1664]{1,0:T(8,128)(2,1)S(1)}, u32[]{:S(2)}, u32[]{:S(2)}) collective-permute-start(bf16[32,1664]{1,0:T(8,128)(2,1)S(1)} %get-tuple-element.61), channel_id=1, source_target_pairs={{0,12},{1,13},{16,28},{17,29},{32,44},{33,45},{48,60},{49,61},{4,0... | collective-permute-start | bytes 319496 | tf_op jit(solution)/shard_map/ppermute | solution.py:33
